TPU v7x, 32 devices: a whole 2x2x4 slice. The times are simulated.
32 devices in a mesh: seq: 16 (over z, y, x), chan: 2 (over core).
Axes of the slice: x: 2, y: 2, z: 4, core: 2. Of those that a mesh axis runs over, the one named last changes fastest.
Arguments:
- query_rows: bfloat16 [6144, 8192], P('seq', 'chan'), may hold values from -6 to 6
- key_rows: bfloat16 [6144, 8192], P('seq', 'chan'), may hold values from -6 to 6
- value_rows: bfloat16 [6144, 8192], P('seq', 'chan'), may hold values from -6 to 6
- residues: float32 [512, 16], P('chan'), may hold values from -9.2 to 9.2
- decay_rates: float32 [512, 16], P('chan'), may hold values from 7.9752604e-06 to 0.0334
- medium_taps: float32 [512, 128], P('chan'), may hold values from -0.5 to 0.5
- out_gain: float32 [8192], P('chan'), may hold values from 0.1 to 1.9
- reader_plan: int32 [512, 9], P('chan'), may hold values from 0 to 15, as said below
Outputs:
- mixed: bfloat16 [6144, 8192], P('seq', 'chan')
- handoff: float32 [2320, 16, 32], P('seq', None, 'chan')
Inputs may be any that keep to these rules, and one draw needn't show every extreme that they name: `reader_plan`: each row names 9 different readers. Within each aligned block of 256 filters (the rows of one device along chan) every reader appears at least once, none more than 145 times, and one reader exactly 145 times.
All inputs are finite; a program needn't handle non-finite values.
Results may differ from a plain program's by a relative error of at most 0.0049.
Values may be sent and summed in bfloat16 or wider, within the bound.
No kernel may reach another device: no remote copies, remote signals or barrier semaphores. Data moves between devices by JAX's collectives and lax.ppermute only.
A program may use at most 128 MiB of HBM per device.

v0:
```python
import functools
import math

import jax
import jax.numpy as jnp
from jax import lax
from jax.experimental import pallas as pl
from jax.experimental.pallas import tpu as pltpu
from jax.sharding import PartitionSpec as P

D = 8192
GW = 16
MODES = 16
CH = 128
LANES = 128
PER_TILE = LANES // GW
f32 = jnp.float32
bf16 = jnp.bfloat16
highest = lax.Precision.HIGHEST


def params(mib=56):
    return pltpu.CompilerParams(vmem_limit_bytes=mib * 1024 * 1024)


def iota(shape, axis):
    return lax.broadcasted_iota(jnp.int32, shape, axis)


def same_filter(rows, lanes):
    return (iota((rows, lanes), 0) // MODES) == ((iota((rows, lanes), 1) % LANES) // GW)


def tn_dot(a, b, precision=None):
    return lax.dot_general(
        a, b, (((0,), (0,)), ((), ())), preferred_element_type=f32, precision=precision
    )


def by_tile(values):
    groups = values.shape[0]
    copies = (iota((MODES, LANES), 1) % MODES == iota((MODES, LANES), 0)).astype(f32)
    wide = jnp.dot(values, copies, preferred_element_type=f32, precision=highest)
    mine = (iota((groups, LANES), 1) // MODES) == (iota((groups, LANES), 0) % PER_TILE)
    return jnp.where(mine, wide, 0.0).reshape(groups // PER_TILE, PER_TILE, LANES).sum(axis=1)


def product_kernel(
    tiles, k_ref, v_ref, rates_ref, x_ref, tail_ref, p1_ref, p2_ref, own_ref, sent_ref, spread_ref, rows_ref, flat_ref
):
    step = pl.program_id(0)

    @pl.when(step == 0)
    def _():
        rates = rates_ref[...].T
        flat_ref[...] = rates
        rows_ref[...] = by_tile(rates)

    to_end = (CH - iota((CH, LANES), 0)).astype(f32)
    mask = same_filter(LANES, 3 * LANES)
    expand = (iota((PER_TILE, LANES), 1) // GW == iota((PER_TILE, LANES), 0)).astype(f32)
    for t in range(tiles):
        lanes = slice(t * LANES, (t + 1) * LANES)
        tile = step * tiles + t
        x = (k_ref[:, lanes].astype(f32) * v_ref[:, lanes].astype(f32)).astype(bf16)
        x_ref[:, lanes] = x
        tail_ref[:, lanes] = x[2 * CH :]
        spread = tn_dot(flat_ref[pl.ds(pl.multiple_of(tile * PER_TILE, PER_TILE), PER_TILE), :], expand, highest)
        spread_ref[:, lanes] = spread
        ends = jnp.exp(-to_end * rows_ref[pl.ds(tile, 1), :]).astype(bf16)
        wide = jnp.concatenate([x[:CH], x[CH : 2 * CH], x[2 * CH :]], axis=1)
        full = tn_dot(ends, wide)
        packed = jnp.where(mask, full, 0.0).reshape(PER_TILE, MODES, 3 * LANES).sum(axis=0)
        u0, u1, u2 = packed[:, :LANES], packed[:, LANES : 2 * LANES], packed[:, 2 * LANES :]
        decay = jnp.exp(-float(CH) * spread)
        p2 = decay * u0 + u1
        own = decay * p2 + u2
        p1_ref[:, lanes] = u0
        p2_ref[:, lanes] = p2
        own_ref[:, lanes] = own
        sent_ref[:, lanes] = own.astype(bf16)


def product_and_states(key_rows, value_rows, rates_t):
    tokens, channels = key_rows.shape
    groups = rates_t.shape[1]
    tiles = 8
    width = tiles * LANES
    wide = pl.BlockSpec((tokens, width), lambda i: (0, i))
    state = pl.BlockSpec((MODES, width), lambda i: (0, i))
    state_shape = jax.ShapeDtypeStruct((MODES, channels), f32)
    whole = lambda *shape: pl.BlockSpec(shape, lambda i: (0, 0))
    return pl.pallas_call(
        functools.partial(product_kernel, tiles),
        grid=(channels // width,),
        in_specs=[wide, wide, whole(*rates_t.shape)],
        out_specs=[
            wide, pl.BlockSpec((CH, width), lambda i: (0, i)), state, state, state, state, state,
            whole(channels // LANES, LANES),
        ],
        out_shape=[
            jax.ShapeDtypeStruct((tokens, channels), bf16), jax.ShapeDtypeStruct((CH, channels), bf16),
            state_shape, state_shape, state_shape, jax.ShapeDtypeStruct((MODES, channels), bf16), state_shape,
            jax.ShapeDtypeStruct((channels // LANES, LANES), f32),
        ],
        scratch_shapes=[pltpu.VMEM((groups, MODES), f32)],
        compiler_params=params(),
        cost_estimate=pl.CostEstimate(
            flops=6 * tokens * channels * CH, bytes_accessed=6 * tokens * channels, transcendentals=channels * CH
        ),
        name="product_states",
    )(key_rows, value_rows, rates_t)


FOLD = 4
PARTS = PER_TILE // FOLD


def toeplitz(row):
    return pltpu.roll(jnp.broadcast_to(row, (CH, LANES)), 0, 1, stride=1, stride_axis=0)


def fold_masks():
    group = iota((CH, LANES), 1) // GW
    return [(group % PARTS == a).astype(f32).astype(bf16) for a in range(PARTS)]


def unfold(stacked):
    member = iota((CH, LANES), 1) // GW // PARTS
    out = stacked[:CH]
    for b in range(1, FOLD):
        out = jnp.where(member == b, stacked[b * CH : (b + 1) * CH], out)
    return out


def reversed_lags(taps):
    flip = ((iota((CH, LANES), 0) + iota((CH, LANES), 1)) % CH == 0).astype(f32)
    return jnp.dot(taps, flip, preferred_element_type=f32, precision=highest)


def local_kernel(first, tiles, x_ref, taps_ref, rates_ref, coeff_ref, *rest):
    out_ref, taps_rev, response, lhs_all, rhs_all = rest[-5:]
    step = pl.program_id(0)
    count = tiles * PER_TILE
    half = PARTS * CH
    at = pl.multiple_of(step * count, count)
    lag = ((CH - iota((1, LANES), 1)) % CH).astype(f32)

    @pl.when(step == 0)
    def _():
        span = slice(first, first + taps_ref.shape[0])
        rates, coeff = rates_ref[...].T[span], coeff_ref[...].T[span]
        sums = reversed_lags(taps_ref[...])
        taps_rev[...] = sums
        for m in range(MODES):
            sums = sums + coeff[:, m : m + 1] * jnp.exp(-rates[:, m : m + 1] * lag)
        response[...] = sums

    lower = iota((CH, LANES), 1) <= iota((CH, LANES), 0)
    masks = fold_masks()
    for t in range(tiles):
        lanes = slice(t * LANES, (t + 1) * LANES)
        lhs_ref, rhs_ref = lhs_all.at[t % 2], rhs_all.at[t % 2]
        chunks = [x_ref[c * CH : (c + 1) * CH, lanes] for c in range(3)]
        for f in range(PER_TILE):
            a, rows = f % PARTS, slice(f // PARTS * CH, (f // PARTS + 1) * CH)
            row = pl.ds(at + t * PER_TILE + f, 1)
            lhs_ref[rows, half + a * CH : half + (a + 1) * CH] = jnp.where(lower, toeplitz(response[row, :]), 0.0).astype(bf16)
            lhs_ref[rows, a * CH : (a + 1) * CH] = jnp.where(lower, 0.0, toeplitz(taps_rev[row, :])).astype(bf16)
        for a in range(PARTS):
            x0, x1, x2 = [chunk * masks[a] for chunk in chunks]
            rhs_ref[a * CH : (a + 1) * CH, :LANES] = x0
            rhs_ref[a * CH : (a + 1) * CH, LANES:] = x1
            rhs_ref[half + a * CH : half + (a + 1) * CH, :LANES] = x1
            rhs_ref[half + a * CH : half + (a + 1) * CH, LANES:] = x2
        later = jnp.dot(lhs_ref[...], rhs_ref[...], preferred_element_type=f32)
        first = jnp.dot(lhs_ref[:, half:], rhs_ref[:half, :LANES], preferred_element_type=f32)
        out_ref[:CH, lanes] = unfold(first)
        out_ref[CH : 2 * CH, lanes] = unfold(later[:, :LANES])
        out_ref[2 * CH :, lanes] = unfold(later[:, LANES:])


def local_part(x, taps, rates_t, coeff_t, piece, pieces, into):
    tokens, channels = x.shape
    groups = taps.shape[0]
    tiles = min(4, channels // LANES // pieces)
    width = tiles * LANES
    steps = channels // width // pieces
    start = piece * steps
    span = groups // pieces
    wide = pl.BlockSpec((tokens, width), lambda i: (0, i + start))
    whole = pl.BlockSpec(rates_t.shape, lambda i: (0, 0))
    args = [x, taps, rates_t, coeff_t]
    specs = [
        wide, pl.BlockSpec((span, CH), lambda i: (piece, 0)), whole, whole,
    ]
    aliases = {}
    if into is not None:
        args.append(into)
        specs.append(pl.BlockSpec(memory_space=pl.ANY))
        aliases = {4: 0}
    return pl.pallas_call(
        functools.partial(local_kernel, piece * span, tiles),
        grid=(steps,),
        in_specs=specs,
        out_specs=wide,
        out_shape=jax.ShapeDtypeStruct((tokens, channels), f32),
        scratch_shapes=[
            pltpu.VMEM((span, CH), f32), pltpu.VMEM((span, CH), f32),
            pltpu.VMEM((2, FOLD * CH, 2 * PARTS * CH), bf16), pltpu.VMEM((2, 2 * PARTS * CH, 2 * LANES), bf16),
        ],
        input_output_aliases=aliases,
        compiler_params=params(),
        cost_estimate=pl.CostEstimate(
            flops=span * CH * 256 * 512 * 2, bytes_accessed=span * GW * tokens * 6, transcendentals=0
        ),
        name="local_conv",
    )(*args)


def cross_of(decays, states):
    mask = same_filter(LANES, len(states) * LANES)
    wide = jnp.concatenate(states, axis=1)
    high = wide.astype(bf16)
    low = wide - high.astype(f32)
    blocks = lambda a: jnp.where(mask, jnp.concatenate([a] * PER_TILE, axis=0), 0.0).astype(bf16)
    stacked = jnp.concatenate([blocks(high.astype(f32)), blocks(low)], axis=0)
    return jnp.dot(jnp.concatenate([decays, decays], axis=1), stacked, preferred_element_type=f32)


def starts_of(lam, weight):
    index = iota((CH, LANES), 0).astype(f32)
    return (weight * jnp.exp(-index * lam)).astype(bf16)


def add_energy(energy_ref, total_ref, step, last, partial):
    @pl.when(step == 0)
    def _():
        total_ref[...] = partial

    @pl.when(step > 0)
    def _():
        total_ref[...] += partial

    @pl.when(step == last)
    def _():
        energy_ref[...] = lax.dot_general(
            jnp.ones((8, LANES), f32), total_ref[...], (((1,), (1,)), ((), ())),
            preferred_element_type=f32, precision=highest,
        )


def later_kernel(
    tiles, steps, local1_ref, local2_ref, q1_ref, q2_ref, in_ref, p1_ref, p2_ref, spread_ref, rates_ref, coeff_ref,
    gated_ref, energy_ref, total_ref, weight_ref,
):
    step = pl.program_id(0)

    @pl.when(step == 0)
    def _():
        weight_ref[...] = by_tile(coeff_ref[...].T)

    partial = jnp.zeros((2 * CH, LANES), f32)
    for t in range(tiles):
        lanes = slice(t * LANES, (t + 1) * LANES)
        decay = jnp.exp(-float(CH) * spread_ref[:, lanes])
        entry = decay * in_ref[:, lanes]
        z1 = entry + p1_ref[:, lanes]
        z2 = decay * entry + p2_ref[:, lanes]
        row = pl.ds(step * tiles + t, 1)
        cross = cross_of(starts_of(rates_ref[row, :], weight_ref[row, :]), [z1, z2])
        one = (local1_ref[:, lanes] + cross[:, :LANES]) * q1_ref[:, lanes].astype(f32)
        two = (local2_ref[:, lanes] + cross[:, LANES:]) * q2_ref[:, lanes].astype(f32)
        gated_ref[:CH, lanes] = one
        gated_ref[CH:, lanes] = two
        partial = partial + jnp.concatenate([one * one, two * two], axis=0)
    add_energy(energy_ref, total_ref, step, steps - 1, partial)


def first_kernel(
    tiles, steps, local_ref, q_ref, in_ref, tail_ref, taps_ref, rates_ref, coeff_ref,
    gated_ref, energy_ref, total_ref, weight_ref, taps_rev, lhs_all,
):
    step = pl.program_id(0)

    @pl.when(step == 0)
    def _():
        weight_ref[...] = by_tile(coeff_ref[...].T)

    taps_rev[...] = reversed_lags(taps_ref[...])
    lower = iota((CH, LANES), 1) <= iota((CH, LANES), 0)
    masks = fold_masks()
    partial = jnp.zeros((CH, LANES), f32)
    for t in range(tiles):
        lanes = slice(t * LANES, (t + 1) * LANES)
        lhs_ref = lhs_all.at[t % 2]
        row = pl.ds(step * tiles + t, 1)
        cross = cross_of(starts_of(rates_ref[row, :], weight_ref[row, :]), [in_ref[:, lanes]])
        for f in range(PER_TILE):
            a, rows = f % PARTS, slice(f // PARTS * CH, (f // PARTS + 1) * CH)
            at = t * PER_TILE + f
            lhs_ref[rows, a * CH : (a + 1) * CH] = jnp.where(lower, 0.0, toeplitz(taps_rev[at : at + 1, :])).astype(bf16)
        tail = tail_ref[:, lanes]
        masked = jnp.concatenate([tail * mask for mask in masks], axis=0)
        carried = unfold(jnp.dot(lhs_ref[...], masked, preferred_element_type=f32))
        one = (local_ref[:, lanes] + cross + carried) * q_ref[:, lanes].astype(f32)
        gated_ref[:, lanes] = one
        partial = partial + one * one
    add_energy(energy_ref, total_ref, step, steps - 1, partial)


def later_part(local, query_rows, incoming, p1, p2, rates_spread, rate_rows, coeff_t):
    tokens, channels = local.shape
    tiles = 8
    width = tiles * LANES
    steps = channels // width
    state = pl.BlockSpec((MODES, width), lambda i: (0, i))
    whole = lambda a: pl.BlockSpec(a.shape, lambda i: (0, 0))
    chunk = lambda c: pl.BlockSpec((CH, width), lambda i: (c, i))
    return pl.pallas_call(
        functools.partial(later_kernel, tiles, steps),
        grid=(steps,),
        in_specs=[
            chunk(1), chunk(2), chunk(1), chunk(2),
            state, state, state, state, whole(rate_rows), whole(coeff_t),
        ],
        out_specs=[
            pl.BlockSpec((2 * CH, width), lambda i: (0, i)),
            pl.BlockSpec((8, 2 * CH), lambda i: (0, 0)),
        ],
        out_shape=[
            jax.ShapeDtypeStruct((2 * CH, channels), f32),
            jax.ShapeDtypeStruct((8, 2 * CH), f32),
        ],
        scratch_shapes=[pltpu.VMEM((2 * CH, LANES), f32), pltpu.VMEM(rate_rows.shape, f32)],
        compiler_params=params(),
        cost_estimate=pl.CostEstimate(
            flops=channels // LANES * CH * 256 * 512, bytes_accessed=channels * 2 * CH * 10, transcendentals=channels * CH
        ),
        name="gate_later",
    )(local, local, query_rows, query_rows, incoming, p1, p2, rates_spread, rate_rows, coeff_t)


def first_part(local, query_rows, incoming, tail, taps, rate_rows, coeff_t):
    tokens, channels = local.shape
    tiles = 8
    width = tiles * LANES
    steps = channels // width
    top = pl.BlockSpec((CH, width), lambda i: (0, i))
    whole = lambda a: pl.BlockSpec(a.shape, lambda i: (0, 0))
    return pl.pallas_call(
        functools.partial(first_kernel, tiles, steps),
        grid=(steps,),
        in_specs=[
            top, top, pl.BlockSpec((MODES, width), lambda i: (0, i)), top,
            pl.BlockSpec((tiles * PER_TILE, CH), lambda i: (i, 0)), whole(rate_rows), whole(coeff_t),
        ],
        out_specs=[top, pl.BlockSpec((8, CH), lambda i: (0, 0))],
        out_shape=[jax.ShapeDtypeStruct((CH, channels), f32), jax.ShapeDtypeStruct((8, CH), f32)],
        scratch_shapes=[
            pltpu.VMEM((CH, LANES), f32), pltpu.VMEM(rate_rows.shape, f32),
            pltpu.VMEM((tiles * PER_TILE, CH), f32), pltpu.VMEM((2, FOLD * CH, PARTS * CH), bf16),
        ],
        compiler_params=params(),
        cost_estimate=pl.CostEstimate(
            flops=channels * CH * 1024, bytes_accessed=channels * CH * 12, transcendentals=channels * CH
        ),
        name="gate_first",
    )(local, query_rows, incoming, tail, taps, rate_rows, coeff_t)


def norm_kernel(energy_ref, gated_ref, gain_ref, *rest):
    out_ref = rest[-1]
    spread = tn_dot(energy_ref[...], jnp.full((8, LANES), 0.125, f32), highest)
    scale = lax.rsqrt(spread / D + 1e-05)
    for t in range(out_ref.shape[1] // LANES):
        lanes = slice(t * LANES, (t + 1) * LANES)
        out_ref[:, lanes] = (gated_ref[:, lanes] * scale * gain_ref[:, lanes]).astype(bf16)


def norm_part(energy, gated, gain_row, tokens, first, into):
    rows, channels = gated.shape
    width = min(channels, 16 * LANES)
    per = CH
    args = [energy, gated, gain_row]
    specs = [
        pl.BlockSpec((8, per), lambda r, i: (0, r)),
        pl.BlockSpec((per, width), lambda r, i: (r, i)),
        pl.BlockSpec((1, width), lambda r, i: (0, i)),
    ]
    aliases = {}
    if into is not None:
        args.append(into)
        specs.append(pl.BlockSpec(memory_space=pl.ANY))
        aliases = {3: 0}
    return pl.pallas_call(
        norm_kernel,
        grid=(rows // per, channels // width),
        in_specs=specs,
        out_specs=pl.BlockSpec((per, width), lambda r, i: (r + first // per, i)),
        out_shape=jax.ShapeDtypeStruct((tokens, channels), bf16),
        input_output_aliases=aliases,
        compiler_params=params(),
        cost_estimate=pl.CostEstimate(flops=rows * channels * 2, bytes_accessed=rows * channels * 6, transcendentals=0),
        name="norm",
    )(*args)


def regroup(block):
    shape = block.shape
    sub = iota(shape, 1)
    lane = iota(shape, 2) // GW
    for k in (1, 2, 4):
        up = pltpu.roll(pltpu.roll(block, 8 - k, 1), GW * k, 2)
        down = pltpu.roll(pltpu.roll(block, k, 1), LANES - GW * k, 2)
        row_bit, lane_bit = (sub & k) != 0, (lane & k) != 0
        block = jnp.where(row_bit == lane_bit, block, jnp.where(lane_bit, up, down))
    return block


def ranks_of(present):
    count = present.shape[1]
    before = (iota((count, count), 0) < iota((count, count), 1)).astype(bf16)
    return jnp.dot(present.astype(bf16), before, preferred_element_type=f32)


def select_kernel(blocks, slots, inner, outer, me_ref, tail_ref, plan_ref, *refs):
    outs, (items_ref, picks_ref) = refs[:inner], refs[inner:]
    groups = plan_ref.shape[1]

    @pl.when(me_ref[0] != inner * outer - 1)
    def _():
        for out in outs:
            out[...] = jnp.zeros_like(out)

    @pl.when(me_ref[0] == inner * outer - 1)
    def _():
        for g in range(0, groups // PER_TILE, 2):
            halves = []
            for side in range(2):
                rows = tail_ref[:, (g + side) * LANES : (g + side + 1) * LANES].astype(f32)
                halves.append(regroup(rows.reshape(2 * blocks, 8, LANES)))
            for b in range(blocks):
                for half in range(2):
                    both = jnp.concatenate([halves[0][2 * b + half], halves[1][2 * b + half]], axis=0)
                    items_ref[
                        b * groups + g * 8 : b * groups + (g + 2) * 8, half * LANES : (half + 1) * LANES
                    ] = both.astype(bf16)
        plan = plan_ref[...]
        readers = iota((inner * outer, 1, 1), 0)
        mine = (plan[None] == readers).astype(f32)
        ranks = ranks_of(jnp.sum(mine, axis=1))
        slot = iota((slots, groups), 0).astype(f32)
        for p in range(inner):
            for o in range(outer):
                r = o * inner + p
                at = jnp.broadcast_to(ranks[r : r + 1], (slots, groups)) == slot
                for b in range(blocks):
                    picks_ref[o * slots : (o + 1) * slots, b * groups : (b + 1) * groups] = jnp.where(
                        at & (plan[b : b + 1] == r), 1.0, 0.0
                    ).astype(bf16)
            total = jnp.dot(picks_ref[...], items_ref[...], preferred_element_type=f32)
            outs[p][...] = total.astype(bf16).reshape(outs[p].shape)


def select_tails(me, tail, plan_cols, inner, outer, slots):
    rows, channels = tail.shape
    groups = plan_cols.shape[1]
    blocks = rows // MODES
    vmem = pl.BlockSpec(memory_space=pltpu.VMEM)
    return pl.pallas_call(
        functools.partial(select_kernel, blocks, slots, inner, outer),
        in_specs=[pl.BlockSpec(memory_space=pltpu.SMEM), vmem, vmem],
        out_specs=[vmem] * inner,
        out_shape=[jax.ShapeDtypeStruct((outer, slots, MODES * GW), bf16)] * inner,
        scratch_shapes=[
            pltpu.VMEM((blocks * groups, MODES * GW), bf16), pltpu.VMEM((outer * slots, blocks * groups), bf16),
        ],
        compiler_params=params(),
        cost_estimate=pl.CostEstimate(flops=10**9, bytes_accessed=2 * 10**6, transcendentals=0),
        name="select_tails",
    )(me, tail, plan_cols)


def handoff_kernel(me_ref, final_ref, norm_ref, plan_ref, got_ref, out_ref, items_ref):
    groups = plan_ref.shape[1]
    capacity = out_ref.shape[2]
    slots = got_ref.shape[0]
    plan = plan_ref[...]
    mine = plan == me_ref[0]
    present = jnp.sum(mine.astype(f32), axis=0, keepdims=True)
    rank = ranks_of(jnp.broadcast_to(present, (8, groups)))[:1]
    final = final_ref[...] * norm_ref[...]
    stack = [
        final[half * 8 : (half + 1) * 8, g * LANES : (g + 1) * LANES]
        for half in range(2) for g in range(groups // PER_TILE)
    ]
    done = regroup(jnp.stack(stack, axis=0)).reshape(2 * groups, LANES).astype(bf16)
    items_ref[:, :LANES] = done[:groups]
    items_ref[:, LANES:] = done[groups:]
    slot = iota((slots, groups), 0).astype(f32)
    last = plan.shape[0] - 1
    at = (jnp.broadcast_to(rank, (slots, groups)) == slot) & mine[last:]
    pick = jnp.where(at, 1.0, 0.0).astype(bf16)
    rows = jnp.dot(pick, items_ref[...], preferred_element_type=f32)
    rows = (rows + got_ref[...].astype(f32)).T
    out_ref[...] = rows[:, :capacity].reshape(out_ref.shape)


def assemble(me, final, norm_spread, plan_cols, got, capacity):
    groups = plan_cols.shape[1]
    vmem = pl.BlockSpec(memory_space=pltpu.VMEM)
    out = pl.pallas_call(
        handoff_kernel,
        in_specs=[pl.BlockSpec(memory_space=pltpu.SMEM), vmem, vmem, vmem, vmem],
        out_specs=vmem,
        out_shape=jax.ShapeDtypeStruct((MODES, GW, capacity), f32),
        scratch_shapes=[pltpu.VMEM((groups, MODES * GW), bf16)],
        compiler_params=params(),
        cost_estimate=pl.CostEstimate(flops=10**9, bytes_accessed=10**6, transcendentals=0),
        name="handoff",
    )(me, final, norm_spread, plan_cols, got)
    return out.transpose(2, 0, 1)


def scatter_tails(selected, inner, outer):
    count = inner * outer
    me = lax.axis_index("seq")
    base = count - inner
    mine = selected[inner - 1]
    for p in range(inner - 1):
        sent = lax.ppermute(selected[p], "seq", [(count - 1, base + p)])
        mine = jnp.where(me == base + p, sent, mine)
    got = mine[outer - 1]
    for o in range(outer - 1):
        sent = lax.ppermute(mine[o], "seq", [(base + p, o * inner + p) for p in range(inner)])
        got = jnp.where(me // inner == o, sent, got)
    return got


def scan_states(own, sent, rates_spread, tokens):
    count = lax.axis_size("seq")
    me = lax.axis_index("seq")
    total, incoming = own, jnp.zeros_like(own)
    step = 1
    while step < count:
        pairs = [(i, i ^ step) for i in range(count)]
        other = lax.ppermute(sent, "seq", pairs).astype(f32)
        right = (me & step) != 0
        offset = ((me & (step - 1)) * tokens).astype(f32)
        incoming = jnp.where(right, incoming + jnp.exp(-rates_spread * offset) * other, incoming)
        decay = jnp.exp(-rates_spread * float(step * tokens))
        total = jnp.where(right, decay * other + total, decay * total + other)
        sent = total.astype(bf16)
        step *= 2
    return total, incoming


def sum_over_chan(energy):
    if lax.axis_size("chan") == 2:
        return energy + lax.ppermute(energy, "chan", [(0, 1), (1, 0)])
    return lax.psum(energy, "chan")


def per_device(
    query_rows, key_rows, value_rows, residues, decay_rates, medium_taps, out_gain, reader_plan
):
    tokens, channels = query_rows.shape
    groups, mode_count = residues.shape
    blocks = medium_taps.shape[1] // mode_count
    seq_count = lax.axis_size("seq")
    me = lax.axis_index("seq")

    rates_t = decay_rates.T
    x, own_tail, p1, p2, own, sent, rates_spread, rate_rows = product_and_states(
        key_rows, value_rows, rates_t
    )
    tail_prev = lax.ppermute(own_tail, "seq", [(i, i + 1) for i in range(seq_count - 1)])
    total, incoming = scan_states(own, sent, rates_spread, tokens)

    coeff_t = residues.T * jnp.sqrt(-jnp.expm1(-2.0 * rates_t))
    norm_spread = jnp.sqrt(-jnp.expm1(-2.0 * rates_spread))
    plan_cols = reader_plan.T

    inner = 1 << (int(math.log2(seq_count)) // 2)
    outer = seq_count // inner
    capacity = (groups * (blocks + 1) + seq_count - 1) // seq_count + 1
    slots = -(-capacity // 16) * 16
    selected = select_tails(me.reshape(1), own_tail, plan_cols, inner, outer, slots)
    got = scatter_tails(selected, inner, outer)

    pieces = 4
    local = None
    for piece in range(pieces):
        local = local_part(x, medium_taps, rates_t, coeff_t, piece, pieces, local)

    gain_row = out_gain[None, :]
    gated_later, energy_later = later_part(
        local, query_rows, incoming, p1, p2, rates_spread, rate_rows, coeff_t
    )
    mixed = norm_part(sum_over_chan(energy_later), gated_later, gain_row, tokens, CH, None)
    gated_first, energy_first = first_part(
        local, query_rows, incoming, tail_prev, medium_taps, rate_rows, coeff_t
    )
    mixed = norm_part(sum_over_chan(energy_first), gated_first, gain_row, tokens, 0, mixed)

    handoff = assemble(me.reshape(1), total, norm_spread, plan_cols, got, capacity)
    return mixed, handoff


def solution(mesh):
    placed = (
        P("seq", "chan"),
        P("seq", "chan"),
        P("seq", "chan"),
        P("chan", None),
        P("chan", None),
        P("chan", None),
        P("chan"),
        P("chan", None),
    )
    return jax.shard_map(
        per_device,
        mesh=mesh,
        in_specs=placed,
        out_specs=(P("seq", "chan"), P("seq", None, "chan")),
        check_vma=False,
    )
```

profile of v0, /device:TPU:0, one launch (start us, length us, event | category | flops | bytes accessed | tf_op | source)
XLA Modules:
  0.0 94.2 jit_solution(552224852608971040)
XLA Ops:
  0.6 6.9 %product_states.1 = (bf16[384,4096]{1,0:T(8,128)(2,1)}, bf16[128,4096]{1,0:T(8,128)(2,1)}, f32[16,4096]{1,0:T(8,128)}, f32[16,4096]{1,0:T(8,128)}, f32[16,4096]{...) custom-call(bf16[384,4096]{1,0:T(8,128)(2,1)} %k_ref.1, bf16[384,4096]{1,0:T(8,128)(2,1)} %v_ref.1, ...), custom_call_target="tpu_custom_call" | custom-call | flops 1207959552 | bytes 9437184 | tf_op jit(solution)/shard_map/product_states/pallas_call | solution.py:93
  7.6 0.0 copy-start.3
  7.6 0.0 copy-start.5
  7.6 3.0 %collective-permute-start = (bf16[16,4096]{1,0:T(8,128)(2,1)}, bf16[16,4096]{1,0:T(8,128)(2,1)S(1)}, u32[]{:S(2)}, u32[]{:S(2)}) collective-permute-start(bf16[16,4096]{1,0:T(8,128)(2,1)} %get-tuple-element.20), channel_id=1, source_target_pairs={{0,2},{2,0},{4,6},{6,4},{8,10},{10,8},{12,14},{14,12},{16,18},{18,... | collective-permute-start | bytes 393224 | tf_op jit(solution)/shard_map/ppermute | solution.py:548
  10.6 2.0 %collective-permute-start.4 = (bf16[128,4096]{1,0:T(8,128)(2,1)}, bf16[128,4096]{1,0:T(8,128)(2,1)S(1)}, u32[]{:S(2)}, u32[]{:S(2)}) collective-permute-start(bf16[128,4096]{1,0:T(8,128)(2,1)} %get-tuple-element.22.tail_ref), channel_id=1, source_target_pairs={{0,2},{2,4},{4,6},{6,8},{8,10},{10,12},{12,14},{14,16},{16,18},{18... | collective-permute-start | bytes 3145736 | tf_op jit(solution)/shard_map/ppermute | solution.py:578
  12.6 2.4 %select_tails.1 = (bf16[4,160,256]{2,1,0:T(8,128)(2,1)}, bf16[4,160,256]{2,1,0:T(8,128)(2,1)}, bf16[4,160,256]{2,1,0:T(8,128)(2,1)}, bf16[4,160,256]{2,1,0:T(8,128)(2,1)}) custom-call(s32[1]{0:T(128)} %bitcast.3.me_ref, bf16[128,4096]{1,0:T(8,128)(2,1)} %get-tuple-element.22.tail_ref, s32[9,256]{1,0:T(8,128)} %bitcast.29), custom_call_target="tpu_custom_call" | custom-call | flops 1000000000 | bytes 2000000 | tf_op jit(solution)/shard_map/select_tails/pallas_call | solution.py:471
  15.0 0.7 collective-permute-start.7
  15.6 0.7 collective-permute-start.8
  16.3 0.7 collective-permute-start.9
  17.0 0.0 copy-done.3
  17.0 0.0 copy-done.5
  17.1 0.6 bitcast_multiply_fusion.coeff_ref
  17.7 4.8 %local_conv.4.rest_0_ = f32[384,4096]{1,0:T(8,128)} custom-call(bf16[384,4096]{1,0:T(8,128)(2,1)} %get-tuple-element.18.x_ref, f32[256,128]{1,0:T(8,128)} %taps_ref.9, f32[16,256]{1,0:T(8,128)} %bitcast.23, f32[16,256]{1,0:T(8,128)} %bitcast_multiply_fusion.coeff_ref), custom_call_target="tpu_custom_call" | custom-call | flops 2147483648 | bytes 2359296 | tf_op jit(solution)/shard_map/local_conv/pallas_call | solution.py:202
  22.5 4.8 %local_conv.5.rest_0_ = f32[384,4096]{1,0:T(8,128)} custom-call(bf16[384,4096]{1,0:T(8,128)(2,1)} %get-tuple-element.18.x_ref, f32[256,128]{1,0:T(8,128)} %taps_ref.9, f32[16,256]{1,0:T(8,128)} %bitcast.24, f32[16,256]{1,0:T(8,128)} %bitcast_multiply_fusion.coeff_ref, f32[384,4096]{1,0:T(8,128)} %local_conv.4.rest_0_), custom_call_target="tpu_custom_call", output_to_operand_aliasing={{}: (4, {})} | custom-call | flops 2147483648 | bytes 2359296 | tf_op jit(solution)/shard_map/local_conv/pallas_call | solution.py:202
  27.3 0.0 copy-start
  27.3 0.0 copy-start.1
  27.3 4.8 %local_conv.6.rest_0_ = f32[384,4096]{1,0:T(8,128)} custom-call(bf16[384,4096]{1,0:T(8,128)(2,1)} %get-tuple-element.18.x_ref, f32[256,128]{1,0:T(8,128)} %taps_ref.9, f32[16,256]{1,0:T(8,128)} %bitcast.25, f32[16,256]{1,0:T(8,128)} %bitcast_multiply_fusion.coeff_ref, f32[384,4096]{1,0:T(8,128)} %local_conv.5.rest_0_), custom_call_target="tpu_custom_call", output_to_operand_aliasing={{}: (4, {})} | custom-call | flops 2147483648 | bytes 2359296 | tf_op jit(solution)/shard_map/local_conv/pallas_call | solution.py:202
  32.2 0.0 collective-permute-done
  32.2 0.0 copy-done
  32.2 0.0 copy-done.1
  32.2 0.1 fusion.13
  32.3 0.0 copy-start.4
  32.3 2.0 %collective-permute-start.1 = (bf16[16,4096]{1,0:T(8,128)(2,1)S(1)}, bf16[16,4096]{1,0:T(8,128)(2,1)S(1)}, u32[]{:S(2)}, u32[]{:S(2)}) collective-permute-start(bf16[16,4096]{1,0:T(8,128)(2,1)S(1)} %fusion.13), channel_id=1, source_target_pairs={{0,4},{2,6},{4,0},{6,2},{8,12},{10,14},{12,8},{14,10},{16,20},{18,... | collective-permute-start | bytes 393224 | tf_op jit(solution)/shard_map/ppermute | solution.py:548
  34.3 4.8 %local_conv.7.local_ref.local1_ref.local2_ref = f32[384,4096]{1,0:T(8,128)} custom-call(bf16[384,4096]{1,0:T(8,128)(2,1)} %get-tuple-element.18.x_ref, f32[256,128]{1,0:T(8,128)} %taps_ref.9, f32[16,256]{1,0:T(8,128)} %bitcast.26, f32[16,256]{1,0:T(8,128)} %bitcast_multiply_fusion.coeff_ref, ...), custom_call_target="tpu_custom_call", output_to_operand_aliasing={{}: (4, {})} | custom-call | flops 2147483648 | bytes 2359296 | tf_op jit(solution)/shard_map/local_conv/pallas_call | solution.py:202
  39.1 0.9 collective-permute-done.1
  40.0 0.2 fusion.14
  40.2 3.5 %collective-permute-start.2 = (bf16[16,4096]{1,0:T(8,128)(2,1)S(1)}, bf16[16,4096]{1,0:T(8,128)(2,1)S(1)}, u32[]{:S(2)}, u32[]{:S(2)}) collective-permute-start(bf16[16,4096]{1,0:T(8,128)(2,1)S(1)} %get-tuple-element.34), channel_id=1, source_target_pairs={{0,8},{2,10},{4,12},{6,14},{8,0},{10,2},{12,4},{14,6},{16,24},{18,... | collective-permute-start | bytes 393224 | tf_op jit(solution)/shard_map/ppermute | solution.py:548
  43.7 0.0 collective-permute-done.7
  43.7 0.0 collective-permute-done.8
  43.7 0.0 collective-permute-done.9
  43.7 0.0 copy-done.4
  43.7 0.1 select_select_fusion
  43.8 0.7 collective-permute-start.10
  44.5 0.7 collective-permute-start.11
  45.2 1.5 %collective-permute-start.12 = (bf16[160,256]{1,0:T(8,128)(2,1)S(1)}, bf16[160,256]{1,0:T(8,128)(2,1)S(1)}, u32[]{:S(2)}, u32[]{:S(2)}) collective-permute-start(bf16[160,256]{1,0:T(8,128)(2,1)S(1)} %get-tuple-element.38), channel_id=1, source_target_pairs={{24,0},{26,2},{28,4},{30,6},{25,1},{27,3},{29,5},{31,7}} | collective-permute-start | bytes 245768 | tf_op jit(solution)/shard_map/ppermute | solution.py:536
  46.7 0.7 collective-permute-done.2
  47.4 0.9 negate_sqrt_fusion
  48.3 2.8 %collective-permute-start.3 = (bf16[16,4096]{1,0:T(8,128)(2,1)S(1)}, bf16[16,4096]{1,0:T(8,128)(2,1)S(1)}, u32[]{:S(2)}, u32[]{:S(2)}) collective-permute-start(bf16[16,4096]{1,0:T(8,128)(2,1)S(1)} %get-tuple-element.42), channel_id=1, source_target_pairs={{0,16},{2,18},{4,20},{6,22},{8,24},{10,26},{12,28},{14,30},{16,0},... | collective-permute-start | bytes 393224 | tf_op jit(solution)/shard_map/ppermute | solution.py:548
  51.1 0.0 collective-permute-done.10
  51.1 0.0 collective-permute-done.11
  51.1 13.6 %collective-permute-done.12 = bf16[160,256]{1,0:T(8,128)(2,1)S(1)} collective-permute-done((bf16[160,256]{1,0:T(8,128)(2,1)S(1)}, bf16[160,256]{1,0:T(8,128)(2,1)S(1)}, u32[]{:S(2)}, u32[]{:S(2)}) %collective-permute-start.12) | collective-permute-done | bytes 81952 | tf_op jit(solution)/shard_map/ppermute | solution.py:536
  64.7 0.7 fusion.11.got_ref
  65.4 0.0 collective-permute-done.3
  65.4 1.2 %fusion.8 = (f32[16,4096]{1,0:T(8,128)}, f32[16,4096]{1,0:T(8,128)}) fusion(bf16[16,4096]{1,0:T(8,128)(2,1)S(1)} %collective-permute-done.3, f32[16,4096]{1,0:T(8,128)S(1)} %copy-done, pred[]{:T(512)S(6)} %ne.24, f32[16,4096]{1,0:T(8,128)S(1)} %get-tuple-element.35, bf16[16,4096]{1,0:T(8,128)(2,1)S(1)} %collective-permute-done.2, pred[]{:T(512)S(6)} %ne.25, ...), kind=kLoop, calls=%fused_computation.24 | loop fusion | flops 2097152 | bytes 1572880 | tf_op jit(solution)/shard_map/jit(_where)/select_n | solution.py:553
  66.6 6.7 %gate_later.1 = (f32[256,4096]{1,0:T(8,128)}, f32[8,256]{1,0:T(8,128)}) custom-call(f32[384,4096]{1,0:T(8,128)} %local_conv.7.local_ref.local1_ref.local2_ref, f32[384,4096]{1,0:T(8,128)} %local_conv.7.local_ref.local1_ref.local2_ref, bf16[384,4096]{1,0:T(8,128)(2,1)} %q2_ref.1, bf16[384,4096]{1,0:T(8,128)(2,1)} %q2_ref.1, ...), custom_call_target="tpu_custom_call" | custom-call | flops 536870912 | bytes 10485760 | tf_op jit(solution)/shard_map/gate_later/pallas_call | solution.py:320
  73.3 0.1 collective-permute-start.6
  73.4 0.0 collective-permute-done.4.tail_ref
  73.4 0.0 copy-start.2
  73.4 1.0 %copy-done.2 = bf16[128,4096]{1,0:T(8,128)(2,1)} copy-done((bf16[128,4096]{1,0:T(8,128)(2,1)}, bf16[128,4096]{1,0:T(8,128)(2,1)S(1)}, u32[]{:S(2)}) %copy-start.2) | copy-done | bytes 1048600
  74.4 8.1 %gate_first.1 = (f32[128,4096]{1,0:T(8,128)}, f32[8,128]{1,0:T(8,128)}) custom-call(f32[384,4096]{1,0:T(8,128)} %local_conv.7.local_ref.local1_ref.local2_ref, bf16[384,4096]{1,0:T(8,128)(2,1)} %q2_ref.1, f32[16,4096]{1,0:T(8,128)} %get-tuple-element.37.in_ref, bf16[128,4096]{1,0:T(8,128)(2,1)} %copy-done.2, f32[256,128]{1,0:T(8,128)} %taps_ref.9, ...), custom_call_target="tpu_custom_call" | custom-call | flops 536870912 | bytes 6291456 | tf_op jit(solution)/shard_map/gate_first/pallas_call | solution.py:351
  82.5 0.0 copy-start.6
  82.5 0.5 collective-permute-start.5
  83.0 2.4 %handoff.1 = f32[16,16,145]{2,1,0:T(8,128)} custom-call(s32[1]{0:T(128)} %bitcast.3.me_ref, f32[16,4096]{1,0:T(8,128)} %get-tuple-element.36.final_ref, f32[16,4096]{1,0:T(8,128)} %get-tuple-element.41.norm_ref, s32[9,256]{1,0:T(8,128)} %bitcast.30, bf16[160,256]{1,0:T(8,128)(2,1)} %fusion.11.got_ref), custom_call_target="tpu_custom_call" | custom-call | flops 1000000000 | bytes 1000000 | tf_op jit(solution)/shard_map/handoff/pallas_call | solution.py:513
  85.4 0.0 collective-permute-done.6
  85.4 0.0 copy-done.6
  85.4 0.6 add.50.energy_ref
  86.0 0.0 copy-start.7
  86.0 4.9 %norm.2.rest_0_ = bf16[384,4096]{1,0:T(8,128)(2,1)} custom-call(f32[8,256]{1,0:T(8,128)} %add.50.energy_ref, f32[256,4096]{1,0:T(8,128)} %get-tuple-element.29.gated_ref, f32[1,4096]{1,0:T(1,128)} %bitcast.27), custom_call_target="tpu_custom_call" | custom-call | flops 2097152 | bytes 6291456 | tf_op jit(solution)/shard_map/norm/pallas_call | solution.py:396
  90.8 0.0 collective-permute-done.5
  90.8 0.0 copy-done.7
  90.8 0.6 add.49.energy_ref
  91.4 2.8 %norm.3 = bf16[384,4096]{1,0:T(8,128)(2,1)} custom-call(f32[8,128]{1,0:T(8,128)} %add.49.energy_ref, f32[128,4096]{1,0:T(8,128)} %get-tuple-element.25.gated_ref, f32[1,4096]{1,0:T(1,128)} %bitcast.28, bf16[384,4096]{1,0:T(8,128)(2,1)} %norm.2.rest_0_), custom_call_target="tpu_custom_call", output_to_operand_aliasing={{}: (3, {})} | custom-call | flops 1048576 | bytes 3145728 | tf_op jit(solution)/shard_map/norm/pallas_call | solution.py:396
  (1 shorter events, 0.0 us)
Async XLA Ops:
  7.6 9.5 %copy-start.3 = (f32[256,16]{0,1:T(8,128)S(1)}, f32[256,16]{0,1:T(8,128)}, u32[]{:S(2)}) copy-start(f32[256,16]{0,1:T(8,128)} %param.12) | copy-start | bytes 49156
  7.6 9.5 %copy-start.5 = (f32[256,16]{0,1:T(8,128)S(1)}, f32[256,16]{0,1:T(8,128)}, u32[]{:S(2)}) copy-start(f32[256,16]{0,1:T(8,128)} %param.11) | copy-start | bytes 49156
  7.6 24.6 %collective-permute-start = (bf16[16,4096]{1,0:T(8,128)(2,1)}, bf16[16,4096]{1,0:T(8,128)(2,1)S(1)}, u32[]{:S(2)}, u32[]{:S(2)}) collective-permute-start(bf16[16,4096]{1,0:T(8,128)(2,1)} %get-tuple-element.20), channel_id=1, source_target_pairs={{0,2},{2,0},{4,6},{6,4},{8,10},{10,8},{12,14},{14,12},{16,18},{18,... | collective-permute-start | bytes 393224 | tf_op jit(solution)/shard_map/ppermute | solution.py:548
  10.6 62.8 %collective-permute-start.4 = (bf16[128,4096]{1,0:T(8,128)(2,1)}, bf16[128,4096]{1,0:T(8,128)(2,1)S(1)}, u32[]{:S(2)}, u32[]{:S(2)}) collective-permute-start(bf16[128,4096]{1,0:T(8,128)(2,1)} %get-tuple-element.22.tail_ref), channel_id=1, source_target_pairs={{0,2},{2,4},{4,6},{6,8},{8,10},{10,12},{12,14},{14,16},{16,18},{18... | collective-permute-start | bytes 3145736 | tf_op jit(solution)/shard_map/ppermute | solution.py:578
  15.0 28.8 %collective-permute-start.7 = (bf16[4,160,256]{2,1,0:T(8,128)(2,1)}, bf16[4,160,256]{2,1,0:T(8,128)(2,1)S(1)}, u32[]{:S(2)}, u32[]{:S(2)}) collective-permute-start(bf16[4,160,256]{2,1,0:T(8,128)(2,1)} %get-tuple-element.30), channel_id=1, source_target_pairs={{30,28},{31,29}} | collective-permute-start | bytes 983048 | tf_op jit(solution)/shard_map/ppermute | solution.py:532
  15.6 28.1 %collective-permute-start.8 = (bf16[4,160,256]{2,1,0:T(8,128)(2,1)}, bf16[4,160,256]{2,1,0:T(8,128)(2,1)S(1)}, u32[]{:S(2)}, u32[]{:S(2)}) collective-permute-start(bf16[4,160,256]{2,1,0:T(8,128)(2,1)} %get-tuple-element.31), channel_id=1, source_target_pairs={{30,26},{31,27}} | collective-permute-start | bytes 983048 | tf_op jit(solution)/shard_map/ppermute | solution.py:532
  16.3 27.4 %collective-permute-start.9 = (bf16[4,160,256]{2,1,0:T(8,128)(2,1)}, bf16[4,160,256]{2,1,0:T(8,128)(2,1)S(1)}, u32[]{:S(2)}, u32[]{:S(2)}) collective-permute-start(bf16[4,160,256]{2,1,0:T(8,128)(2,1)} %get-tuple-element.32), channel_id=1, source_target_pairs={{30,24},{31,25}} | collective-permute-start | bytes 983048 | tf_op jit(solution)/shard_map/ppermute | solution.py:532
  27.3 4.9 %copy-start = (f32[16,4096]{1,0:T(8,128)S(1)}, f32[16,4096]{1,0:T(8,128)}, u32[]{:S(2)}) copy-start(f32[16,4096]{1,0:T(8,128)} %get-tuple-element.19.spread_ref) | copy-start | bytes 786436
  27.3 4.9 %copy-start.1 = (f32[16,4096]{1,0:T(8,128)S(1)}, f32[16,4096]{1,0:T(8,128)}, u32[]{:S(2)}) copy-start(f32[16,4096]{1,0:T(8,128)} %get-tuple-element.21) | copy-start | bytes 786436
  32.3 11.4 %copy-start.4 = (bf16[4,160,256]{2,1,0:T(8,128)(2,1)S(1)}, bf16[4,160,256]{2,1,0:T(8,128)(2,1)}, u32[]{:S(2)}) copy-start(bf16[4,160,256]{2,1,0:T(8,128)(2,1)} %get-tuple-element.33) | copy-start | bytes 983044
  32.3 7.7 %collective-permute-start.1 = (bf16[16,4096]{1,0:T(8,128)(2,1)S(1)}, bf16[16,4096]{1,0:T(8,128)(2,1)S(1)}, u32[]{:S(2)}, u32[]{:S(2)}) collective-permute-start(bf16[16,4096]{1,0:T(8,128)(2,1)S(1)} %fusion.13), channel_id=1, source_target_pairs={{0,4},{2,6},{4,0},{6,2},{8,12},{10,14},{12,8},{14,10},{16,20},{18,... | collective-permute-start | bytes 393224 | tf_op jit(solution)/shard_map/ppermute | solution.py:548
  40.2 7.2 %collective-permute-start.2 = (bf16[16,4096]{1,0:T(8,128)(2,1)S(1)}, bf16[16,4096]{1,0:T(8,128)(2,1)S(1)}, u32[]{:S(2)}, u32[]{:S(2)}) collective-permute-start(bf16[16,4096]{1,0:T(8,128)(2,1)S(1)} %get-tuple-element.34), channel_id=1, source_target_pairs={{0,8},{2,10},{4,12},{6,14},{8,0},{10,2},{12,4},{14,6},{16,24},{18,... | collective-permute-start | bytes 393224 | tf_op jit(solution)/shard_map/ppermute | solution.py:548
  43.8 7.3 %collective-permute-start.10 = (bf16[160,256]{1,0:T(8,128)(2,1)S(1)}, bf16[160,256]{1,0:T(8,128)(2,1)S(1)}, u32[]{:S(2)}, u32[]{:S(2)}) collective-permute-start(bf16[160,256]{1,0:T(8,128)(2,1)S(1)} %get-tuple-element.40), channel_id=1, source_target_pairs={{24,16},{26,18},{28,20},{30,22},{25,17},{27,19},{29,21},{31,23}} | collective-permute-start | bytes 245768 | tf_op jit(solution)/shard_map/ppermute | solution.py:536
  44.5 6.6 %collective-permute-start.11 = (bf16[160,256]{1,0:T(8,128)(2,1)S(1)}, bf16[160,256]{1,0:T(8,128)(2,1)S(1)}, u32[]{:S(2)}, u32[]{:S(2)}) collective-permute-start(bf16[160,256]{1,0:T(8,128)(2,1)S(1)} %get-tuple-element.39), channel_id=1, source_target_pairs={{24,8},{26,10},{28,12},{30,14},{25,9},{27,11},{29,13},{31,15}} | collective-permute-start | bytes 245768 | tf_op jit(solution)/shard_map/ppermute | solution.py:536
  45.2 19.6 %collective-permute-start.12 = (bf16[160,256]{1,0:T(8,128)(2,1)S(1)}, bf16[160,256]{1,0:T(8,128)(2,1)S(1)}, u32[]{:S(2)}, u32[]{:S(2)}) collective-permute-start(bf16[160,256]{1,0:T(8,128)(2,1)S(1)} %get-tuple-element.38), channel_id=1, source_target_pairs={{24,0},{26,2},{28,4},{30,6},{25,1},{27,3},{29,5},{31,7}} | collective-permute-start | bytes 245768 | tf_op jit(solution)/shard_map/ppermute | solution.py:536
  48.3 17.1 %collective-permute-start.3 = (bf16[16,4096]{1,0:T(8,128)(2,1)S(1)}, bf16[16,4096]{1,0:T(8,128)(2,1)S(1)}, u32[]{:S(2)}, u32[]{:S(2)}) collective-permute-start(bf16[16,4096]{1,0:T(8,128)(2,1)S(1)} %get-tuple-element.42), channel_id=1, source_target_pairs={{0,16},{2,18},{4,20},{6,22},{8,24},{10,26},{12,28},{14,30},{16,0},... | collective-permute-start | bytes 393224 | tf_op jit(solution)/shard_map/ppermute | solution.py:548
  73.3 12.0 %collective-permute-start.6 = (f32[8,256]{1,0:T(8,128)}, f32[8,256]{1,0:T(8,128)S(1)}, u32[]{:S(2)}, u32[]{:S(2)}) collective-permute-start(f32[8,256]{1,0:T(8,128)} %get-tuple-element.28), channel_id=1, source_target_pairs={{0,1},{1,0},{2,3},{3,2},{4,5},{5,4},{6,7},{7,6},{8,9},{9,8},{10,11... | collective-permute-start | bytes 24584 | tf_op jit(solution)/shard_map/ppermute | solution.py:561
  73.4 1.0 %copy-start.2 = (bf16[128,4096]{1,0:T(8,128)(2,1)}, bf16[128,4096]{1,0:T(8,128)(2,1)S(1)}, u32[]{:S(2)}) copy-start(bf16[128,4096]{1,0:T(8,128)(2,1)S(1)} %collective-permute-done.4.tail_ref) | copy-start | bytes 3145732
  82.5 2.9 %copy-start.6 = (f32[8,256]{1,0:T(8,128)S(1)}, f32[8,256]{1,0:T(8,128)}, u32[]{:S(2)}) copy-start(f32[8,256]{1,0:T(8,128)} %get-tuple-element.28) | copy-start | bytes 24580
  82.5 8.4 %collective-permute-start.5 = (f32[8,128]{1,0:T(8,128)}, f32[8,128]{1,0:T(8,128)S(1)}, u32[]{:S(2)}, u32[]{:S(2)}) collective-permute-start(f32[8,128]{1,0:T(8,128)} %get-tuple-element.24), channel_id=1, source_target_pairs={{0,1},{1,0},{2,3},{3,2},{4,5},{5,4},{6,7},{7,6},{8,9},{9,8},{10,11... | collective-permute-start | bytes 12296 | tf_op jit(solution)/shard_map/ppermute | solution.py:561
  86.0 4.9 %copy-start.7 = (f32[8,128]{1,0:T(8,128)S(1)}, f32[8,128]{1,0:T(8,128)}, u32[]{:S(2)}) copy-start(f32[8,128]{1,0:T(8,128)} %get-tuple-element.24) | copy-start | bytes 12292
where the time goes:
time: 94.9 us; the launch traced here: 94.2 us
  Pallas kernels  53.4 us (56%)
  starting transfers between devices  18.7 us (20%)
  waiting for transfers between devices  15.3 us (16%)
  other arithmetic  4.94 us (5%)
  local copies, waits for them, and re-layouts  1.01 us (1%)
    pallas_call x4, Pallas kernels, local_part(): pl.pallas_call(functools.partial(local_kernel, piece * span, tiles), grid...  19.3 us
    ppermute x3, waiting for transfers between devices, scatter_tails(): lax.ppermute(mine[o], 'seq', [(base + p, o * inner + p) for p in range(in...  13.7 us
    ppermute x4, starting transfers between devices, scan_states(): other = lax.ppermute(sent, 'seq', pairs).astype(f32)  11.3 us
    pallas_call x1, Pallas kernels, first_part(): pl.pallas_call(functools.partial(first_kernel, tiles, steps), grid=(steps...  8.06 us
    pallas_call x2, Pallas kernels, norm_part(): pl.pallas_call(norm_kernel, grid=(rows // per, channels // width), in_spe...  7.65 us
    pallas_call x1, Pallas kernels, product_and_states(): pl.pallas_call(functools.partial(product_kernel, tiles), grid=(channels /...  6.93 us
    pallas_call x1, Pallas kernels, later_part(): pl.pallas_call(functools.partial(later_kernel, tiles, steps), grid=(steps...  6.73 us
    ppermute x3, starting transfers between devices, scatter_tails(): lax.ppermute(mine[o], 'seq', [(base + p, o * inner + p) for p in range(in...  2.8 us
  transfers between devices with their start and end apart: 13, of which 3 were waited for; matrix products, arithmetic and copies ran while one was open for 5% of the time, Pallas kernels for 46%

commit v1 on v0

v1 whole, which is shorter than its diff:
```python
import functools
import math

import jax
import jax.numpy as jnp
from jax import lax
from jax.experimental import pallas as pl
from jax.experimental.pallas import tpu as pltpu
from jax.sharding import PartitionSpec as P

D = 8192
GW = 16
MODES = 16
CH = 128
LANES = 128
PER_TILE = LANES // GW
f32 = jnp.float32
bf16 = jnp.bfloat16
highest = lax.Precision.HIGHEST


def params(mib=20):
    return pltpu.CompilerParams(vmem_limit_bytes=mib * 1024 * 1024)


def iota(shape, axis):
    return lax.broadcasted_iota(jnp.int32, shape, axis)


def same_filter(rows, lanes):
    return (iota((rows, lanes), 0) // MODES) == ((iota((rows, lanes), 1) % LANES) // GW)


def tn_dot(a, b, precision=None):
    return lax.dot_general(
        a, b, (((0,), (0,)), ((), ())), preferred_element_type=f32, precision=precision
    )


def by_tile(values):
    groups = values.shape[0]
    copies = (iota((MODES, LANES), 1) % MODES == iota((MODES, LANES), 0)).astype(f32)
    wide = jnp.dot(values, copies, preferred_element_type=f32, precision=highest)
    mine = (iota((groups, LANES), 1) // MODES) == (iota((groups, LANES), 0) % PER_TILE)
    return jnp.where(mine, wide, 0.0).reshape(groups // PER_TILE, PER_TILE, LANES).sum(axis=1)


ANY = pl.BlockSpec(memory_space=pl.ANY)
VMEM = pl.BlockSpec(memory_space=pltpu.VMEM)
HBM = pl.BlockSpec(memory_space=pltpu.HBM)


def lanes_at(index, width):
    return pl.ds(pl.multiple_of(index * width, width), width)


def copies(pairs, sems, chunk, width):
    out = []
    for i, (source, target, from_lane, to_lane) in enumerate(pairs):
        out.append(
            pltpu.make_async_copy(
                source.at[:, pl.ds(pl.multiple_of(from_lane + chunk * width, LANES), width)],
                target.at[:, pl.ds(pl.multiple_of(to_lane + chunk * width, LANES), width)],
                sems.at[i, chunk],
            )
        )
    return out


def drain(chunks, width, outputs, out_sems):
    for c in range(chunks):
        for copy in copies(outputs, out_sems, c, width):
            copy.wait()


def product_of(k_ref, v_ref, lanes):
    return (k_ref[:, lanes].astype(f32) * v_ref[:, lanes].astype(f32)).astype(bf16)


def product_kernel(
    chunks, tiles, k_hbm, v_hbm, rates_ref, tail_ref, p1_ref, p2_ref, own_ref, sent_ref, rows_ref,
    k_ref, v_ref, in_sems,
):
    width = tiles * LANES
    inputs = [(k_hbm, k_ref, 0, 0), (v_hbm, v_ref, 0, 0)]
    for c in range(chunks):
        for copy in copies(inputs, in_sems, c, width):
            copy.start()
    rows_ref[...] = by_tile(rates_ref[...].T)
    to_end = (CH - iota((CH, LANES), 0)).astype(f32)
    mask = same_filter(LANES, 3 * LANES)
    none = jnp.zeros((CH, LANES), bf16)

    @pl.loop(0, chunks)
    def _(c):
        for copy in copies(inputs, in_sems, c, width):
            copy.wait()
        for t in range(tiles):
            lanes = lanes_at(c * tiles + t, LANES)
            x = product_of(k_ref, v_ref, lanes)
            tail_ref[:, lanes] = x[2 * CH :]
            lam = rows_ref[pl.ds(c * tiles + t, 1), :]
            near = jnp.exp(-to_end * lam)
            decay = jnp.exp(-float(CH) * lam)
            middle = near * decay
            ends = jnp.concatenate([(middle * decay).astype(bf16), middle.astype(bf16), near.astype(bf16)], axis=0)
            x0, x1 = x[:CH], x[CH : 2 * CH]
            wide = jnp.concatenate(
                [x, jnp.concatenate([none, x0, x1], axis=0), jnp.concatenate([none, none, x0], axis=0)], axis=1
            )
            full = tn_dot(ends, wide)
            packed = jnp.where(mask, full, 0.0).reshape(PER_TILE, MODES, 3 * LANES).sum(axis=0)
            own_ref[:, lanes] = packed[:, :LANES]
            sent_ref[:, lanes] = packed[:, :LANES].astype(bf16)
            p2_ref[:, lanes] = packed[:, LANES : 2 * LANES]
            p1_ref[:, lanes] = packed[:, 2 * LANES :]


def product_and_states(key_rows, value_rows, rates_t):
    tokens, channels = key_rows.shape
    chunks = 4
    tiles = channels // LANES // chunks
    state_shape = jax.ShapeDtypeStruct((MODES, channels), f32)
    return pl.pallas_call(
        functools.partial(product_kernel, chunks, tiles),
        in_specs=[HBM, HBM, VMEM],
        out_specs=[VMEM] * 6,
        out_shape=[
            jax.ShapeDtypeStruct((CH, channels), bf16),
            state_shape, state_shape, state_shape, jax.ShapeDtypeStruct((MODES, channels), bf16),
            jax.ShapeDtypeStruct((channels // LANES, LANES), f32),
        ],
        scratch_shapes=[
            pltpu.VMEM((tokens, channels), bf16), pltpu.VMEM((tokens, channels), bf16),
            pltpu.SemaphoreType.DMA((2, chunks)),
        ],
        compiler_params=params(56),
        cost_estimate=pl.CostEstimate(
            flops=6 * tokens * channels * CH, bytes_accessed=6 * tokens * channels, transcendentals=channels * CH
        ),
        name="product_states",
    )(key_rows, value_rows, rates_t)


def spread_kernel(rates_ref, out_ref):
    rates = rates_ref[...].T
    high = rates.astype(bf16).astype(f32)
    middle = (rates - high).astype(bf16).astype(f32)
    parts = jnp.concatenate([high, middle, rates - high - middle], axis=1)
    expand = (iota((PER_TILE, LANES), 1) // GW == iota((PER_TILE, LANES), 0)).astype(f32).astype(bf16)
    for t in range(out_ref.shape[1] // LANES):
        wide = tn_dot(parts[t * PER_TILE : (t + 1) * PER_TILE].astype(bf16), expand)
        out_ref[:, t * LANES : (t + 1) * LANES] = wide[:MODES] + wide[MODES : 2 * MODES] + wide[2 * MODES :]


def spread_rates(rates_t):
    return pl.pallas_call(
        spread_kernel,
        out_shape=jax.ShapeDtypeStruct((MODES, rates_t.shape[1] * GW), f32),
        compiler_params=params(),
        name="spread_rates",
    )(rates_t)


FOLD = 4
PARTS = PER_TILE // FOLD


def toeplitz(row):
    return pltpu.roll(jnp.broadcast_to(row, (CH, LANES)), 0, 1, stride=1, stride_axis=0)


def fold_masks():
    group = iota((CH, LANES), 1) // GW
    return [(group % PARTS == a).astype(f32).astype(bf16) for a in range(PARTS)]


def unfold(stacked):
    member = iota((CH, LANES), 1) // GW // PARTS
    out = stacked[:CH]
    for b in range(1, FOLD):
        out = jnp.where(member == b, stacked[b * CH : (b + 1) * CH], out)
    return out


def reversed_lags(taps):
    flip = ((iota((CH, LANES), 0) + iota((CH, LANES), 1)) % CH == 0).astype(f32)
    return jnp.dot(taps, flip, preferred_element_type=f32, precision=highest)


def local_kernel(
    chunks, tiles, k_hbm, v_hbm, taps_ref, rates_ref, coeff_ref, after,
    out_ref, k_ref, v_ref, taps_rev, response, lhs_all, rhs_all, in_sems,
):
    half = PARTS * CH
    width = tiles * LANES
    inputs = [(k_hbm, k_ref, 0, 0), (v_hbm, v_ref, 0, 0)]
    for c in range(chunks):
        for copy in copies(inputs, in_sems, c, width):
            copy.start()
    lag = ((CH - iota((1, LANES), 1)) % CH).astype(f32)
    rates, coeff = rates_ref[...].T, coeff_ref[...].T
    sums = reversed_lags(taps_ref[...])
    taps_rev[...] = sums
    for m in range(MODES):
        sums = sums + coeff[:, m : m + 1] * jnp.exp(-rates[:, m : m + 1] * lag)
    response[...] = sums
    lower = iota((CH, LANES), 1) <= iota((CH, LANES), 0)
    masks = fold_masks()

    @pl.loop(0, chunks)
    def _(c):
        for copy in copies(inputs, in_sems, c, width):
            copy.wait()
        for t in range(tiles):
            lanes = lanes_at(c * tiles + t, LANES)
            lhs_ref, rhs_ref = lhs_all.at[t % 2], rhs_all.at[t % 2]
            x = product_of(k_ref, v_ref, lanes)
            for f in range(PER_TILE):
                a, rows = f % PARTS, slice(f // PARTS * CH, (f // PARTS + 1) * CH)
                row = pl.ds((c * tiles + t) * PER_TILE + f, 1)
                lhs_ref[rows, half + a * CH : half + (a + 1) * CH] = jnp.where(lower, toeplitz(response[row, :]), 0.0).astype(bf16)
                lhs_ref[rows, a * CH : (a + 1) * CH] = jnp.where(lower, 0.0, toeplitz(taps_rev[row, :])).astype(bf16)
            for a in range(PARTS):
                x0, x1, x2 = [x[i * CH : (i + 1) * CH] * masks[a] for i in range(3)]
                rhs_ref[a * CH : (a + 1) * CH, :LANES] = x0
                rhs_ref[a * CH : (a + 1) * CH, LANES:] = x1
                rhs_ref[half + a * CH : half + (a + 1) * CH, :LANES] = x1
                rhs_ref[half + a * CH : half + (a + 1) * CH, LANES:] = x2
            later = jnp.dot(lhs_ref[...], rhs_ref[...], preferred_element_type=f32)
            early = jnp.dot(lhs_ref[:, half:], rhs_ref[:half, :LANES], preferred_element_type=f32)
            out_ref[:CH, lanes] = unfold(early).astype(bf16)
            out_ref[CH : 2 * CH, lanes] = unfold(later[:, :LANES]).astype(bf16)
            out_ref[2 * CH :, lanes] = unfold(later[:, LANES:]).astype(bf16)


def local_part(key_rows, value_rows, taps, rates_t, coeff_t, after):
    tokens, channels = key_rows.shape
    groups = taps.shape[0]
    chunks = 4
    tiles = channels // LANES // chunks
    return pl.pallas_call(
        functools.partial(local_kernel, chunks, tiles),
        in_specs=[HBM, HBM, VMEM, VMEM, VMEM, ANY],
        out_specs=VMEM,
        out_shape=jax.ShapeDtypeStruct((tokens, channels), bf16),
        scratch_shapes=[
            pltpu.VMEM((tokens, channels), bf16), pltpu.VMEM((tokens, channels), bf16),
            pltpu.VMEM((groups, CH), f32), pltpu.VMEM((groups, CH), f32),
            pltpu.VMEM((2, FOLD * CH, 2 * PARTS * CH), bf16), pltpu.VMEM((2, 2 * PARTS * CH, 2 * LANES), bf16),
            pltpu.SemaphoreType.DMA((2, chunks)),
        ],
        compiler_params=params(),
        cost_estimate=pl.CostEstimate(
            flops=groups * CH * 256 * 512 * 2, bytes_accessed=groups * GW * tokens * 4, transcendentals=0
        ),
        name="local_conv",
    )(key_rows, value_rows, taps, rates_t, coeff_t, after)


def cross_of(decays, states):
    mask = same_filter(LANES, len(states) * LANES)
    wide = jnp.concatenate(states, axis=1)
    high = wide.astype(bf16)
    low = wide - high.astype(f32)
    blocks = lambda a: jnp.where(mask, jnp.concatenate([a] * PER_TILE, axis=0), 0.0).astype(bf16)
    stacked = jnp.concatenate([blocks(high.astype(f32)), blocks(low)], axis=0)
    return jnp.dot(jnp.concatenate([decays, decays], axis=1), stacked, preferred_element_type=f32)


def starts_of(lam, weight):
    index = iota((CH, LANES), 0).astype(f32)
    return (weight * jnp.exp(-index * lam)).astype(bf16)


def energy_row(partial):
    return lax.dot_general(
        jnp.ones((8, LANES), f32), partial, (((1,), (1,)), ((), ())), preferred_element_type=f32, precision=highest
    )


def gate_kernel(
    chunks, tiles, local_ref, q_hbm, in_ref, p1_ref, p2_ref, spread_ref, tail_ref, taps_ref, rates_ref, coeff_ref,
    gated_ref, energy_ref, q_ref, weight_ref, taps_rev, lhs_all, total_ref, in_sems,
):
    width = tiles * LANES
    inputs = [(q_hbm, q_ref, 0, 0)]
    for c in range(chunks):
        for copy in copies(inputs, in_sems, c, width):
            copy.start()
    weight_ref[...] = by_tile(coeff_ref[...].T)
    taps_rev[...] = reversed_lags(taps_ref[...])
    total_ref[...] = jnp.zeros_like(total_ref)
    lower = iota((CH, LANES), 1) <= iota((CH, LANES), 0)
    masks = fold_masks()

    @pl.loop(0, chunks)
    def _(c):
        for copy in copies(inputs, in_sems, c, width):
            copy.wait()
        for t in range(tiles):
            lanes = lanes_at(c * tiles + t, LANES)
            lhs_ref = lhs_all.at[t % 2]
            for f in range(PER_TILE):
                a, rows = f % PARTS, slice(f // PARTS * CH, (f // PARTS + 1) * CH)
                at = pl.ds((c * tiles + t) * PER_TILE + f, 1)
                lhs_ref[rows, a * CH : (a + 1) * CH] = jnp.where(lower, 0.0, toeplitz(taps_rev[at, :])).astype(bf16)
            tail = tail_ref[:, lanes]
            masked = jnp.concatenate([tail * mask for mask in masks], axis=0)
            carried = unfold(jnp.dot(lhs_ref[...], masked, preferred_element_type=f32))
            decay = jnp.exp(-float(CH) * spread_ref[:, lanes])
            z0 = in_ref[:, lanes]
            entry = decay * z0
            z1 = entry + p1_ref[:, lanes]
            z2 = decay * entry + p2_ref[:, lanes]
            row = pl.ds(c * tiles + t, 1)
            cross = cross_of(starts_of(rates_ref[row, :], weight_ref[row, :]), [z0, z1, z2])
            for i in range(3):
                rows = slice(i * CH, (i + 1) * CH)
                conv = local_ref[rows, lanes].astype(f32) + cross[:, i * LANES : (i + 1) * LANES]
                if i == 0:
                    conv = conv + carried
                gated = conv * q_ref[rows, lanes].astype(f32)
                gated_ref[rows, lanes] = gated.astype(bf16)
                total_ref[rows] += gated * gated

    energy_ref[...] = energy_row(total_ref[...])


def gate_part(local, query_rows, incoming, p1, p2, rates_spread, tail, taps, rate_rows, coeff_t):
    tokens, channels = local.shape
    chunks = 4
    tiles = channels // LANES // chunks
    return pl.pallas_call(
        functools.partial(gate_kernel, chunks, tiles),
        in_specs=[VMEM, HBM] + [VMEM] * 8,
        out_specs=[VMEM, VMEM],
        out_shape=[jax.ShapeDtypeStruct((tokens, channels), bf16), jax.ShapeDtypeStruct((8, tokens), f32)],
        scratch_shapes=[
            pltpu.VMEM((tokens, channels), bf16), pltpu.VMEM(rate_rows.shape, f32), pltpu.VMEM(taps.shape, f32),
            pltpu.VMEM((2, FOLD * CH, PARTS * CH), bf16), pltpu.VMEM((tokens, LANES), f32),
            pltpu.SemaphoreType.DMA((1, chunks)),
        ],
        compiler_params=params(),
        cost_estimate=pl.CostEstimate(
            flops=channels * CH * 2048, bytes_accessed=channels * tokens * 6, transcendentals=channels * CH
        ),
        name="gate",
    )(local, query_rows, incoming, p1, p2, rates_spread, tail, taps, rate_rows, coeff_t)


def norm_kernel(terms, chunks, tiles, *refs):
    energies, (gated_ref, gain_ref) = refs[:terms], refs[terms : terms + 2]
    out_hbm, out_ref, scale_ref, out_sems = refs[-4:]
    width = tiles * LANES
    rows = gated_ref.shape[0]
    outputs = [(out_ref, out_hbm, 0, 0)]
    energy = sum(ref[...] for ref in energies)
    scale_ref[...] = lax.rsqrt(tn_dot(energy, jnp.full((8, LANES), 0.125, f32), highest) / D + 1e-05)

    @pl.loop(0, chunks)
    def _(c):
        for r in range(0, rows, CH):
            scale = scale_ref[r : r + CH]
            for t in range(tiles):
                lanes = lanes_at(c * tiles + t, LANES)
                value = gated_ref[r : r + CH, lanes].astype(f32) * scale * gain_ref[:, lanes]
                out_ref[r : r + CH, lanes] = value.astype(bf16)
        for copy in copies(outputs, out_sems, c, width):
            copy.start()

    drain(chunks, width, outputs, out_sems)


def norm_part(energies, gated, gain_row):
    rows, channels = gated.shape
    chunks = 4
    tiles = channels // LANES // chunks
    return pl.pallas_call(
        functools.partial(norm_kernel, len(energies), chunks, tiles),
        in_specs=[VMEM] * (len(energies) + 2),
        out_specs=HBM,
        out_shape=jax.ShapeDtypeStruct((rows, channels), bf16),
        scratch_shapes=[
            pltpu.VMEM((rows, channels), bf16), pltpu.VMEM((rows, LANES), f32), pltpu.SemaphoreType.DMA((1, chunks)),
        ],
        compiler_params=params(),
        cost_estimate=pl.CostEstimate(flops=rows * channels * 2, bytes_accessed=rows * channels * 4, transcendentals=0),
        name="norm",
    )(*energies, gated, gain_row)


def regroup(block):
    shape = block.shape
    sub = iota(shape, 1)
    lane = iota(shape, 2) // GW
    for k in (1, 2, 4):
        up = pltpu.roll(pltpu.roll(block, 8 - k, 1), GW * k, 2)
        down = pltpu.roll(pltpu.roll(block, k, 1), LANES - GW * k, 2)
        row_bit, lane_bit = (sub & k) != 0, (lane & k) != 0
        block = jnp.where(row_bit == lane_bit, block, jnp.where(lane_bit, up, down))
    return block


def ranks_of(present):
    count = present.shape[1]
    before = (iota((count, count), 0) < iota((count, count), 1)).astype(bf16)
    return jnp.dot(present.astype(bf16), before, preferred_element_type=f32)


def select_kernel(blocks, slots, inner, outer, me_ref, tail_ref, plan_ref, *refs):
    outs, (items_ref, picks_ref) = refs[:2], refs[2:]
    groups = plan_ref.shape[1]

    @pl.when(me_ref[0] != inner * outer - 1)
    def _():
        for out in outs:
            out[...] = jnp.zeros_like(out)

    @pl.when(me_ref[0] == inner * outer - 1)
    def _():
        for g in range(0, groups // PER_TILE, 2):
            halves = []
            for side in range(2):
                tile = g + side
                rows = tail_ref[:, tile * LANES : (tile + 1) * LANES].astype(f32)
                halves.append(regroup(rows.reshape(2 * blocks, 8, LANES)))
            for b in range(blocks):
                for half in range(2):
                    both = jnp.concatenate([halves[0][2 * b + half], halves[1][2 * b + half]], axis=0)
                    items_ref[
                        b * groups + g * 8 : b * groups + (g + 2) * 8, half * LANES : (half + 1) * LANES
                    ] = both.astype(bf16)
        plan = plan_ref[...]
        readers = iota((inner * outer, 1, 1), 0)
        mine = (plan[None] == readers).astype(f32)
        ranks = ranks_of(jnp.sum(mine, axis=1))
        slot = iota((slots, groups), 0).astype(f32).astype(bf16)
        low = inner // 2
        for o in range(outer):
            for p in range(inner):
                r = o * inner + p
                for b in range(blocks):
                    rank = jnp.where(plan[b : b + 1] == r, ranks[r : r + 1], -1.0)
                    rank = jnp.broadcast_to(rank, (slots, groups)).astype(bf16)
                    picks_ref[p * slots : (p + 1) * slots, b * groups : (b + 1) * groups] = jnp.where(
                        rank == slot, jnp.ones((), bf16), jnp.zeros((), bf16)
                    )
            total = jnp.dot(picks_ref[...], items_ref[...], preferred_element_type=f32)
            total = total.astype(bf16).reshape(2, low, slots, MODES * GW)
            for side in range(2):
                outs[side][o] = total[side]


def select_tails(me, tail, plan_cols, inner, outer, slots):
    rows = tail.shape[0]
    groups = plan_cols.shape[1]
    blocks = rows // MODES
    vmem = pl.BlockSpec(memory_space=pltpu.VMEM)
    return pl.pallas_call(
        functools.partial(select_kernel, blocks, slots, inner, outer),
        in_specs=[pl.BlockSpec(memory_space=pltpu.SMEM), vmem, vmem],
        out_specs=[vmem] * 2,
        out_shape=[jax.ShapeDtypeStruct((outer, inner // 2, slots, MODES * GW), bf16)] * 2,
        scratch_shapes=[
            pltpu.VMEM((blocks * groups, MODES * GW), bf16), pltpu.VMEM((inner * slots, blocks * groups), bf16),
        ],
        compiler_params=params(),
        cost_estimate=pl.CostEstimate(flops=10**9, bytes_accessed=2 * 10**6, transcendentals=0),
        name="select_tails",
    )(me, tail, plan_cols)


def handoff_kernel(me_ref, final_ref, norm_ref, plan_ref, got_ref, out_ref, items_ref):
    groups = plan_ref.shape[1]
    capacity = out_ref.shape[2]
    slots = got_ref.shape[0]
    plan = plan_ref[...]
    mine = plan == me_ref[0]
    present = jnp.sum(mine.astype(f32), axis=0, keepdims=True)
    rank = ranks_of(jnp.broadcast_to(present, (8, groups)))[:1]
    final = final_ref[...] * norm_ref[...]
    stack = [
        final[half * 8 : (half + 1) * 8, g * LANES : (g + 1) * LANES]
        for half in range(2) for g in range(groups // PER_TILE)
    ]
    done = regroup(jnp.stack(stack, axis=0)).reshape(2 * groups, LANES).astype(bf16)
    items_ref[:, :LANES] = done[:groups]
    items_ref[:, LANES:] = done[groups:]
    slot = iota((slots, groups), 0).astype(f32)
    last = plan.shape[0] - 1
    at = (jnp.broadcast_to(rank, (slots, groups)) == slot) & mine[last:]
    pick = jnp.where(at, 1.0, 0.0).astype(bf16)
    rows = jnp.dot(pick, items_ref[...], preferred_element_type=f32)
    rows = (rows + got_ref[...].astype(f32)).T
    out_ref[...] = rows[:, :capacity].reshape(out_ref.shape)


def assemble(me, final, norm_spread, plan_cols, got, capacity):
    groups = plan_cols.shape[1]
    vmem = pl.BlockSpec(memory_space=pltpu.VMEM)
    out = pl.pallas_call(
        handoff_kernel,
        in_specs=[pl.BlockSpec(memory_space=pltpu.SMEM), vmem, vmem, vmem, vmem],
        out_specs=vmem,
        out_shape=jax.ShapeDtypeStruct((MODES, GW, capacity), f32),
        scratch_shapes=[pltpu.VMEM((groups, MODES * GW), bf16)],
        compiler_params=params(),
        cost_estimate=pl.CostEstimate(flops=10**9, bytes_accessed=10**6, transcendentals=0),
        name="handoff",
    )(me, final, norm_spread, plan_cols, got)
    return out.transpose(2, 0, 1)


def hold_kernel(*refs):
    pass


def hold(array, after):
    anywhere = pl.BlockSpec(memory_space=pl.ANY)
    return pl.pallas_call(
        hold_kernel,
        in_specs=[anywhere, anywhere],
        out_specs=anywhere,
        out_shape=jax.ShapeDtypeStruct(array.shape, array.dtype),
        input_output_aliases={0: 0},
        name="hold",
    )(array, after)


def scatter_tails(selected, inner, outer):
    count = inner * outer
    me = lax.axis_index("seq")
    half = inner // 2
    low, high = selected
    sent = lax.ppermute(low, "seq", [(count - 1, count - 1 - half)])
    block = jnp.where((me & half) != 0, high, sent)
    heads = [half - 1, inner - 1]
    own = block[outer - 1]
    for o in range(outer - 1):
        pairs = [(count - inner + h, o * inner + h) for h in heads]
        sent = lax.ppermute(block[o], "seq", pairs)
        own = jnp.where(me // inner == o, sent, own)
    half //= 2
    while half:
        pairs = [(i, i - half) for i in range(count) if (i + 1) % (2 * half) == 0]
        sent = lax.ppermute(own[:half], "seq", pairs)
        own = jnp.where((me & half) != 0, own[half:], sent)
        half //= 2
    return own[0]


def scan_states(own, sent, rates_spread, tokens):
    count = lax.axis_size("seq")
    me = lax.axis_index("seq")
    total, incoming = own, jnp.zeros_like(own)
    stages = []
    step = 1
    while step < count:
        pairs = [(i, i ^ step) for i in range(count)]
        other = lax.ppermute(sent, "seq", pairs).astype(f32)
        right = (me & step) != 0
        offset = ((me & (step - 1)) * tokens).astype(f32)
        incoming = jnp.where(right, incoming + jnp.exp(-rates_spread * offset) * other, incoming)
        decay = jnp.exp(-rates_spread * float(step * tokens))
        total = jnp.where(right, decay * other + total, decay * total + other)
        sent = total.astype(bf16)
        stages.append(sent)
        step *= 2
    return total, incoming, stages


def sum_over_chan(energy):
    if lax.axis_size("chan") == 2:
        return [energy, lax.ppermute(energy, "chan", [(0, 1), (1, 0)])]
    return [lax.psum(energy, "chan")]


def per_device(
    query_rows, key_rows, value_rows, residues, decay_rates, medium_taps, out_gain, reader_plan
):
    tokens, channels = query_rows.shape
    groups, mode_count = residues.shape
    blocks = medium_taps.shape[1] // mode_count
    seq_count = lax.axis_size("seq")
    me = lax.axis_index("seq")

    rates_t = decay_rates.T
    own_tail, p1, p2, own, sent, rate_rows = product_and_states(key_rows, value_rows, rates_t)
    rates_spread = spread_rates(rates_t)
    total, incoming, stages = scan_states(own, sent, rates_spread, tokens)
    onward = [(i, i + 1) for i in range(seq_count - 1)]
    tail_prev = lax.ppermute(hold(own_tail, stages[0]), "seq", onward)

    coeff_t = residues.T * jnp.sqrt(-jnp.expm1(-2.0 * rates_t))
    norm_spread = jnp.sqrt(-jnp.expm1(-2.0 * rates_spread))
    plan_cols = reader_plan.T

    inner = 1 << (int(math.log2(seq_count)) // 2)
    outer = seq_count // inner
    capacity = (groups * (blocks + 1) + seq_count - 1) // seq_count + 1
    slots = -(-capacity // 16) * 16
    selected = select_tails(me.reshape(1), own_tail, plan_cols, inner, outer, slots)
    got = scatter_tails(selected, inner, outer)

    local = local_part(key_rows, value_rows, medium_taps, rates_t, coeff_t, stages[0])
    gated, energy = gate_part(
        local, query_rows, incoming, p1, p2, rates_spread, tail_prev, medium_taps, rate_rows, coeff_t
    )
    mixed = norm_part(sum_over_chan(energy), gated, out_gain[None, :])
    handoff = assemble(me.reshape(1), total, norm_spread, plan_cols, got, capacity)
    return mixed, handoff


def solution(mesh):
    placed = (
        P("seq", "chan"),
        P("seq", "chan"),
        P("seq", "chan"),
        P("chan", None),
        P("chan", None),
        P("chan", None),
        P("chan"),
        P("chan", None),
    )
    return jax.shard_map(
        per_device,
        mesh=mesh,
        in_specs=placed,
        out_specs=(P("seq", "chan"), P("seq", None, "chan")),
        check_vma=False,
    )
```

time: 94.9 us -> 74.2 us (0.78)
  the two profiles are of different devices: /device:TPU:0 before, /device:TPU:17 now
where the time goes in v1:
time: 74.2 us; the launch traced here: 73.7 us
  Pallas kernels  31 us (42%)
  starting transfers between devices  19.5 us (26%)
  waiting for transfers between devices  9.74 us (13%)
  local copies, waits for them, and re-layouts  6.6 us (9%)
  other arithmetic  5.82 us (8%)
  between operations  1.13 us (2%)
    pallas_call x1, Pallas kernels, local_part(): pl.pallas_call(functools.partial(local_kernel, chunks, tiles), in_specs=[...  11.4 us
    ppermute x4, starting transfers between devices, scan_states(): other = lax.ppermute(sent, 'seq', pairs).astype(f32)  8.23 us
    pallas_call x1, Pallas kernels, gate_part(): pl.pallas_call(functools.partial(gate_kernel, chunks, tiles), in_specs=[V...  7.08 us
    unnamed x42, local copies, waits for them, and re-layouts  6.56 us
    pallas_call x1, Pallas kernels, product_and_states(): pl.pallas_call(functools.partial(product_kernel, chunks, tiles), in_specs...  6.56 us
    ppermute x1, waiting for transfers between devices, scatter_tails(): sent = lax.ppermute(own[:half], 'seq', pairs)  5.96 us
    ppermute x1, starting transfers between devices, sum_over_chan(): return [energy, lax.ppermute(energy, 'chan', [(0, 1), (1, 0)])]  4.1 us
    ppermute x4, waiting for transfers between devices, scan_states(): other = lax.ppermute(sent, 'seq', pairs).astype(f32)  3.76 us
  transfers between devices with their start and end apart: 11, of which 2 were waited for; matrix products, arithmetic and copies ran while one was open for 8% of the time, Pallas kernels for 20%

profile of v1, /device:TPU:17, one launch (start us, length us, event | category | flops | bytes accessed | tf_op | source)
XLA Modules:
  0.0 73.7 jit_solution(1610876958473192380)
XLA Ops:
  0.6 0.0 copy-start.17
  0.6 0.0 copy-start.10
  0.7 0.0 copy-start.20
  0.7 6.6 %product_states.1 = (bf16[128,4096]{1,0:T(8,128)(2,1)}, f32[16,4096]{1,0:T(8,128)}, f32[16,4096]{1,0:T(8,128)}, f32[16,4096]{1,0:T(8,128)}, bf16[16,4096]{1,0:T(8,128)(2,1)}, /*index=5*/f32[32,128]{1,0:T(8,128)}) custom-call(bf16[384,4096]{1,0:T(8,128)(2,1)} %k_hbm.3, bf16[384,4096]{1,0:T(8,128)(2,1)} %v_hbm.3, f32[16,256]{1,0:T(8,128)} %bitcast.24), custom_call_target="tpu_custom_call" | custom-call | flops 1207959552 | bytes 9437184 | tf_op jit(solution)/shard_map/product_states/pallas_call | solution.py:124
  7.2 1.3 %collective-permute-start = (bf16[16,4096]{1,0:T(8,128)(2,1)}, bf16[16,4096]{1,0:T(8,128)(2,1)}, u32[]{:S(2)}, u32[]{:S(2)}) collective-permute-start(bf16[16,4096]{1,0:T(8,128)(2,1)} %get-tuple-element.12), channel_id=1, source_target_pairs={{0,2},{2,0},{4,6},{6,4},{8,10},{10,8},{12,14},{14,12},{16,18},{18,... | collective-permute-start | bytes 393224 | tf_op jit(solution)/shard_map/ppermute | solution.py:561
  8.5 0.0 copy-done.17
  8.5 1.2 %copy-done.3 = bf16[128,4096]{1,0:T(8,128)(2,1)S(1)} copy-done((bf16[128,4096]{1,0:T(8,128)(2,1)S(1)}, bf16[128,4096]{1,0:T(8,128)(2,1)}, u32[]{:S(2)}) %copy-start.3) | copy-done | bytes 1048600
  9.7 0.9 %select_tails.1 = (bf16[4,2,160,256]{3,2,1,0:T(8,128)(2,1)}, bf16[4,2,160,256]{3,2,1,0:T(8,128)(2,1)S(1)}) custom-call(s32[1]{0:T(128)} %bitcast.3.me_ref, bf16[128,4096]{1,0:T(8,128)(2,1)S(1)} %copy-done.3, s32[9,256]{1,0:T(8,128)S(1)} %bitcast.28), custom_call_target="tpu_custom_call" | custom-call | flops 1000000000 | bytes 2000000 | tf_op jit(solution)/shard_map/select_tails/pallas_call | solution.py:460
  10.7 0.9 %copy-done.4 = bf16[4,2,160,256]{3,2,1,0:T(8,128)(2,1)} copy-done((bf16[4,2,160,256]{3,2,1,0:T(8,128)(2,1)}, bf16[4,2,160,256]{3,2,1,0:T(8,128)(2,1)S(1)}, u32[]{:S(2)}) %copy-start.4) | copy-done | bytes 655384
  11.5 1.5 %collective-permute-start.6 = (bf16[4,2,160,256]{3,2,1,0:T(8,128)(2,1)}, bf16[4,2,160,256]{3,2,1,0:T(8,128)(2,1)}, u32[]{:S(2)}, u32[]{:S(2)}) collective-permute-start(bf16[4,2,160,256]{3,2,1,0:T(8,128)(2,1)} %get-tuple-element.21), channel_id=1, source_target_pairs={{30,26},{31,27}} | collective-permute-start | bytes 1966088 | tf_op jit(solution)/shard_map/ppermute | solution.py:536
  13.0 0.0 copy-done.10
  13.0 0.7 %spread_rates.1.spread_ref = f32[16,4096]{1,0:T(8,128)S(1)} custom-call(f32[16,256]{1,0:T(8,128)S(1)} %bitcast.25), custom_call_target="tpu_custom_call" | custom-call | tf_op jit(solution)/shard_map/spread_rates/pallas_call | solution.py:157
  13.8 0.0 copy-done.20
  13.8 0.6 bitcast_multiply_fusion.coeff_ref
  14.4 0.0 collective-permute-done
  14.4 1.1 %fusion.14.after.refs_1_ = bf16[16,4096]{1,0:T(8,128)(2,1)S(1)} fusion(f32[16,4096]{1,0:T(8,128)} %get-tuple-element.13, bf16[16,4096]{1,0:T(8,128)(2,1)} %collective-permute-done, f32[16,4096]{1,0:T(8,128)S(1)} %spread_rates.1.spread_ref, pred[]{:T(512)S(6)} %ne.26), kind=kLoop, calls=%fused_computation.36 | loop fusion | flops 589824 | bytes 786433 | tf_op jit(solution)/shard_map/convert_element_type | solution.py:567
  15.5 0.0 copy-start.6
  15.5 1.3 %collective-permute-start.1 = (bf16[16,4096]{1,0:T(8,128)(2,1)S(1)}, bf16[16,4096]{1,0:T(8,128)(2,1)}, u32[]{:S(2)}, u32[]{:S(2)}) collective-permute-start(bf16[16,4096]{1,0:T(8,128)(2,1)S(1)} %fusion.14.after.refs_1_), channel_id=1, source_target_pairs={{0,4},{2,6},{4,0},{6,2},{8,12},{10,14},{12,8},{14,10},{16,20},{18,... | collective-permute-start | bytes 393224 | tf_op jit(solution)/shard_map/ppermute | solution.py:561
  16.8 0.0 copy-done.6
  16.8 2.2 %collective-permute-start.4 = (bf16[128,4096]{1,0:T(8,128)(2,1)}, bf16[128,4096]{1,0:T(8,128)(2,1)S(1)}, u32[]{:S(2)}, u32[]{:S(2)}) collective-permute-start(bf16[128,4096]{1,0:T(8,128)(2,1)} %hold.1), channel_id=1, source_target_pairs={{0,2},{2,4},{4,6},{6,8},{8,10},{10,12},{12,14},{14,16},{16,18},{18... | collective-permute-start | bytes 3145736 | tf_op jit(solution)/shard_map/ppermute | solution.py:593
  19.0 0.0 copy-done
  19.0 0.0 copy-start.1
  19.0 1.9 %copy-done.1 = bf16[384,4096]{1,0:T(8,128)(2,1)S(1)} copy-done((bf16[384,4096]{1,0:T(8,128)(2,1)S(1)}, bf16[384,4096]{1,0:T(8,128)(2,1)}, u32[]{:S(2)}) %copy-start.1) | copy-done | bytes 3145752
  20.9 0.9 %copy-done.7 = bf16[16,4096]{1,0:T(8,128)(2,1)S(1)} copy-done((bf16[16,4096]{1,0:T(8,128)(2,1)S(1)}, bf16[16,4096]{1,0:T(8,128)(2,1)}, u32[]{:S(2)}) %copy-start.7) | copy-done | bytes 131096
  21.8 0.9 %copy-done.11 = f32[256,128]{1,0:T(8,128)S(1)} copy-done((f32[256,128]{1,0:T(8,128)S(1)}, f32[256,128]{1,0:T(8,128)}, u32[]{:S(2)}) %copy-start.11) | copy-done | bytes 131096
  22.7 0.7 copy-done.13
  23.4 11.4 %local_conv.1.local_ref = bf16[384,4096]{1,0:T(8,128)(2,1)S(1)} custom-call(bf16[384,4096]{1,0:T(8,128)(2,1)S(1)} %copy-done, bf16[384,4096]{1,0:T(8,128)(2,1)S(1)} %copy-done.1, f32[256,128]{1,0:T(8,128)S(1)} %copy-done.11, f32[16,256]{1,0:T(8,128)S(1)} %bitcast.26, f32[16,256]{1,0:T(8,128)S(1)} %copy-done.13, bf16[16,4096]{1,0:T(8,128)(2,1)S(1)} %copy-done.7), custom_call_target="tpu_custom_call" | custom-call | flops 8589934592 | bytes 6291456 | tf_op jit(solution)/shard_map/local_conv/pallas_call | solution.py:242
  34.8 0.0 collective-permute-done.1
  34.8 0.0 copy-done.19
  34.8 1.1 %fusion.15 = (bf16[16,4096]{1,0:T(8,128)(2,1)S(1)}, f32[16,4096]{1,0:T(8,128)S(1)}) fusion(f32[16,4096]{1,0:T(8,128)S(1)} %copy-done.19, bf16[16,4096]{1,0:T(8,128)(2,1)} %collective-permute-done, pred[]{:T(512)S(6)} %ne.26, bf16[16,4096]{1,0:T(8,128)(2,1)} %collective-permute-done.1, f32[16,4096]{1,0:T(8,128)S(1)} %spread_rates.1.spread_ref, pred[]{:T(512)S(6)} %ne.29), kind=kLoop, calls=%fused_computation.38 | loop fusion | flops 1048576 | bytes 1179650 | tf_op jit(solution)/shard_map/convert_element_type | solution.py:567
  36.0 5.6 %collective-permute-start.2 = (bf16[16,4096]{1,0:T(8,128)(2,1)S(1)}, bf16[16,4096]{1,0:T(8,128)(2,1)S(1)}, u32[]{:S(2)}, u32[]{:S(2)}) collective-permute-start(bf16[16,4096]{1,0:T(8,128)(2,1)S(1)} %get-tuple-element.22), channel_id=1, source_target_pairs={{0,8},{2,10},{4,12},{6,14},{8,0},{10,2},{12,4},{14,6},{16,24},{18,... | collective-permute-start | bytes 393224 | tf_op jit(solution)/shard_map/ppermute | solution.py:561
  41.6 0.0 collective-permute-done.6
  41.6 0.0 copy-done.5
  41.6 0.0 copy-start.9
  41.6 0.0 copy-start.12
  41.6 0.0 copy-start.14
  41.6 0.0 copy-start.16
  41.6 1.3 %broadcast_select_fusion = bf16[4,2,160,256]{3,2,1,0:T(8,128)(2,1)S(1)} fusion(bf16[4,2,160,256]{3,2,1,0:T(8,128)(2,1)S(1)} %copy-done.5, bf16[4,2,160,256]{3,2,1,0:T(8,128)(2,1)} %collective-permute-done.6, pred[]{:T(512)S(6)} %ne.29), kind=kLoop, calls=%fused_computation | loop fusion | flops 327680 | bytes 1966081 | tf_op jit(solution)/shard_map/jit(_where)/select_n | solution.py:537
  43.0 0.7 collective-permute-start.9
  43.7 0.7 collective-permute-start.8
  44.3 0.7 collective-permute-start.7
  45.0 0.0 collective-permute-done.2
  45.0 0.2 negate_sqrt_fusion
  45.3 0.1 collective-permute-start.3
  45.3 0.0 collective-permute-done.9
  45.4 0.0 collective-permute-done.8
  45.4 0.0 collective-permute-done.7
  45.4 0.1 fusion.11
  45.4 1.5 %collective-permute-start.10 = (bf16[1,160,256]{2,1,0:T(8,128)(2,1)S(1)}, bf16[1,160,256]{2,1,0:T(8,128)(2,1)S(1)}, u32[]{:S(2)}, u32[]{:S(2)}) collective-permute-start(bf16[1,160,256]{2,1,0:T(8,128)(2,1)S(1)} %slice.29), channel_id=1, source_target_pairs={{2,0},{6,4},{10,8},{14,12},{18,16},{22,20},{26,24},{30,28},{3,1},{... | collective-permute-start | bytes 245768 | tf_op jit(solution)/shard_map/ppermute | solution.py:547
  46.9 3.8 %collective-permute-done.3 = bf16[16,4096]{1,0:T(8,128)(2,1)S(1)} collective-permute-done((bf16[16,4096]{1,0:T(8,128)(2,1)S(1)}, bf16[16,4096]{1,0:T(8,128)(2,1)S(1)}, u32[]{:S(2)}, u32[]{:S(2)}) %collective-permute-start.3) | collective-permute-done | bytes 131104 | tf_op jit(solution)/shard_map/ppermute | solution.py:561
  50.7 1.4 %fusion.8 = (f32[16,4096]{1,0:T(8,128)S(1)}, f32[16,4096]{1,0:T(8,128)S(1)}) fusion(bf16[16,4096]{1,0:T(8,128)(2,1)S(1)} %collective-permute-done.3, f32[16,4096]{1,0:T(8,128)S(1)} %spread_rates.1.spread_ref, pred[]{:T(512)S(6)} %ne.27, f32[16,4096]{1,0:T(8,128)S(1)} %get-tuple-element.23, bf16[16,4096]{1,0:T(8,128)(2,1)S(1)} %collective-permute-done.2, ...), kind=kLoop, calls=%fused_computation.24 | loop fusion | flops 2097152 | bytes 1572880 | tf_op jit(solution)/shard_map/jit(_where)/select_n | solution.py:566
  52.0 6.0 %collective-permute-done.10 = bf16[1,160,256]{2,1,0:T(8,128)(2,1)S(1)} collective-permute-done((bf16[1,160,256]{2,1,0:T(8,128)(2,1)S(1)}, bf16[1,160,256]{2,1,0:T(8,128)(2,1)S(1)}, u32[]{:S(2)}, u32[]{:S(2)}) %collective-permute-start.10) | collective-permute-done | bytes 81952 | tf_op jit(solution)/shard_map/ppermute | solution.py:547
  58.0 0.0 collective-permute-done.4.tail_ref
  58.0 0.0 copy-done.2
  58.0 0.0 copy-done.8
  58.1 0.0 copy-start.18
  58.1 7.1 %gate.1 = (bf16[384,4096]{1,0:T(8,128)(2,1)S(1)}, f32[8,384]{1,0:T(8,128)S(1)}) custom-call(bf16[384,4096]{1,0:T(8,128)(2,1)S(1)} %local_conv.1.local_ref, bf16[384,4096]{1,0:T(8,128)(2,1)S(1)} %copy-done.2, f32[16,4096]{1,0:T(8,128)S(1)} %get-tuple-element.28.in_ref, f32[16,4096]{1,0:T(8,128)S(1)} %copy-done.8, f32[16,4096]{1,0:T(8,128)S(1)} %copy-done.9, ...), custom_call_target="tpu_custom_call" | custom-call | flops 1073741824 | bytes 9437184 | tf_op jit(solution)/shard_map/gate/pallas_call | solution.py:334
  65.2 0.0 copy-start.15
  65.2 4.1 %collective-permute-start.5 = (f32[8,384]{1,0:T(8,128)S(1)}, f32[8,384]{1,0:T(8,128)S(1)}, u32[]{:S(2)}, u32[]{:S(2)}) collective-permute-start(f32[8,384]{1,0:T(8,128)S(1)} %get-tuple-element.18.refs_0_), channel_id=1, source_target_pairs={{0,1},{1,0},{2,3},{3,2},{4,5},{5,4},{6,7},{7,6},{8,9},{9,8},{10,11... | collective-permute-start | bytes 36872 | tf_op jit(solution)/shard_map/ppermute | solution.py:575
  69.3 0.0 copy-done.18
  69.3 1.3 %handoff.1 = f32[16,16,145]{2,1,0:T(8,128)} custom-call(s32[1]{0:T(128)} %bitcast.3.me_ref, f32[16,4096]{1,0:T(8,128)S(1)} %get-tuple-element.27.final_ref, f32[16,4096]{1,0:T(8,128)S(1)} %get-tuple-element.29.norm_ref, s32[9,256]{1,0:T(8,128)S(1)} %bitcast.29, bf16[160,256]{1,0:T(8,128)(2,1)S(1)} %fusion.12.got_ref), custom_call_target="tpu_custom_call" | custom-call | flops 1000000000 | bytes 1000000 | tf_op jit(solution)/shard_map/handoff/pallas_call | solution.py:502
  70.6 0.0 collective-permute-done.5.refs_1_
  70.6 0.0 copy-done.15
  70.6 3.0 %norm.1 = bf16[384,4096]{1,0:T(8,128)(2,1)} custom-call(f32[8,384]{1,0:T(8,128)S(1)} %get-tuple-element.18.refs_0_, f32[8,384]{1,0:T(8,128)S(1)} %collective-permute-done.5.refs_1_, bf16[384,4096]{1,0:T(8,128)(2,1)S(1)} %get-tuple-element.19.refs_2_, f32[1,4096]{1,0:T(1,128)S(1)} %bitcast.27), custom_call_target="tpu_custom_call" | custom-call | flops 3145728 | bytes 6291456 | tf_op jit(solution)/shard_map/norm/pallas_call | solution.py:379
  (18 shorter events, 0.1 us)
Async XLA Ops:
  0.6 7.9 %copy-start.17 = (s32[256,9]{0,1:T(8,128)S(1)}, s32[256,9]{0,1:T(8,128)}, u32[]{:S(2)}) copy-start(s32[256,9]{0,1:T(8,128)} %param.15) | copy-start | bytes 27652
  0.6 12.4 %copy-start.10 = (f32[256,16]{0,1:T(8,128)S(1)}, f32[256,16]{0,1:T(8,128)}, u32[]{:S(2)}) copy-start(f32[256,16]{0,1:T(8,128)} %param.12) | copy-start | bytes 49156
  0.7 13.1 %copy-start.20 = (f32[256,16]{0,1:T(8,128)S(1)}, f32[256,16]{0,1:T(8,128)}, u32[]{:S(2)}) copy-start(f32[256,16]{0,1:T(8,128)} %param.11) | copy-start | bytes 49156
  7.2 7.2 %collective-permute-start = (bf16[16,4096]{1,0:T(8,128)(2,1)}, bf16[16,4096]{1,0:T(8,128)(2,1)}, u32[]{:S(2)}, u32[]{:S(2)}) collective-permute-start(bf16[16,4096]{1,0:T(8,128)(2,1)} %get-tuple-element.12), channel_id=1, source_target_pairs={{0,2},{2,0},{4,6},{6,4},{8,10},{10,8},{12,14},{14,12},{16,18},{18,... | collective-permute-start | bytes 393224 | tf_op jit(solution)/shard_map/ppermute | solution.py:561
  8.5 1.2 %copy-start.3 = (bf16[128,4096]{1,0:T(8,128)(2,1)S(1)}, bf16[128,4096]{1,0:T(8,128)(2,1)}, u32[]{:S(2)}) copy-start(bf16[128,4096]{1,0:T(8,128)(2,1)} %get-tuple-element.16.refs_0_.tail_ref) | copy-start | bytes 3145732
  9.7 9.3 %copy-start = (bf16[384,4096]{1,0:T(8,128)(2,1)S(1)}, bf16[384,4096]{1,0:T(8,128)(2,1)}, u32[]{:S(2)}) copy-start(bf16[384,4096]{1,0:T(8,128)(2,1)} %k_hbm.3) | copy-start | bytes 9437188
  10.7 0.9 %copy-start.4 = (bf16[4,2,160,256]{3,2,1,0:T(8,128)(2,1)}, bf16[4,2,160,256]{3,2,1,0:T(8,128)(2,1)S(1)}, u32[]{:S(2)}) copy-start(bf16[4,2,160,256]{3,2,1,0:T(8,128)(2,1)S(1)} %get-tuple-element.20) | copy-start | bytes 1966084
  11.5 30.0 %collective-permute-start.6 = (bf16[4,2,160,256]{3,2,1,0:T(8,128)(2,1)}, bf16[4,2,160,256]{3,2,1,0:T(8,128)(2,1)}, u32[]{:S(2)}, u32[]{:S(2)}) collective-permute-start(bf16[4,2,160,256]{3,2,1,0:T(8,128)(2,1)} %get-tuple-element.21), channel_id=1, source_target_pairs={{30,26},{31,27}} | collective-permute-start | bytes 1966088 | tf_op jit(solution)/shard_map/ppermute | solution.py:536
  15.5 1.3 %copy-start.6 = (bf16[16,4096]{1,0:T(8,128)(2,1)}, bf16[16,4096]{1,0:T(8,128)(2,1)S(1)}, u32[]{:S(2)}) copy-start(bf16[16,4096]{1,0:T(8,128)(2,1)S(1)} %fusion.14.after.refs_1_) | copy-start | bytes 393220
  15.5 19.3 %collective-permute-start.1 = (bf16[16,4096]{1,0:T(8,128)(2,1)S(1)}, bf16[16,4096]{1,0:T(8,128)(2,1)}, u32[]{:S(2)}, u32[]{:S(2)}) collective-permute-start(bf16[16,4096]{1,0:T(8,128)(2,1)S(1)} %fusion.14.after.refs_1_), channel_id=1, source_target_pairs={{0,4},{2,6},{4,0},{6,2},{8,12},{10,14},{12,8},{14,10},{16,20},{18,... | collective-permute-start | bytes 393224 | tf_op jit(solution)/shard_map/ppermute | solution.py:561
  16.8 41.2 %collective-permute-start.4 = (bf16[128,4096]{1,0:T(8,128)(2,1)}, bf16[128,4096]{1,0:T(8,128)(2,1)S(1)}, u32[]{:S(2)}, u32[]{:S(2)}) collective-permute-start(bf16[128,4096]{1,0:T(8,128)(2,1)} %hold.1), channel_id=1, source_target_pairs={{0,2},{2,4},{4,6},{6,8},{8,10},{10,12},{12,14},{14,16},{16,18},{18... | collective-permute-start | bytes 3145736 | tf_op jit(solution)/shard_map/ppermute | solution.py:593
  19.0 1.9 %copy-start.1 = (bf16[384,4096]{1,0:T(8,128)(2,1)S(1)}, bf16[384,4096]{1,0:T(8,128)(2,1)}, u32[]{:S(2)}) copy-start(bf16[384,4096]{1,0:T(8,128)(2,1)} %v_hbm.3) | copy-start | bytes 9437188
  20.9 0.9 %copy-start.7 = (bf16[16,4096]{1,0:T(8,128)(2,1)S(1)}, bf16[16,4096]{1,0:T(8,128)(2,1)}, u32[]{:S(2)}) copy-start(bf16[16,4096]{1,0:T(8,128)(2,1)} %copy-done.6) | copy-start | bytes 393220
  21.8 0.9 %copy-start.11 = (f32[256,128]{1,0:T(8,128)S(1)}, f32[256,128]{1,0:T(8,128)}, u32[]{:S(2)}) copy-start(f32[256,128]{1,0:T(8,128)} %taps_ref.3) | copy-start | bytes 393220
  22.7 0.7 copy-start.13
  23.4 11.4 %copy-start.19 = (f32[16,4096]{1,0:T(8,128)S(1)}, f32[16,4096]{1,0:T(8,128)}, u32[]{:S(2)}) copy-start(f32[16,4096]{1,0:T(8,128)} %get-tuple-element.13) | copy-start | bytes 786436
  23.4 18.2 %copy-start.5 = (bf16[4,2,160,256]{3,2,1,0:T(8,128)(2,1)S(1)}, bf16[4,2,160,256]{3,2,1,0:T(8,128)(2,1)}, u32[]{:S(2)}) copy-start(bf16[4,2,160,256]{3,2,1,0:T(8,128)(2,1)} %copy-done.4) | copy-start | bytes 1966084
  36.0 9.0 %collective-permute-start.2 = (bf16[16,4096]{1,0:T(8,128)(2,1)S(1)}, bf16[16,4096]{1,0:T(8,128)(2,1)S(1)}, u32[]{:S(2)}, u32[]{:S(2)}) collective-permute-start(bf16[16,4096]{1,0:T(8,128)(2,1)S(1)} %get-tuple-element.22), channel_id=1, source_target_pairs={{0,8},{2,10},{4,12},{6,14},{8,0},{10,2},{12,4},{14,6},{16,24},{18,... | collective-permute-start | bytes 393224 | tf_op jit(solution)/shard_map/ppermute | solution.py:561
  41.6 16.5 %copy-start.2 = (bf16[384,4096]{1,0:T(8,128)(2,1)S(1)}, bf16[384,4096]{1,0:T(8,128)(2,1)}, u32[]{:S(2)}) copy-start(bf16[384,4096]{1,0:T(8,128)(2,1)} %q_hbm.1) | copy-start | bytes 9437188
  41.6 16.5 %copy-start.8 = (f32[16,4096]{1,0:T(8,128)S(1)}, f32[16,4096]{1,0:T(8,128)}, u32[]{:S(2)}) copy-start(f32[16,4096]{1,0:T(8,128)} %get-tuple-element.14.p1_ref) | copy-start | bytes 786436
  41.6 16.5 %copy-start.9 = (f32[16,4096]{1,0:T(8,128)S(1)}, f32[16,4096]{1,0:T(8,128)}, u32[]{:S(2)}) copy-start(f32[16,4096]{1,0:T(8,128)} %get-tuple-element.15.p2_ref) | copy-start | bytes 786436
  41.6 16.5 %copy-start.12 = (f32[256,128]{1,0:T(8,128)S(1)}, f32[256,128]{1,0:T(8,128)}, u32[]{:S(2)}) copy-start(f32[256,128]{1,0:T(8,128)} %taps_ref.3) | copy-start | bytes 393220
  41.6 16.5 %copy-start.14 = (f32[16,256]{1,0:T(8,128)S(1)}, f32[16,256]{1,0:T(8,128)}, u32[]{:S(2)}) copy-start(f32[16,256]{1,0:T(8,128)} %bitcast_multiply_fusion.coeff_ref) | copy-start | bytes 49156
  41.6 16.5 %copy-start.16 = (f32[32,128]{1,0:T(8,128)S(1)}, f32[32,128]{1,0:T(8,128)}, u32[]{:S(2)}) copy-start(f32[32,128]{1,0:T(8,128)} %get-tuple-element.17.rates_ref) | copy-start | bytes 49156
  43.0 2.4 %collective-permute-start.9 = (bf16[2,160,256]{2,1,0:T(8,128)(2,1)S(1)}, bf16[2,160,256]{2,1,0:T(8,128)(2,1)S(1)}, u32[]{:S(2)}, u32[]{:S(2)}) collective-permute-start(bf16[2,160,256]{2,1,0:T(8,128)(2,1)S(1)} %get-tuple-element.24), channel_id=1, source_target_pairs={{26,2},{30,6},{27,3},{31,7}} | collective-permute-start | bytes 491528 | tf_op jit(solution)/shard_map/ppermute | solution.py:542
  43.7 1.7 %collective-permute-start.8 = (bf16[2,160,256]{2,1,0:T(8,128)(2,1)S(1)}, bf16[2,160,256]{2,1,0:T(8,128)(2,1)S(1)}, u32[]{:S(2)}, u32[]{:S(2)}) collective-permute-start(bf16[2,160,256]{2,1,0:T(8,128)(2,1)S(1)} %get-tuple-element.25), channel_id=1, source_target_pairs={{26,10},{30,14},{27,11},{31,15}} | collective-permute-start | bytes 491528 | tf_op jit(solution)/shard_map/ppermute | solution.py:542
  44.3 1.0 %collective-permute-start.7 = (bf16[2,160,256]{2,1,0:T(8,128)(2,1)S(1)}, bf16[2,160,256]{2,1,0:T(8,128)(2,1)S(1)}, u32[]{:S(2)}, u32[]{:S(2)}) collective-permute-start(bf16[2,160,256]{2,1,0:T(8,128)(2,1)S(1)} %get-tuple-element.26), channel_id=1, source_target_pairs={{26,18},{30,22},{27,19},{31,23}} | collective-permute-start | bytes 491528 | tf_op jit(solution)/shard_map/ppermute | solution.py:542
  45.3 5.4 %collective-permute-start.3 = (bf16[16,4096]{1,0:T(8,128)(2,1)S(1)}, bf16[16,4096]{1,0:T(8,128)(2,1)S(1)}, u32[]{:S(2)}, u32[]{:S(2)}) collective-permute-start(bf16[16,4096]{1,0:T(8,128)(2,1)S(1)} %get-tuple-element.30), channel_id=1, source_target_pairs={{0,16},{2,18},{4,20},{6,22},{8,24},{10,26},{12,28},{14,30},{16,0},... | collective-permute-start | bytes 393224 | tf_op jit(solution)/shard_map/ppermute | solution.py:561
  45.4 12.6 %collective-permute-start.10 = (bf16[1,160,256]{2,1,0:T(8,128)(2,1)S(1)}, bf16[1,160,256]{2,1,0:T(8,128)(2,1)S(1)}, u32[]{:S(2)}, u32[]{:S(2)}) collective-permute-start(bf16[1,160,256]{2,1,0:T(8,128)(2,1)S(1)} %slice.29), channel_id=1, source_target_pairs={{2,0},{6,4},{10,8},{14,12},{18,16},{22,20},{26,24},{30,28},{3,1},{... | collective-permute-start | bytes 245768 | tf_op jit(solution)/shard_map/ppermute | solution.py:547
  58.1 11.2 %copy-start.18 = (s32[256,9]{0,1:T(8,128)S(1)}, s32[256,9]{0,1:T(8,128)}, u32[]{:S(2)}) copy-start(s32[256,9]{0,1:T(8,128)} %param.15) | copy-start | bytes 27652
  65.2 5.4 %copy-start.15 = (f32[4096]{0:T(1024)S(1)}, f32[4096]{0:T(1024)}, u32[]{:S(2)}) copy-start(f32[4096]{0:T(1024)} %param.14) | copy-start | bytes 49156
  65.2 5.4 %collective-permute-start.5 = (f32[8,384]{1,0:T(8,128)S(1)}, f32[8,384]{1,0:T(8,128)S(1)}, u32[]{:S(2)}, u32[]{:S(2)}) collective-permute-start(f32[8,384]{1,0:T(8,128)S(1)} %get-tuple-element.18.refs_0_), channel_id=1, source_target_pairs={{0,1},{1,0},{2,3},{3,2},{4,5},{5,4},{6,7},{7,6},{8,9},{9,8},{10,11... | collective-permute-start | bytes 36872 | tf_op jit(solution)/shard_map/ppermute | solution.py:575

commit v2 on v1

--- a/solution.py
+++ b/solution.py
@@ -48,6 +48,8 @@
 ANY = pl.BlockSpec(memory_space=pl.ANY)
 VMEM = pl.BlockSpec(memory_space=pltpu.VMEM)
 HBM = pl.BlockSpec(memory_space=pltpu.HBM)
+SMEM = pl.BlockSpec(memory_space=pltpu.SMEM)
+TOKEN = jax.ShapeDtypeStruct((8, 128), jnp.float32)
 
 
 def lanes_at(index, width):
@@ -78,11 +80,15 @@
 
 
 def product_kernel(
-    chunks, tiles, k_hbm, v_hbm, rates_ref, tail_ref, p1_ref, p2_ref, own_ref, sent_ref, rows_ref,
-    k_ref, v_ref, in_sems,
+    chunks, tiles, k_hbm, v_hbm, rates_ref, tail_hbm, p1_hbm, p2_hbm, own_hbm, sent_hbm, rows_ref,
+    k_ref, v_ref, tail_ref, p1_ref, p2_ref, own_ref, sent_ref, in_sems, out_sems,
 ):
     width = tiles * LANES
     inputs = [(k_hbm, k_ref, 0, 0), (v_hbm, v_ref, 0, 0)]
+    outputs = [
+        (sent_ref, sent_hbm, 0, 0), (own_ref, own_hbm, 0, 0), (tail_ref, tail_hbm, 0, 0),
+        (p1_ref, p1_hbm, 0, 0), (p2_ref, p2_hbm, 0, 0),
+    ]
     for c in range(chunks):
         for copy in copies(inputs, in_sems, c, width):
             copy.start()
@@ -114,25 +120,31 @@
             sent_ref[:, lanes] = packed[:, :LANES].astype(bf16)
             p2_ref[:, lanes] = packed[:, LANES : 2 * LANES]
             p1_ref[:, lanes] = packed[:, 2 * LANES :]
+        for copy in copies(outputs, out_sems, c, width):
+            copy.start()
+
+    drain(chunks, width, outputs, out_sems)
 
 
 def product_and_states(key_rows, value_rows, rates_t):
     tokens, channels = key_rows.shape
-    chunks = 4
+    chunks = min(8, channels // LANES // 2)
     tiles = channels // LANES // chunks
     state_shape = jax.ShapeDtypeStruct((MODES, channels), f32)
     return pl.pallas_call(
         functools.partial(product_kernel, chunks, tiles),
         in_specs=[HBM, HBM, VMEM],
-        out_specs=[VMEM] * 6,
+        out_specs=[ANY] * 5 + [VMEM],
         out_shape=[
             jax.ShapeDtypeStruct((CH, channels), bf16),
             state_shape, state_shape, state_shape, jax.ShapeDtypeStruct((MODES, channels), bf16),
             jax.ShapeDtypeStruct((channels // LANES, LANES), f32),
         ],
         scratch_shapes=[
-            pltpu.VMEM((tokens, channels), bf16), pltpu.VMEM((tokens, channels), bf16),
-            pltpu.SemaphoreType.DMA((2, chunks)),
+            pltpu.VMEM((tokens, channels), bf16), pltpu.VMEM((tokens, channels), bf16), pltpu.VMEM((CH, channels), bf16),
+            pltpu.VMEM((MODES, channels), f32), pltpu.VMEM((MODES, channels), f32), pltpu.VMEM((MODES, channels), f32),
+            pltpu.VMEM((MODES, channels), bf16),
+            pltpu.SemaphoreType.DMA((2, chunks)), pltpu.SemaphoreType.DMA((5, chunks)),
         ],
         compiler_params=params(56),
         cost_estimate=pl.CostEstimate(
@@ -142,26 +154,6 @@
     )(key_rows, value_rows, rates_t)
 
 
-def spread_kernel(rates_ref, out_ref):
-    rates = rates_ref[...].T
-    high = rates.astype(bf16).astype(f32)
-    middle = (rates - high).astype(bf16).astype(f32)
-    parts = jnp.concatenate([high, middle, rates - high - middle], axis=1)
-    expand = (iota((PER_TILE, LANES), 1) // GW == iota((PER_TILE, LANES), 0)).astype(f32).astype(bf16)
-    for t in range(out_ref.shape[1] // LANES):
-        wide = tn_dot(parts[t * PER_TILE : (t + 1) * PER_TILE].astype(bf16), expand)
-        out_ref[:, t * LANES : (t + 1) * LANES] = wide[:MODES] + wide[MODES : 2 * MODES] + wide[2 * MODES :]
-
-
-def spread_rates(rates_t):
-    return pl.pallas_call(
-        spread_kernel,
-        out_shape=jax.ShapeDtypeStruct((MODES, rates_t.shape[1] * GW), f32),
-        compiler_params=params(),
-        name="spread_rates",
-    )(rates_t)
-
-
 FOLD = 4
 PARTS = PER_TILE // FOLD
 
@@ -189,22 +181,16 @@
 
 
 def local_kernel(
-    chunks, tiles, k_hbm, v_hbm, taps_ref, rates_ref, coeff_ref, after,
-    out_ref, k_ref, v_ref, taps_rev, response, lhs_all, rhs_all, in_sems,
+    chunks, tiles, k_hbm, v_hbm, taps_rev, response, after,
+    out_ref, token_ref, k_ref, v_ref, lhs_all, rhs_all, in_sems,
 ):
+    token_ref[...] = jnp.zeros_like(token_ref)
     half = PARTS * CH
     width = tiles * LANES
     inputs = [(k_hbm, k_ref, 0, 0), (v_hbm, v_ref, 0, 0)]
     for c in range(chunks):
         for copy in copies(inputs, in_sems, c, width):
             copy.start()
-    lag = ((CH - iota((1, LANES), 1)) % CH).astype(f32)
-    rates, coeff = rates_ref[...].T, coeff_ref[...].T
-    sums = reversed_lags(taps_ref[...])
-    taps_rev[...] = sums
-    for m in range(MODES):
-        sums = sums + coeff[:, m : m + 1] * jnp.exp(-rates[:, m : m + 1] * lag)
-    response[...] = sums
     lower = iota((CH, LANES), 1) <= iota((CH, LANES), 0)
     masks = fold_masks()
 
@@ -234,19 +220,17 @@
             out_ref[2 * CH :, lanes] = unfold(later[:, LANES:]).astype(bf16)
 
 
-def local_part(key_rows, value_rows, taps, rates_t, coeff_t, after):
+def local_part(key_rows, value_rows, taps_rev, response, after):
     tokens, channels = key_rows.shape
-    groups = taps.shape[0]
+    groups = taps_rev.shape[0]
     chunks = 4
     tiles = channels // LANES // chunks
     return pl.pallas_call(
         functools.partial(local_kernel, chunks, tiles),
-        in_specs=[HBM, HBM, VMEM, VMEM, VMEM, ANY],
-        out_specs=VMEM,
-        out_shape=jax.ShapeDtypeStruct((tokens, channels), bf16),
-        scratch_shapes=[
-            pltpu.VMEM((tokens, channels), bf16), pltpu.VMEM((tokens, channels), bf16),
-            pltpu.VMEM((groups, CH), f32), pltpu.VMEM((groups, CH), f32),
+        in_specs=[ANY, ANY, VMEM, VMEM, ANY],
+        out_specs=[VMEM, VMEM],
+        out_shape=[jax.ShapeDtypeStruct((tokens, channels), bf16), TOKEN],
+        scratch_shapes=[pltpu.VMEM((tokens, channels), bf16)] * 2 + [
             pltpu.VMEM((2, FOLD * CH, 2 * PARTS * CH), bf16), pltpu.VMEM((2, 2 * PARTS * CH, 2 * LANES), bf16),
             pltpu.SemaphoreType.DMA((2, chunks)),
         ],
@@ -255,49 +239,27 @@
             flops=groups * CH * 256 * 512 * 2, bytes_accessed=groups * GW * tokens * 4, transcendentals=0
         ),
         name="local_conv",
-    )(key_rows, value_rows, taps, rates_t, coeff_t, after)
-
-
-def cross_of(decays, states):
-    mask = same_filter(LANES, len(states) * LANES)
-    wide = jnp.concatenate(states, axis=1)
-    high = wide.astype(bf16)
-    low = wide - high.astype(f32)
-    blocks = lambda a: jnp.where(mask, jnp.concatenate([a] * PER_TILE, axis=0), 0.0).astype(bf16)
-    stacked = jnp.concatenate([blocks(high.astype(f32)), blocks(low)], axis=0)
-    return jnp.dot(jnp.concatenate([decays, decays], axis=1), stacked, preferred_element_type=f32)
-
-
-def starts_of(lam, weight):
-    index = iota((CH, LANES), 0).astype(f32)
-    return (weight * jnp.exp(-index * lam)).astype(bf16)
-
-
-def energy_row(partial):
-    return lax.dot_general(
-        jnp.ones((8, LANES), f32), partial, (((1,), (1,)), ((), ())), preferred_element_type=f32, precision=highest
-    )
-
-
-def gate_kernel(
-    chunks, tiles, local_ref, q_hbm, in_ref, p1_ref, p2_ref, spread_ref, tail_ref, taps_ref, rates_ref, coeff_ref,
-    gated_ref, energy_ref, q_ref, weight_ref, taps_rev, lhs_all, total_ref, in_sems,
+    )(key_rows, value_rows, taps_rev, response, after)
+
+
+def carry_kernel(
+    chunks, tiles, local_ref, tail_ref, taps_rev, q_hbm, p1_hbm, p2_hbm, weight_hbm, after,
+    out_ref, token_ref, q_ref, p1_ref, p2_ref, weight_ref, lhs_all, sems,
 ):
-    width = tiles * LANES
-    inputs = [(q_hbm, q_ref, 0, 0)]
-    for c in range(chunks):
-        for copy in copies(inputs, in_sems, c, width):
-            copy.start()
-    weight_ref[...] = by_tile(coeff_ref[...].T)
-    taps_rev[...] = reversed_lags(taps_ref[...])
-    total_ref[...] = jnp.zeros_like(total_ref)
+    bring = [
+        pltpu.make_async_copy(source, target, sems.at[i])
+        for i, (source, target) in enumerate(
+            [(q_hbm, q_ref), (p1_hbm, p1_ref), (p2_hbm, p2_ref), (weight_hbm, weight_ref)]
+        )
+    ]
+    for copy in bring:
+        copy.start()
+    token_ref[...] = jnp.zeros_like(token_ref)
     lower = iota((CH, LANES), 1) <= iota((CH, LANES), 0)
     masks = fold_masks()
 
     @pl.loop(0, chunks)
     def _(c):
-        for copy in copies(inputs, in_sems, c, width):
-            copy.wait()
         for t in range(tiles):
             lanes = lanes_at(c * tiles + t, LANES)
             lhs_ref = lhs_all.at[t % 2]
@@ -308,8 +270,104 @@
             tail = tail_ref[:, lanes]
             masked = jnp.concatenate([tail * mask for mask in masks], axis=0)
             carried = unfold(jnp.dot(lhs_ref[...], masked, preferred_element_type=f32))
-            decay = jnp.exp(-float(CH) * spread_ref[:, lanes])
-            z0 = in_ref[:, lanes]
+            out_ref[:, lanes] = (local_ref[:CH, lanes].astype(f32) + carried).astype(bf16)
+
+    for copy in bring:
+        copy.wait()
+
+
+def carry_part(local, tail, taps_rev, query_rows, p1, p2, weight_rows, after):
+    tokens, channels = local.shape
+    chunks = 4
+    tiles = channels // LANES // chunks
+    return pl.pallas_call(
+        functools.partial(carry_kernel, chunks, tiles),
+        in_specs=[VMEM, VMEM, VMEM] + [ANY] * 5,
+        out_specs=[VMEM] * 6,
+        out_shape=[jax.ShapeDtypeStruct((CH, channels), bf16), TOKEN]
+        + [jax.ShapeDtypeStruct(a.shape, a.dtype) for a in (query_rows, p1, p2, weight_rows)],
+        scratch_shapes=[pltpu.VMEM((2, FOLD * CH, PARTS * CH), bf16), pltpu.SemaphoreType.DMA((4,))],
+        compiler_params=params(),
+        cost_estimate=pl.CostEstimate(flops=channels * CH * 1024, bytes_accessed=channels * CH * 6, transcendentals=0),
+        name="carry",
+    )(local, tail, taps_rev, query_rows, p1, p2, weight_rows, after)
+
+
+def exact_parts(values):
+    high = values.astype(bf16).astype(f32)
+    middle = (values - high).astype(bf16).astype(f32)
+    return jnp.concatenate([high, middle, values - high - middle], axis=1)
+
+
+def prepare_kernel(
+    rates_ref, factor_ref, residues_ref, taps_ref, spread_ref, norm_ref, taps_rev_ref, response_ref, weight_ref
+):
+    rates, factor = rates_ref[...].T, factor_ref[...].T
+    coeff = residues_ref[...].T * factor
+    expand = (iota((PER_TILE, LANES), 1) // GW == iota((PER_TILE, LANES), 0)).astype(f32).astype(bf16)
+    for source, target in ((exact_parts(rates), spread_ref), (exact_parts(factor), norm_ref)):
+        for t in range(target.shape[1] // LANES):
+            wide = tn_dot(source[t * PER_TILE : (t + 1) * PER_TILE].astype(bf16), expand)
+            target[:, t * LANES : (t + 1) * LANES] = wide[:MODES] + wide[MODES : 2 * MODES] + wide[2 * MODES :]
+    weight_ref[...] = by_tile(coeff)
+    lag = ((CH - iota((1, LANES), 1)) % CH).astype(f32)
+    sums = reversed_lags(taps_ref[...])
+    taps_rev_ref[...] = sums
+    for m in range(MODES):
+        sums = sums + coeff[:, m : m + 1] * jnp.exp(-rates[:, m : m + 1] * lag)
+    response_ref[...] = sums
+
+
+def prepare(rates_t, factor_t, residues_t, taps):
+    groups = taps.shape[0]
+    shapes = [(MODES, groups * GW), (MODES, groups * GW), taps.shape, taps.shape, (groups // PER_TILE, LANES)]
+    return pl.pallas_call(
+        prepare_kernel,
+        in_specs=[VMEM] * 4,
+        out_specs=[VMEM] * 5,
+        out_shape=[jax.ShapeDtypeStruct(shape, f32) for shape in shapes],
+        compiler_params=params(),
+        name="prepare",
+    )(rates_t, factor_t, residues_t, taps)
+
+
+def cross_of(decays, states):
+    mask = same_filter(LANES, len(states) * LANES)
+    wide = jnp.concatenate(states, axis=1)
+    high = wide.astype(bf16)
+    low = wide - high.astype(f32)
+    blocks = lambda a: jnp.where(mask, jnp.concatenate([a] * PER_TILE, axis=0), 0.0).astype(bf16)
+    stacked = jnp.concatenate([blocks(high.astype(f32)), blocks(low)], axis=0)
+    return jnp.dot(jnp.concatenate([decays, decays], axis=1), stacked, preferred_element_type=f32)
+
+
+def starts_of(lam, weight):
+    index = iota((CH, LANES), 0).astype(f32)
+    return (weight * jnp.exp(-index * lam)).astype(bf16)
+
+
+def energy_row(partial):
+    return lax.dot_general(
+        jnp.ones((8, LANES), f32), partial, (((1,), (1,)), ((), ())), preferred_element_type=f32, precision=highest
+    )
+
+
+def gate_kernel(
+    chunks, tiles, step, me_ref, first_ref, local_ref, q_ref, in_ref, other_ref, p1_ref, p2_ref, spread_ref, rates_ref, weight_ref,
+    gated_ref, energy_ref, total_ref,
+):
+    me = me_ref[0]
+    offset = ((me & (step - 1)) * gated_ref.shape[0]).astype(f32)
+    right = jnp.where((me & step) != 0, 1.0, 0.0)
+    total_ref[...] = jnp.zeros_like(total_ref)
+
+    @pl.loop(0, chunks)
+    def _(c):
+        for t in range(tiles):
+            lanes = lanes_at(c * tiles + t, LANES)
+            spread = spread_ref[:, lanes]
+            decay = jnp.exp(-float(CH) * spread)
+            z0 = in_ref[:, lanes] + right * (jnp.exp(-spread * offset) * other_ref[:, lanes].astype(f32))
             entry = decay * z0
             z1 = entry + p1_ref[:, lanes]
             z2 = decay * entry + p2_ref[:, lanes]
@@ -317,41 +375,38 @@
             cross = cross_of(starts_of(rates_ref[row, :], weight_ref[row, :]), [z0, z1, z2])
             for i in range(3):
                 rows = slice(i * CH, (i + 1) * CH)
-                conv = local_ref[rows, lanes].astype(f32) + cross[:, i * LANES : (i + 1) * LANES]
-                if i == 0:
-                    conv = conv + carried
-                gated = conv * q_ref[rows, lanes].astype(f32)
+                own = first_ref[:, lanes] if i == 0 else local_ref[rows, lanes]
+                gated = (own.astype(f32) + cross[:, i * LANES : (i + 1) * LANES]) * q_ref[rows, lanes].astype(f32)
                 gated_ref[rows, lanes] = gated.astype(bf16)
                 total_ref[rows] += gated * gated
 
     energy_ref[...] = energy_row(total_ref[...])
 
 
-def gate_part(local, query_rows, incoming, p1, p2, rates_spread, tail, taps, rate_rows, coeff_t):
-    tokens, channels = local.shape
+def gate_part(me, step, first, local, query_rows, incoming, other, p1, p2, rates_spread, rate_rows, weight_rows):
+    tokens, channels = query_rows.shape
     chunks = 4
     tiles = channels // LANES // chunks
     return pl.pallas_call(
-        functools.partial(gate_kernel, chunks, tiles),
-        in_specs=[VMEM, HBM] + [VMEM] * 8,
+        functools.partial(gate_kernel, chunks, tiles, step),
+        in_specs=[SMEM] + [VMEM] * 10,
         out_specs=[VMEM, VMEM],
-        out_shape=[jax.ShapeDtypeStruct((tokens, channels), bf16), jax.ShapeDtypeStruct((8, tokens), f32)],
-        scratch_shapes=[
-            pltpu.VMEM((tokens, channels), bf16), pltpu.VMEM(rate_rows.shape, f32), pltpu.VMEM(taps.shape, f32),
-            pltpu.VMEM((2, FOLD * CH, PARTS * CH), bf16), pltpu.VMEM((tokens, LANES), f32),
-            pltpu.SemaphoreType.DMA((1, chunks)),
+        out_shape=[
+            jax.ShapeDtypeStruct((tokens, channels), bf16), jax.ShapeDtypeStruct((8, tokens), f32),
         ],
+        scratch_shapes=[pltpu.VMEM((tokens, LANES), f32)],
         compiler_params=params(),
         cost_estimate=pl.CostEstimate(
             flops=channels * CH * 2048, bytes_accessed=channels * tokens * 6, transcendentals=channels * CH
         ),
         name="gate",
-    )(local, query_rows, incoming, p1, p2, rates_spread, tail, taps, rate_rows, coeff_t)
+    )(me, first, local, query_rows, incoming, other, p1, p2, rates_spread, rate_rows, weight_rows)
 
 
 def norm_kernel(terms, chunks, tiles, *refs):
     energies, (gated_ref, gain_ref) = refs[:terms], refs[terms : terms + 2]
-    out_hbm, out_ref, scale_ref, out_sems = refs[-4:]
+    out_hbm, token_ref, out_ref, scale_ref, out_sems = refs[-5:]
+    token_ref[...] = jnp.zeros_like(token_ref)
     width = tiles * LANES
     rows = gated_ref.shape[0]
     outputs = [(out_ref, out_hbm, 0, 0)]
@@ -379,8 +434,8 @@
     return pl.pallas_call(
         functools.partial(norm_kernel, len(energies), chunks, tiles),
         in_specs=[VMEM] * (len(energies) + 2),
-        out_specs=HBM,
-        out_shape=jax.ShapeDtypeStruct((rows, channels), bf16),
+        out_specs=[HBM, VMEM],
+        out_shape=[jax.ShapeDtypeStruct((rows, channels), bf16), TOKEN],
         scratch_shapes=[
             pltpu.VMEM((rows, channels), bf16), pltpu.VMEM((rows, LANES), f32), pltpu.SemaphoreType.DMA((1, chunks)),
         ],
@@ -408,8 +463,8 @@
     return jnp.dot(present.astype(bf16), before, preferred_element_type=f32)
 
 
-def select_kernel(blocks, slots, inner, outer, me_ref, tail_ref, plan_ref, *refs):
-    outs, (items_ref, picks_ref) = refs[:2], refs[2:]
+def select_kernel(blocks, slots, inner, outer, me_ref, tail_hbm, plan_ref, *refs):
+    outs, (items_ref, picks_ref, tail_ref, sem) = refs[:2], refs[2:]
     groups = plan_ref.shape[1]
 
     @pl.when(me_ref[0] != inner * outer - 1)
@@ -419,6 +474,9 @@
 
     @pl.when(me_ref[0] == inner * outer - 1)
     def _():
+        copy = pltpu.make_async_copy(tail_hbm, tail_ref, sem)
+        copy.start()
+        copy.wait()
         for g in range(0, groups // PER_TILE, 2):
             halves = []
             for side in range(2):
@@ -459,27 +517,32 @@
     vmem = pl.BlockSpec(memory_space=pltpu.VMEM)
     return pl.pallas_call(
         functools.partial(select_kernel, blocks, slots, inner, outer),
-        in_specs=[pl.BlockSpec(memory_space=pltpu.SMEM), vmem, vmem],
-        out_specs=[vmem] * 2,
+        in_specs=[SMEM, ANY, vmem],
+        out_specs=[vmem, vmem],
         out_shape=[jax.ShapeDtypeStruct((outer, inner // 2, slots, MODES * GW), bf16)] * 2,
         scratch_shapes=[
             pltpu.VMEM((blocks * groups, MODES * GW), bf16), pltpu.VMEM((inner * slots, blocks * groups), bf16),
+            pltpu.VMEM(tail.shape, bf16), pltpu.SemaphoreType.DMA,
         ],
-        compiler_params=params(),
+        compiler_params=params(56),
         cost_estimate=pl.CostEstimate(flops=10**9, bytes_accessed=2 * 10**6, transcendentals=0),
         name="select_tails",
     )(me, tail, plan_cols)
 
 
-def handoff_kernel(me_ref, final_ref, norm_ref, plan_ref, got_ref, out_ref, items_ref):
+def handoff_kernel(step, tokens, me_ref, total_ref, other_ref, spread_ref, norm_ref, plan_ref, kept_ref, sent_ref, after, out_ref, items_ref):
     groups = plan_ref.shape[1]
     capacity = out_ref.shape[2]
-    slots = got_ref.shape[0]
+    slots = sent_ref.shape[0]
+    kept = me_ref[0] % 2 == 1
     plan = plan_ref[...]
     mine = plan == me_ref[0]
     present = jnp.sum(mine.astype(f32), axis=0, keepdims=True)
     rank = ranks_of(jnp.broadcast_to(present, (8, groups)))[:1]
-    final = final_ref[...] * norm_ref[...]
+    total, other = total_ref[...], other_ref[...].astype(f32)
+    right = (me_ref[0] & step) != 0
+    earlier, later = jnp.where(right, other, total), jnp.where(right, total, other)
+    final = (jnp.exp(-spread_ref[...] * float(step * tokens)) * earlier + later) * norm_ref[...]
     stack = [
         final[half * 8 : (half + 1) * 8, g * LANES : (g + 1) * LANES]
         for half in range(2) for g in range(groups // PER_TILE)
@@ -492,23 +555,23 @@
     at = (jnp.broadcast_to(rank, (slots, groups)) == slot) & mine[last:]
     pick = jnp.where(at, 1.0, 0.0).astype(bf16)
     rows = jnp.dot(pick, items_ref[...], preferred_element_type=f32)
-    rows = (rows + got_ref[...].astype(f32)).T
+    rows = (rows + jnp.where(kept, kept_ref[...].astype(f32), sent_ref[...].astype(f32))).T
     out_ref[...] = rows[:, :capacity].reshape(out_ref.shape)
 
 
-def assemble(me, final, norm_spread, plan_cols, got, capacity):
+def assemble(me, step, tokens, total, other, rates_spread, norm_spread, plan_cols, kept, sent, capacity, after):
     groups = plan_cols.shape[1]
     vmem = pl.BlockSpec(memory_space=pltpu.VMEM)
     out = pl.pallas_call(
-        handoff_kernel,
-        in_specs=[pl.BlockSpec(memory_space=pltpu.SMEM), vmem, vmem, vmem, vmem],
+        functools.partial(handoff_kernel, step, tokens),
+        in_specs=[SMEM] + [vmem] * 7 + [ANY],
         out_specs=vmem,
         out_shape=jax.ShapeDtypeStruct((MODES, GW, capacity), f32),
         scratch_shapes=[pltpu.VMEM((groups, MODES * GW), bf16)],
         compiler_params=params(),
         cost_estimate=pl.CostEstimate(flops=10**9, bytes_accessed=10**6, transcendentals=0),
         name="handoff",
-    )(me, final, norm_spread, plan_cols, got)
+    )(me, total, other, rates_spread, norm_spread, plan_cols, kept, sent, after)
     return out.transpose(2, 0, 1)
 
 
@@ -516,58 +579,71 @@
     pass
 
 
-def hold(array, after):
-    anywhere = pl.BlockSpec(memory_space=pl.ANY)
+def hold(array, *after):
     return pl.pallas_call(
         hold_kernel,
-        in_specs=[anywhere, anywhere],
-        out_specs=anywhere,
+        in_specs=[ANY] * (1 + len(after)),
+        out_specs=ANY,
         out_shape=jax.ShapeDtypeStruct(array.shape, array.dtype),
         input_output_aliases={0: 0},
         name="hold",
-    )(array, after)
-
-
-def scatter_tails(selected, inner, outer):
+    )(array, *after)
+
+
+def scatter_high(low, high, inner, outer, token):
     count = inner * outer
-    me = lax.axis_index("seq")
-    half = inner // 2
-    low, high = selected
-    sent = lax.ppermute(low, "seq", [(count - 1, count - 1 - half)])
-    block = jnp.where((me & half) != 0, high, sent)
-    heads = [half - 1, inner - 1]
-    own = block[outer - 1]
-    for o in range(outer - 1):
-        pairs = [(count - inner + h, o * inner + h) for h in heads]
-        sent = lax.ppermute(block[o], "seq", pairs)
-        own = jnp.where(me // inner == o, sent, own)
-    half //= 2
-    while half:
-        pairs = [(i, i - half) for i in range(count) if (i + 1) % (2 * half) == 0]
+    sent = lax.ppermute(low, "seq", [(count - 1, count - 1 - inner // 2)])
+    return jnp.where((lax.axis_index("seq") & (inner // 2)) != 0, high, sent + token[0, 0].astype(bf16))
+
+
+def scatter_outer(block, inner, outer):
+    base = inner * (outer - 1)
+    heads = (inner // 2 - 1, inner - 1)
+    return [
+        lax.ppermute(block[o], "seq", [(base + h, o * inner + h) for h in heads]) for o in range(outer - 1)
+    ]
+
+
+def scatter_low(own, inner, outer):
+    half = inner // 4
+    while True:
+        pairs = [(i, i - half) for i in range(inner * outer) if (i + 1) % (2 * half) == 0]
         sent = lax.ppermute(own[:half], "seq", pairs)
-        own = jnp.where((me & half) != 0, own[half:], sent)
+        if half == 1:
+            return own[1], sent[0]
+        own = jnp.where((lax.axis_index("seq") & half) != 0, own[half:], sent)
         half //= 2
-    return own[0]
-
-
-def scan_states(own, sent, rates_spread, tokens):
+
+
+def exchange(sent, count, inner, step):
+    pairs = [(i, i ^ step) for i in range(count)]
+    if step != inner:
+        return [lax.ppermute(sent, "seq", pairs)]
+    last = lambda i: i % inner == inner - 1
+    main = [(i, j) for i, j in pairs if not (last(i) and j > i)]
+    extra = [(i - inner // 2, j) for i, j in pairs if last(i) and j > i]
+    return [lax.ppermute(sent, "seq", main), lax.ppermute(sent, "seq", extra)]
+
+
+def scan_states(own, sent, rates_spread, tokens, inner, beside):
     count = lax.axis_size("seq")
     me = lax.axis_index("seq")
     total, incoming = own, jnp.zeros_like(own)
-    stages = []
     step = 1
-    while step < count:
-        pairs = [(i, i ^ step) for i in range(count)]
-        other = lax.ppermute(sent, "seq", pairs).astype(f32)
+    while True:
+        got = exchange(sent, count, inner, step)
+        if beside:
+            beside.pop(0)(sent)
+        if 2 * step >= count:
+            return total, incoming, functools.reduce(jnp.add, got), step
+        other = sum(part.astype(f32) for part in got)
         right = (me & step) != 0
         offset = ((me & (step - 1)) * tokens).astype(f32)
-        incoming = jnp.where(right, incoming + jnp.exp(-rates_spread * offset) * other, incoming)
         decay = jnp.exp(-rates_spread * float(step * tokens))
         total = jnp.where(right, decay * other + total, decay * total + other)
+        incoming = jnp.where(right, incoming + jnp.exp(-rates_spread * offset) * other, incoming)
         sent = total.astype(bf16)
-        stages.append(sent)
         step *= 2
-    return total, incoming, stages
 
 
 def sum_over_chan(energy):
@@ -586,29 +662,52 @@
     me = lax.axis_index("seq")
 
     rates_t = decay_rates.T
+    factor_t = jnp.sqrt(-jnp.expm1(-2.0 * rates_t))
     own_tail, p1, p2, own, sent, rate_rows = product_and_states(key_rows, value_rows, rates_t)
-    rates_spread = spread_rates(rates_t)
-    total, incoming, stages = scan_states(own, sent, rates_spread, tokens)
-    onward = [(i, i + 1) for i in range(seq_count - 1)]
-    tail_prev = lax.ppermute(hold(own_tail, stages[0]), "seq", onward)
-
-    coeff_t = residues.T * jnp.sqrt(-jnp.expm1(-2.0 * rates_t))
-    norm_spread = jnp.sqrt(-jnp.expm1(-2.0 * rates_spread))
-    plan_cols = reader_plan.T
-
+    rates_spread, norm_spread, taps_rev, response, weight_rows = prepare(rates_t, factor_t, residues.T, medium_taps)
     inner = 1 << (int(math.log2(seq_count)) // 2)
     outer = seq_count // inner
+
+    plan_cols = reader_plan.T
+
     capacity = (groups * (blocks + 1) + seq_count - 1) // seq_count + 1
     slots = -(-capacity // 16) * 16
-    selected = select_tails(me.reshape(1), own_tail, plan_cols, inner, outer, slots)
-    got = scatter_tails(selected, inner, outer)
-
-    local = local_part(key_rows, value_rows, medium_taps, rates_t, coeff_t, stages[0])
+    done = {}
+    onward = [(i, i + 1) for i in range(seq_count - 1)]
+
+    def while_first(sent):
+        return None
+
+    def while_second(sent):
+        held = hold(own_tail, sent)
+        done["tail"] = lax.ppermute(held, "seq", onward)
+        done["low"], done["high"] = select_tails(me.reshape(1), held, plan_cols, inner, outer, slots)
+
+    def while_third(sent):
+        done["local"], token = local_part(key_rows, value_rows, taps_rev, response, sent)
+        done["block"] = scatter_high(done["low"], done["high"], inner, outer, token)
+
+    def while_fourth(sent):
+        done["first"], token, *done["brought"] = carry_part(
+            done["local"], done["tail"], taps_rev, query_rows, p1, p2, weight_rows, sent
+        )
+        done["token"] = token[:1, :1]
+
+    beside = [while_first, while_second, while_third, while_fourth]
+    total, incoming, other, last_step = scan_states(own, sent, rates_spread, tokens, inner, beside)
+    own_block = done["block"][outer - 1]
+    for o, sent_block in enumerate(scatter_outer(done["block"], inner, outer)):
+        sent_block = sent_block + done["token"][0, 0].astype(bf16)
+        own_block = jnp.where(me // inner == o, sent_block, own_block)
+    kept, sent_last = scatter_low(own_block, inner, outer)
+    queries, p1_near, p2_near, weights_near = done["brought"]
     gated, energy = gate_part(
-        local, query_rows, incoming, p1, p2, rates_spread, tail_prev, medium_taps, rate_rows, coeff_t
+        me.reshape(1), last_step, done["first"], done["local"], queries, incoming, other, p1_near, p2_near,
+        rates_spread, rate_rows, weights_near,
     )
-    mixed = norm_part(sum_over_chan(energy), gated, out_gain[None, :])
-    handoff = assemble(me.reshape(1), total, norm_spread, plan_cols, got, capacity)
+    mixed, token = norm_part(sum_over_chan(energy), gated, out_gain[None, :])
+    handoff = assemble(
+        me.reshape(1), last_step, tokens, total, other, rates_spread, norm_spread, plan_cols, kept, sent_last, capacity, token)
     return mixed, handoff
 
 

time: 74.2 us -> 71.5 us (0.964)
  the two profiles are of different devices: /device:TPU:17 before, /device:TPU:11 now
where the time goes in v2:
time: 71.5 us; the launch traced here: 71.1 us
  Pallas kernels  33.3 us (47%)
  starting transfers between devices  24.7 us (35%)
  other arithmetic  5.96 us (8%)
  waiting for transfers between devices  4.33 us (6%)
  local copies, waits for them, and re-layouts  1.86 us (3%)
  between operations  1.03 us (1%)
    ppermute x3, starting transfers between devices, exchange(): return [lax.ppermute(sent, 'seq', pairs)]  11.8 us
    pallas_call x1, Pallas kernels, local_part(): pl.pallas_call(functools.partial(local_kernel, chunks, tiles), in_specs=[...  9.91 us
    pallas_call x1, Pallas kernels, product_and_states(): pl.pallas_call(functools.partial(product_kernel, chunks, tiles), in_specs...  7.57 us
    convert_element_type x3, other arithmetic, scan_states(): sent = total.astype(bf16)  4.27 us
    pallas_call x1, Pallas kernels, carry_part(): pl.pallas_call(functools.partial(carry_kernel, chunks, tiles), in_specs=[...  4.03 us
    pallas_call x1, Pallas kernels, gate_part(): pl.pallas_call(functools.partial(gate_kernel, chunks, tiles, step), in_sp...  3.86 us
    ppermute x3, waiting for transfers between devices, exchange(): return [lax.ppermute(sent, 'seq', pairs)]  2.99 us
    pallas_call x1, Pallas kernels, norm_part(): pl.pallas_call(functools.partial(norm_kernel, len(energies), chunks, tile...  2.98 us
  transfers between devices with their start and end apart: 12, of which 4 were waited for; matrix products, arithmetic and copies ran while one was open for 7% of the time, Pallas kernels for 34%

profile of v2, /device:TPU:11, one launch (start us, length us, event | category | flops | bytes accessed | tf_op | source)
XLA Modules:
  0.0 71.1 jit_solution(11456885844474366923)
XLA Ops:
  0.6 0.0 copy-start.5
  0.6 0.0 copy-start.6
  0.7 0.0 copy-start.9
  0.7 7.6 %product_states.1 = (bf16[128,4096]{1,0:T(8,128)(2,1)}, f32[16,4096]{1,0:T(8,128)}, f32[16,4096]{1,0:T(8,128)}, f32[16,4096]{1,0:T(8,128)}, bf16[16,4096]{1,0:T(8,128)(2,1)}, /*index=5*/f32[32,128]{1,0:T(8,128)}) custom-call(bf16[384,4096]{1,0:T(8,128)(2,1)} %k_hbm.3, bf16[384,4096]{1,0:T(8,128)(2,1)} %v_hbm.3, f32[16,256]{1,0:T(8,128)} %bitcast.26), custom_call_target="tpu_custom_call" | custom-call | flops 1207959552 | bytes 9437184 | tf_op jit(solution)/shard_map/product_states/pallas_call | solution.py:134
  8.2 0.3 collective-permute-start
  8.6 0.0 copy-done.5
  8.6 0.0 copy-done.6
  8.6 0.0 copy-done.9
  8.6 1.6 %prepare.1 = (f32[16,4096]{1,0:T(8,128)S(1)}, f32[16,4096]{1,0:T(8,128)S(1)}, f32[256,128]{1,0:T(8,128)S(1)}, f32[256,128]{1,0:T(8,128)S(1)}, f32[32,128]{1,0:T(8,128)S(1)}) custom-call(f32[16,256]{1,0:T(8,128)S(1)} %bitcast.27, f32[16,256]{1,0:T(8,128)S(1)} %negate_sqrt_fusion.factor_ref, f32[16,256]{1,0:T(8,128)S(1)} %bitcast.29, f32[256,128]{1,0:T(8,128)S(1)} %copy-done.6), custom_call_target="tpu_custom_call" | custom-call | tf_op jit(solution)/shard_map/prepare/pallas_call | solution.py:324
  10.3 0.0 copy-start.10
  10.3 0.7 copy-done.10
  11.0 1.9 %collective-permute-done = bf16[16,4096]{1,0:T(8,128)(2,1)S(1)} collective-permute-done((bf16[16,4096]{1,0:T(8,128)(2,1)}, bf16[16,4096]{1,0:T(8,128)(2,1)S(1)}, u32[]{:S(2)}, u32[]{:S(2)}) %collective-permute-start) | collective-permute-done | bytes 131104 | tf_op jit(solution)/shard_map/ppermute | solution.py:621
  12.9 1.7 %fusion.9.refs_1_ = bf16[16,4096]{1,0:T(8,128)(2,1)} fusion(f32[16,4096]{1,0:T(8,128)} %get-tuple-element.31, bf16[16,4096]{1,0:T(8,128)(2,1)S(1)} %collective-permute-done, f32[16,4096]{1,0:T(8,128)S(1)} %get-tuple-element.29.spread_ref, pred[]{:T(512)S(6)} %ne.23), kind=kLoop, calls=%fused_computation.26 | loop fusion | flops 589824 | bytes 786433 | tf_op jit(solution)/shard_map/convert_element_type | solution.py:645
  14.6 1.2 %collective-permute-start.1 = (bf16[16,4096]{1,0:T(8,128)(2,1)}, bf16[16,4096]{1,0:T(8,128)(2,1)}, u32[]{:S(2)}, u32[]{:S(2)}) collective-permute-start(bf16[16,4096]{1,0:T(8,128)(2,1)} %fusion.9.refs_1_), channel_id=1, source_target_pairs={{0,4},{2,6},{4,0},{6,2},{8,12},{10,14},{12,8},{14,10},{16,20},{18,... | collective-permute-start | bytes 393224 | tf_op jit(solution)/shard_map/ppermute | solution.py:621
  15.8 0.0 copy-done.12
  15.8 0.0 copy-done.16
  15.9 0.0 copy-start.1
  15.9 0.0 copy-start.13
  15.9 2.5 %collective-permute-start.2 = (bf16[128,4096]{1,0:T(8,128)(2,1)}, bf16[128,4096]{1,0:T(8,128)(2,1)S(1)}, u32[]{:S(2)}, u32[]{:S(2)}) collective-permute-start(bf16[128,4096]{1,0:T(8,128)(2,1)} %hold.1.tail_hbm), channel_id=1, source_target_pairs={{0,2},{2,4},{4,6},{6,8},{8,10},{10,12},{12,14},{14,16},{16,18},{18... | collective-permute-start | bytes 3145736 | tf_op jit(solution)/shard_map/ppermute | solution.py:683
  18.4 1.9 %select_tails.1 = (bf16[4,2,160,256]{3,2,1,0:T(8,128)(2,1)}, bf16[4,2,160,256]{3,2,1,0:T(8,128)(2,1)}) custom-call(s32[1]{0:T(128)} %bitcast.me_ref, bf16[128,4096]{1,0:T(8,128)(2,1)} %hold.1.tail_hbm, s32[9,256]{1,0:T(8,128)} %bitcast.31), custom_call_target="tpu_custom_call" | custom-call | flops 1000000000 | bytes 2000000 | tf_op jit(solution)/shard_map/select_tails/pallas_call | solution.py:518
  20.3 0.7 collective-permute-start.7
  21.0 0.0 collective-permute-done.1
  21.0 1.2 %fusion.8.after = bf16[16,4096]{1,0:T(8,128)(2,1)S(1)} fusion(bf16[16,4096]{1,0:T(8,128)(2,1)} %collective-permute-done.1, f32[16,4096]{1,0:T(8,128)S(1)} %get-tuple-element.29.spread_ref, pred[]{:T(512)S(6)} %ne.22, f32[16,4096]{1,0:T(8,128)} %get-tuple-element.31, bf16[16,4096]{1,0:T(8,128)(2,1)} %copy-done.16, pred[]{:T(512)S(6)} %ne.23), kind=kLoop, calls=%fused_computation.24 | loop fusion | flops 1048576 | bytes 917506 | tf_op jit(solution)/shard_map/convert_element_type | solution.py:645
  22.2 2.1 %collective-permute-start.3 = (bf16[16,4096]{1,0:T(8,128)(2,1)S(1)}, bf16[16,4096]{1,0:T(8,128)(2,1)S(1)}, u32[]{:S(2)}, u32[]{:S(2)}) collective-permute-start(bf16[16,4096]{1,0:T(8,128)(2,1)S(1)} %fusion.8.after), channel_id=1, source_target_pairs={{0,8},{2,10},{4,12},{8,0},{10,2},{12,4},{14,6},{16,24},{18,26},{20... | collective-permute-start | bytes 393224 | tf_op jit(solution)/shard_map/ppermute | solution.py:625
  24.4 0.7 collective-permute-start.4
  25.1 0.0 copy-done
  25.1 0.0 copy-done.1
  25.1 0.0 copy-done.13
  25.1 0.0 copy-start.18
  25.1 0.0 copy-start.15
  25.1 0.0 copy-start.17
  25.1 9.9 %local_conv.1 = (bf16[384,4096]{1,0:T(8,128)(2,1)S(1)}, f32[8,128]{1,0:T(8,128)S(1)}) custom-call(bf16[384,4096]{1,0:T(8,128)(2,1)S(1)} %copy-done, bf16[384,4096]{1,0:T(8,128)(2,1)S(1)} %copy-done.1, f32[256,128]{1,0:T(8,128)S(1)} %get-tuple-element.27.taps_rev, f32[256,128]{1,0:T(8,128)S(1)} %copy-done.13, bf16[16,4096]{1,0:T(8,128)(2,1)S(1)} %fusion.8.after), custom_call_target="tpu_custom_call" | custom-call | flops 8589934592 | bytes 6291456 | tf_op jit(solution)/shard_map/local_conv/pallas_call | solution.py:228
  35.0 0.0 copy-start.2
  35.1 0.0 copy-start.3
  35.1 0.0 copy-start.4
  35.1 0.5 slice.26
  35.6 0.0 collective-permute-done.7
  35.6 0.0 copy-done.18
  35.6 1.0 %add_select_fusion = bf16[4,2,160,256]{3,2,1,0:T(8,128)(2,1)S(1)} fusion(bf16[4,2,160,256]{3,2,1,0:T(8,128)(2,1)S(1)} %copy-done.18, bf16[4,2,160,256]{3,2,1,0:T(8,128)(2,1)S(1)} %collective-permute-done.7, pred[]{:T(512)S(6)} %ne.22, bf16[]{:T(256)} %bitcast.5), kind=kLoop, calls=%fused_computation | loop fusion | flops 655360 | bytes 1966083 | tf_op jit(solution)/shard_map/jit(_where)/select_n | solution.py:596
  36.6 0.7 collective-permute-start.10
  37.3 0.7 collective-permute-start.8
  38.0 0.0 collective-permute-done.3
  38.0 1.3 %collective-permute-start.9 = (bf16[2,160,256]{2,1,0:T(8,128)(2,1)S(1)}, bf16[2,160,256]{2,1,0:T(8,128)(2,1)S(1)}, u32[]{:S(2)}, u32[]{:S(2)}) collective-permute-start(bf16[2,160,256]{2,1,0:T(8,128)(2,1)S(1)} %get-tuple-element.57), channel_id=1, source_target_pairs={{26,10},{30,14},{27,11},{31,15}} | collective-permute-start | bytes 491528 | tf_op jit(solution)/shard_map/ppermute | solution.py:603
  39.3 0.0 collective-permute-done.4
  39.3 0.0 copy-done.15
  39.3 0.0 copy-done.17
  39.3 1.3 %fusion.10 = (bf16[16,4096]{1,0:T(8,128)(2,1)S(1)}, f32[16,4096]{1,0:T(8,128)S(1)}, f32[16,4096]{1,0:T(8,128)S(1)}) fusion(f32[16,4096]{1,0:T(8,128)S(1)} %copy-done.15, bf16[16,4096]{1,0:T(8,128)(2,1)S(1)} %copy-done.17, pred[]{:T(512)S(6)} %ne.23, bf16[16,4096]{1,0:T(8,128)(2,1)} %collective-permute-done.1, pred[]{:T(512)S(6)} %ne.22, ...), kind=kLoop, calls=%fused_computation.27 | loop fusion | flops 2359296 | bytes 1703947 | tf_op jit(solution)/shard_map/convert_element_type | solution.py:645
  40.7 10.2 %collective-permute-start.5 = (bf16[16,4096]{1,0:T(8,128)(2,1)S(1)}, bf16[16,4096]{1,0:T(8,128)(2,1)S(1)}, u32[]{:S(2)}, u32[]{:S(2)}) collective-permute-start(bf16[16,4096]{1,0:T(8,128)(2,1)S(1)} %get-tuple-element.52.after), channel_id=1, source_target_pairs={{0,16},{2,18},{4,20},{6,22},{8,24},{10,26},{12,28},{14,30},{16,0},... | collective-permute-start | bytes 393224 | tf_op jit(solution)/shard_map/ppermute | solution.py:621
  50.9 0.0 collective-permute-done.2.tail_ref
  50.9 0.0 copy-done.2
  50.9 4.0 %carry.1 = (bf16[128,4096]{1,0:T(8,128)(2,1)S(1)}, f32[8,128]{1,0:T(8,128)S(1)}, bf16[384,4096]{1,0:T(8,128)(2,1)S(1)}, f32[16,4096]{1,0:T(8,128)S(1)}, f32[16,4096]{1,0:T(8,128)S(1)}, /*index=5*/f32[32,128]{1,0:T(8,128)S(1)}) custom-call(bf16[384,4096]{1,0:T(8,128)(2,1)S(1)} %get-tuple-element.32.local_ref, ...), custom_call_target="tpu_custom_call" | custom-call | flops 536870912 | bytes 3145728 | tf_op jit(solution)/shard_map/carry/pallas_call | solution.py:283
  55.0 0.5 slice.28
  55.5 0.0 collective-permute-done.10
  55.5 0.0 collective-permute-done.8
  55.5 0.5 collective-permute-done.9
  56.0 0.7 fusion.7
  56.7 1.3 %collective-permute-start.11 = (bf16[1,160,256]{2,1,0:T(8,128)(2,1)S(1)}, bf16[1,160,256]{2,1,0:T(8,128)(2,1)S(1)}, u32[]{:S(2)}, u32[]{:S(2)}) collective-permute-start(bf16[1,160,256]{2,1,0:T(8,128)(2,1)S(1)} %get-tuple-element.58), channel_id=1, source_target_pairs={{2,0},{6,4},{10,8},{14,12},{18,16},{22,20},{26,24},{30,28},{3,1},{... | collective-permute-start | bytes 245768 | tf_op jit(solution)/shard_map/ppermute | solution.py:611
  58.0 1.1 %collective-permute-done.5.other_ref = bf16[16,4096]{1,0:T(8,128)(2,1)S(1)} collective-permute-done((bf16[16,4096]{1,0:T(8,128)(2,1)S(1)}, bf16[16,4096]{1,0:T(8,128)(2,1)S(1)}, u32[]{:S(2)}, u32[]{:S(2)}) %collective-permute-start.5) | collective-permute-done | bytes 131104 | tf_op jit(solution)/shard_map/ppermute | solution.py:621
  59.1 3.9 %gate.1 = (bf16[384,4096]{1,0:T(8,128)(2,1)S(1)}, f32[8,384]{1,0:T(8,128)S(1)}) custom-call(s32[1]{0:T(128)} %bitcast.me_ref, bf16[128,4096]{1,0:T(8,128)(2,1)S(1)} %get-tuple-element.37.first_ref, bf16[384,4096]{1,0:T(8,128)(2,1)S(1)} %get-tuple-element.32.local_ref, bf16[384,4096]{1,0:T(8,128)(2,1)S(1)} %get-tuple-element.38.q_ref, ...), custom_call_target="tpu_custom_call" | custom-call | flops 1073741824 | bytes 9437184 | tf_op jit(solution)/shard_map/gate/pallas_call | solution.py:390
  63.0 2.9 %collective-permute-start.6 = (f32[8,384]{1,0:T(8,128)S(1)}, f32[8,384]{1,0:T(8,128)S(1)}, u32[]{:S(2)}, u32[]{:S(2)}) collective-permute-start(f32[8,384]{1,0:T(8,128)S(1)} %get-tuple-element.43.refs_0_), channel_id=1, source_target_pairs={{0,1},{1,0},{2,3},{3,2},{4,5},{5,4},{6,7},{7,6},{8,9},{9,8},{10,11... | collective-permute-start | bytes 36872 | tf_op jit(solution)/shard_map/ppermute | solution.py:651
  65.9 0.8 %collective-permute-done.6.refs_1_ = f32[8,384]{1,0:T(8,128)S(1)} collective-permute-done((f32[8,384]{1,0:T(8,128)S(1)}, f32[8,384]{1,0:T(8,128)S(1)}, u32[]{:S(2)}, u32[]{:S(2)}) %collective-permute-start.6) | collective-permute-done | bytes 12320 | tf_op jit(solution)/shard_map/ppermute | solution.py:651
  66.7 3.0 %norm.1 = (bf16[384,4096]{1,0:T(8,128)(2,1)}, f32[8,128]{1,0:T(8,128)S(1)}) custom-call(f32[8,384]{1,0:T(8,128)S(1)} %get-tuple-element.43.refs_0_, f32[8,384]{1,0:T(8,128)S(1)} %collective-permute-done.6.refs_1_, bf16[384,4096]{1,0:T(8,128)(2,1)S(1)} %get-tuple-element.44.refs_2_, f32[1,4096]{1,0:T(1,128)S(1)} %bitcast.28), custom_call_target="tpu_custom_call" | custom-call | flops 3145728 | bytes 6291456 | tf_op jit(solution)/shard_map/norm/pallas_call | solution.py:434
  69.7 0.0 collective-permute-done.11
  69.7 1.4 %handoff.1 = f32[16,16,145]{2,1,0:T(8,128)} custom-call(s32[1]{0:T(128)} %bitcast.me_ref, f32[16,4096]{1,0:T(8,128)S(1)} %get-tuple-element.53.total_ref, bf16[16,4096]{1,0:T(8,128)(2,1)S(1)} %collective-permute-done.5.other_ref, f32[16,4096]{1,0:T(8,128)S(1)} %get-tuple-element.29.spread_ref, f32[16,4096]{1,0:T(8,128)S(1)} %copy-done.11, ...), custom_call_target="tpu_custom_call" | custom-call | flops 1000000000 | bytes 1000000 | tf_op jit(solution)/shard_map/handoff/pallas_call | solution.py:565
  (19 shorter events, 0.1 us)
Async XLA Ops:
  0.6 7.9 %copy-start.5 = (f32[256,16]{0,1:T(8,128)S(1)}, f32[256,16]{0,1:T(8,128)}, u32[]{:S(2)}) copy-start(f32[256,16]{0,1:T(8,128)} %param.12) | copy-start | bytes 49156
  0.6 7.9 %copy-start.6 = (f32[256,128]{1,0:T(8,128)S(1)}, f32[256,128]{1,0:T(8,128)}, u32[]{:S(2)}) copy-start(f32[256,128]{1,0:T(8,128)} %taps_ref.1) | copy-start | bytes 393220
  0.7 7.9 %copy-start.9 = (f32[256,16]{0,1:T(8,128)S(1)}, f32[256,16]{0,1:T(8,128)}, u32[]{:S(2)}) copy-start(f32[256,16]{0,1:T(8,128)} %param.11) | copy-start | bytes 49156
  8.2 4.6 %collective-permute-start = (bf16[16,4096]{1,0:T(8,128)(2,1)}, bf16[16,4096]{1,0:T(8,128)(2,1)S(1)}, u32[]{:S(2)}, u32[]{:S(2)}) collective-permute-start(bf16[16,4096]{1,0:T(8,128)(2,1)} %get-tuple-element.30), channel_id=1, source_target_pairs={{0,2},{2,0},{4,6},{6,4},{8,10},{10,8},{12,14},{14,12},{16,18},{18,... | collective-permute-start | bytes 393224 | tf_op jit(solution)/shard_map/ppermute | solution.py:621
  10.3 0.7 copy-start.10
  11.0 4.9 %copy-start.12 = (f32[256,128]{1,0:T(8,128)}, f32[256,128]{1,0:T(8,128)S(1)}, u32[]{:S(2)}) copy-start(f32[256,128]{1,0:T(8,128)S(1)} %get-tuple-element.28.response) | copy-start | bytes 393220
  12.9 3.0 %copy-start.16 = (bf16[16,4096]{1,0:T(8,128)(2,1)}, bf16[16,4096]{1,0:T(8,128)(2,1)S(1)}, u32[]{:S(2)}) copy-start(bf16[16,4096]{1,0:T(8,128)(2,1)S(1)} %collective-permute-done) | copy-start | bytes 393220
  14.6 6.4 %collective-permute-start.1 = (bf16[16,4096]{1,0:T(8,128)(2,1)}, bf16[16,4096]{1,0:T(8,128)(2,1)}, u32[]{:S(2)}, u32[]{:S(2)}) collective-permute-start(bf16[16,4096]{1,0:T(8,128)(2,1)} %fusion.9.refs_1_), channel_id=1, source_target_pairs={{0,4},{2,6},{4,0},{6,2},{8,12},{10,14},{12,8},{14,10},{16,20},{18,... | collective-permute-start | bytes 393224 | tf_op jit(solution)/shard_map/ppermute | solution.py:621
  15.8 9.2 %copy-start = (bf16[384,4096]{1,0:T(8,128)(2,1)S(1)}, bf16[384,4096]{1,0:T(8,128)(2,1)}, u32[]{:S(2)}) copy-start(bf16[384,4096]{1,0:T(8,128)(2,1)} %k_hbm.3) | copy-start | bytes 9437188
  15.9 9.2 %copy-start.1 = (bf16[384,4096]{1,0:T(8,128)(2,1)S(1)}, bf16[384,4096]{1,0:T(8,128)(2,1)}, u32[]{:S(2)}) copy-start(bf16[384,4096]{1,0:T(8,128)(2,1)} %v_hbm.3) | copy-start | bytes 9437188
  15.9 9.2 %copy-start.13 = (f32[256,128]{1,0:T(8,128)S(1)}, f32[256,128]{1,0:T(8,128)}, u32[]{:S(2)}) copy-start(f32[256,128]{1,0:T(8,128)} %copy-done.12) | copy-start | bytes 393220
  15.9 35.0 %collective-permute-start.2 = (bf16[128,4096]{1,0:T(8,128)(2,1)}, bf16[128,4096]{1,0:T(8,128)(2,1)S(1)}, u32[]{:S(2)}, u32[]{:S(2)}) collective-permute-start(bf16[128,4096]{1,0:T(8,128)(2,1)} %hold.1.tail_hbm), channel_id=1, source_target_pairs={{0,2},{2,4},{4,6},{6,8},{8,10},{10,12},{12,14},{14,16},{16,18},{18... | collective-permute-start | bytes 3145736 | tf_op jit(solution)/shard_map/ppermute | solution.py:683
  20.3 15.3 %collective-permute-start.7 = (bf16[4,2,160,256]{3,2,1,0:T(8,128)(2,1)}, bf16[4,2,160,256]{3,2,1,0:T(8,128)(2,1)S(1)}, u32[]{:S(2)}, u32[]{:S(2)}) collective-permute-start(bf16[4,2,160,256]{3,2,1,0:T(8,128)(2,1)} %get-tuple-element.48), channel_id=1, source_target_pairs={{30,26},{31,27}} | collective-permute-start | bytes 1966088 | tf_op jit(solution)/shard_map/ppermute | solution.py:595
  22.2 15.8 %collective-permute-start.3 = (bf16[16,4096]{1,0:T(8,128)(2,1)S(1)}, bf16[16,4096]{1,0:T(8,128)(2,1)S(1)}, u32[]{:S(2)}, u32[]{:S(2)}) collective-permute-start(bf16[16,4096]{1,0:T(8,128)(2,1)S(1)} %fusion.8.after), channel_id=1, source_target_pairs={{0,8},{2,10},{4,12},{8,0},{10,2},{12,4},{14,6},{16,24},{18,26},{20... | collective-permute-start | bytes 393224 | tf_op jit(solution)/shard_map/ppermute | solution.py:625
  24.4 14.9 %collective-permute-start.4 = (bf16[16,4096]{1,0:T(8,128)(2,1)S(1)}, bf16[16,4096]{1,0:T(8,128)(2,1)S(1)}, u32[]{:S(2)}, u32[]{:S(2)}) collective-permute-start(bf16[16,4096]{1,0:T(8,128)(2,1)S(1)} %fusion.8.after), channel_id=1, source_target_pairs={{2,14},{18,30},{3,15},{19,31}} | collective-permute-start | bytes 393224 | tf_op jit(solution)/shard_map/ppermute | solution.py:625
  25.1 10.5 %copy-start.18 = (bf16[4,2,160,256]{3,2,1,0:T(8,128)(2,1)S(1)}, bf16[4,2,160,256]{3,2,1,0:T(8,128)(2,1)}, u32[]{:S(2)}) copy-start(bf16[4,2,160,256]{3,2,1,0:T(8,128)(2,1)} %get-tuple-element.47) | copy-start | bytes 1966084
  25.1 14.2 %copy-start.15 = (f32[16,4096]{1,0:T(8,128)S(1)}, f32[16,4096]{1,0:T(8,128)}, u32[]{:S(2)}) copy-start(f32[16,4096]{1,0:T(8,128)} %get-tuple-element.31) | copy-start | bytes 786436
  25.1 14.2 %copy-start.17 = (bf16[16,4096]{1,0:T(8,128)(2,1)S(1)}, bf16[16,4096]{1,0:T(8,128)(2,1)}, u32[]{:S(2)}) copy-start(bf16[16,4096]{1,0:T(8,128)(2,1)} %copy-done.16) | copy-start | bytes 393220
  35.0 15.9 %copy-start.2 = (bf16[384,4096]{1,0:T(8,128)(2,1)S(1)}, bf16[384,4096]{1,0:T(8,128)(2,1)}, u32[]{:S(2)}) copy-start(bf16[384,4096]{1,0:T(8,128)(2,1)} %q_hbm.1) | copy-start | bytes 9437188
  35.1 15.8 %copy-start.3 = (f32[16,4096]{1,0:T(8,128)S(1)}, f32[16,4096]{1,0:T(8,128)}, u32[]{:S(2)}) copy-start(f32[16,4096]{1,0:T(8,128)} %get-tuple-element.34.p1_hbm) | copy-start | bytes 786436
  35.1 15.8 %copy-start.4 = (f32[16,4096]{1,0:T(8,128)S(1)}, f32[16,4096]{1,0:T(8,128)}, u32[]{:S(2)}) copy-start(f32[16,4096]{1,0:T(8,128)} %get-tuple-element.35.p2_hbm) | copy-start | bytes 786436
  36.6 18.8 %collective-permute-start.10 = (bf16[2,160,256]{2,1,0:T(8,128)(2,1)S(1)}, bf16[2,160,256]{2,1,0:T(8,128)(2,1)S(1)}, u32[]{:S(2)}, u32[]{:S(2)}) collective-permute-start(bf16[2,160,256]{2,1,0:T(8,128)(2,1)S(1)} %get-tuple-element.56), channel_id=1, source_target_pairs={{26,2},{30,6},{27,3},{31,7}} | collective-permute-start | bytes 491528 | tf_op jit(solution)/shard_map/ppermute | solution.py:603
  37.3 18.2 %collective-permute-start.8 = (bf16[2,160,256]{2,1,0:T(8,128)(2,1)S(1)}, bf16[2,160,256]{2,1,0:T(8,128)(2,1)S(1)}, u32[]{:S(2)}, u32[]{:S(2)}) collective-permute-start(bf16[2,160,256]{2,1,0:T(8,128)(2,1)S(1)} %get-tuple-element.55), channel_id=1, source_target_pairs={{26,18},{30,22},{27,19},{31,23}} | collective-permute-start | bytes 491528 | tf_op jit(solution)/shard_map/ppermute | solution.py:603
  38.0 18.0 %collective-permute-start.9 = (bf16[2,160,256]{2,1,0:T(8,128)(2,1)S(1)}, bf16[2,160,256]{2,1,0:T(8,128)(2,1)S(1)}, u32[]{:S(2)}, u32[]{:S(2)}) collective-permute-start(bf16[2,160,256]{2,1,0:T(8,128)(2,1)S(1)} %get-tuple-element.57), channel_id=1, source_target_pairs={{26,10},{30,14},{27,11},{31,15}} | collective-permute-start | bytes 491528 | tf_op jit(solution)/shard_map/ppermute | solution.py:603
  40.7 18.4 %collective-permute-start.5 = (bf16[16,4096]{1,0:T(8,128)(2,1)S(1)}, bf16[16,4096]{1,0:T(8,128)(2,1)S(1)}, u32[]{:S(2)}, u32[]{:S(2)}) collective-permute-start(bf16[16,4096]{1,0:T(8,128)(2,1)S(1)} %get-tuple-element.52.after), channel_id=1, source_target_pairs={{0,16},{2,18},{4,20},{6,22},{8,24},{10,26},{12,28},{14,30},{16,0},... | collective-permute-start | bytes 393224 | tf_op jit(solution)/shard_map/ppermute | solution.py:621
  50.9 8.2 %copy-start.8 = (f32[32,128]{1,0:T(8,128)S(1)}, f32[32,128]{1,0:T(8,128)}, u32[]{:S(2)}) copy-start(f32[32,128]{1,0:T(8,128)} %get-tuple-element.41.rates_ref) | copy-start | bytes 49156
  56.7 13.0 %collective-permute-start.11 = (bf16[1,160,256]{2,1,0:T(8,128)(2,1)S(1)}, bf16[1,160,256]{2,1,0:T(8,128)(2,1)S(1)}, u32[]{:S(2)}, u32[]{:S(2)}) collective-permute-start(bf16[1,160,256]{2,1,0:T(8,128)(2,1)S(1)} %get-tuple-element.58), channel_id=1, source_target_pairs={{2,0},{6,4},{10,8},{14,12},{18,16},{22,20},{26,24},{30,28},{3,1},{... | collective-permute-start | bytes 245768 | tf_op jit(solution)/shard_map/ppermute | solution.py:611
  59.1 7.6 %copy-start.7 = (f32[4096]{0:T(1024)S(1)}, f32[4096]{0:T(1024)}, u32[]{:S(2)}) copy-start(f32[4096]{0:T(1024)} %param.14) | copy-start | bytes 49156
  62.9 6.8 %copy-start.11 = (f32[16,4096]{1,0:T(8,128)S(1)}, f32[16,4096]{1,0:T(8,128)}, u32[]{:S(2)}) copy-start(f32[16,4096]{1,0:T(8,128)} %copy-done.10) | copy-start | bytes 786436
  63.0 6.8 %copy-start.14 = (s32[256,9]{0,1:T(8,128)S(1)}, s32[256,9]{0,1:T(8,128)}, u32[]{:S(2)}) copy-start(s32[256,9]{0,1:T(8,128)} %param.15) | copy-start | bytes 27652
  63.0 3.8 %collective-permute-start.6 = (f32[8,384]{1,0:T(8,128)S(1)}, f32[8,384]{1,0:T(8,128)S(1)}, u32[]{:S(2)}, u32[]{:S(2)}) collective-permute-start(f32[8,384]{1,0:T(8,128)S(1)} %get-tuple-element.43.refs_0_), channel_id=1, source_target_pairs={{0,1},{1,0},{2,3},{3,2},{4,5},{5,4},{6,7},{7,6},{8,9},{9,8},{10,11... | collective-permute-start | bytes 36872 | tf_op jit(solution)/shard_map/ppermute | solution.py:651

commit v3 on v2

--- a/solution.py
+++ b/solution.py
@@ -128,7 +128,7 @@
 
 def product_and_states(key_rows, value_rows, rates_t):
     tokens, channels = key_rows.shape
-    chunks = min(8, channels // LANES // 2)
+    chunks = 4
     tiles = channels // LANES // chunks
     state_shape = jax.ShapeDtypeStruct((MODES, channels), f32)
     return pl.pallas_call(
@@ -499,8 +499,8 @@
             for p in range(inner):
                 r = o * inner + p
                 for b in range(blocks):
-                    rank = jnp.where(plan[b : b + 1] == r, ranks[r : r + 1], -1.0)
-                    rank = jnp.broadcast_to(rank, (slots, groups)).astype(bf16)
+                    rank = jnp.where(plan[b : b + 1] == r, ranks[r : r + 1], -1.0).astype(bf16)
+                    rank = jnp.broadcast_to(rank, (slots, groups))
                     picks_ref[p * slots : (p + 1) * slots, b * groups : (b + 1) * groups] = jnp.where(
                         rank == slot, jnp.ones((), bf16), jnp.zeros((), bf16)
                     )
@@ -524,7 +524,7 @@
             pltpu.VMEM((blocks * groups, MODES * GW), bf16), pltpu.VMEM((inner * slots, blocks * groups), bf16),
             pltpu.VMEM(tail.shape, bf16), pltpu.SemaphoreType.DMA,
         ],
-        compiler_params=params(56),
+        compiler_params=params(20),
         cost_estimate=pl.CostEstimate(flops=10**9, bytes_accessed=2 * 10**6, transcendentals=0),
         name="select_tails",
     )(me, tail, plan_cols)

time: 71.5 us -> 70.2 us (0.982)
  local copies, waits for them, and re-layouts: 1.86 us -> 4.49 us
  Pallas kernels: 33.3 us -> 30.9 us
  waiting for transfers between devices: 4.33 us -> 2.58 us
    unnamed x38 -> x40, local copies, waits for them, and re-layouts: 0.78 us -> 3.35 us
    pallas_call x1, Pallas kernels: 1.9 us -> 0.1 us  [select_tails(): pl.pallas_call(functools.partial(select_kernel, blocks, slots, inner, out...]
    ppermute x3, waiting for transfers between devices: 2.99 us -> 1.73 us  [exchange(): return [lax.ppermute(sent, 'seq', pairs)]]
    ppermute x1, starting transfers between devices: 2.93 us -> 4.08 us  [sum_over_chan(): return [energy, lax.ppermute(energy, 'chan', [(0, 1), (1, 0)])]]
    ppermute x3, starting transfers between devices: 11.8 us -> 10.7 us  [exchange(): return [lax.ppermute(sent, 'seq', pairs)]]
  transfers between devices with their start and end apart: 12 -> 12, of which waited for: 4 -> 3; matrix products, arithmetic and copies ran while one was open for 7% -> 8% of each run, Pallas kernels for 34% -> 32%
where the time goes in v3:
time: 70.2 us; the launch traced here: 69.7 us
  Pallas kernels  30.9 us (44%)
  starting transfers between devices  24.7 us (35%)
  other arithmetic  6.03 us (9%)
  local copies, waits for them, and re-layouts  4.49 us (6%)
  waiting for transfers between devices  2.58 us (4%)
  between operations  1.02 us (1%)
    ppermute x3, starting transfers between devices, exchange(): return [lax.ppermute(sent, 'seq', pairs)]  10.7 us
    pallas_call x1, Pallas kernels, local_part(): pl.pallas_call(functools.partial(local_kernel, chunks, tiles), in_specs=[...  9.92 us
    pallas_call x1, Pallas kernels, product_and_states(): pl.pallas_call(functools.partial(product_kernel, chunks, tiles), in_specs...  7.02 us
    convert_element_type x3, other arithmetic, scan_states(): sent = total.astype(bf16)  4.27 us
    ppermute x1, starting transfers between devices, sum_over_chan(): return [energy, lax.ppermute(energy, 'chan', [(0, 1), (1, 0)])]  4.08 us
    pallas_call x1, Pallas kernels, carry_part(): pl.pallas_call(functools.partial(carry_kernel, chunks, tiles), in_specs=[...  4.03 us
    pallas_call x1, Pallas kernels, gate_part(): pl.pallas_call(functools.partial(gate_kernel, chunks, tiles, step), in_sp...  3.86 us
    unnamed x40, local copies, waits for them, and re-layouts  3.35 us
  transfers between devices with their start and end apart: 12, of which 3 were waited for; matrix products, arithmetic and copies ran while one was open for 8% of the time, Pallas kernels for 32%

profile of v3, /device:TPU:11, one launch (start us, length us, event | category | flops | bytes accessed | tf_op | source)
XLA Modules:
  0.0 69.7 jit_solution(8021404891273072750)
XLA Ops:
  0.6 0.0 copy-start.6
  0.6 0.0 copy-start.7
  0.7 0.0 copy-start.10
  0.7 7.0 %product_states.1 = (bf16[128,4096]{1,0:T(8,128)(2,1)}, f32[16,4096]{1,0:T(8,128)}, f32[16,4096]{1,0:T(8,128)}, f32[16,4096]{1,0:T(8,128)}, bf16[16,4096]{1,0:T(8,128)(2,1)}, /*index=5*/f32[32,128]{1,0:T(8,128)}) custom-call(bf16[384,4096]{1,0:T(8,128)(2,1)} %k_hbm.3, bf16[384,4096]{1,0:T(8,128)(2,1)} %v_hbm.3, f32[16,256]{1,0:T(8,128)} %bitcast.26), custom_call_target="tpu_custom_call" | custom-call | flops 1207959552 | bytes 9437184 | tf_op jit(solution)/shard_map/product_states/pallas_call | solution.py:134
  7.7 0.3 collective-permute-start
  8.0 0.0 copy-done.6
  8.0 0.0 copy-done.7
  8.1 0.0 copy-done.10
  8.1 1.6 %prepare.1 = (f32[16,4096]{1,0:T(8,128)S(1)}, f32[16,4096]{1,0:T(8,128)S(1)}, f32[256,128]{1,0:T(8,128)S(1)}, f32[256,128]{1,0:T(8,128)S(1)}, f32[32,128]{1,0:T(8,128)S(1)}) custom-call(f32[16,256]{1,0:T(8,128)S(1)} %bitcast.27, f32[16,256]{1,0:T(8,128)S(1)} %negate_sqrt_fusion.factor_ref, f32[16,256]{1,0:T(8,128)S(1)} %bitcast.29, f32[256,128]{1,0:T(8,128)S(1)} %copy-done.7), custom_call_target="tpu_custom_call" | custom-call | tf_op jit(solution)/shard_map/prepare/pallas_call | solution.py:324
  9.7 0.0 copy-start.11
  9.7 0.7 copy-done.11
  10.4 0.7 copy-done.13
  11.1 1.3 %collective-permute-done = bf16[16,4096]{1,0:T(8,128)(2,1)S(1)} collective-permute-done((bf16[16,4096]{1,0:T(8,128)(2,1)}, bf16[16,4096]{1,0:T(8,128)(2,1)S(1)}, u32[]{:S(2)}, u32[]{:S(2)}) %collective-permute-start) | collective-permute-done | bytes 131104 | tf_op jit(solution)/shard_map/ppermute | solution.py:621
  12.3 1.7 %fusion.9.refs_1_ = bf16[16,4096]{1,0:T(8,128)(2,1)} fusion(f32[16,4096]{1,0:T(8,128)} %get-tuple-element.31, bf16[16,4096]{1,0:T(8,128)(2,1)S(1)} %collective-permute-done, f32[16,4096]{1,0:T(8,128)S(1)} %get-tuple-element.29.spread_ref, pred[]{:T(512)S(6)} %ne.23), kind=kLoop, calls=%fused_computation.26 | loop fusion | flops 589824 | bytes 786433 | tf_op jit(solution)/shard_map/convert_element_type | solution.py:645
  14.1 1.2 %collective-permute-start.1 = (bf16[16,4096]{1,0:T(8,128)(2,1)}, bf16[16,4096]{1,0:T(8,128)(2,1)}, u32[]{:S(2)}, u32[]{:S(2)}) collective-permute-start(bf16[16,4096]{1,0:T(8,128)(2,1)} %fusion.9.refs_1_), channel_id=1, source_target_pairs={{0,4},{2,6},{4,0},{6,2},{8,12},{10,14},{12,8},{14,10},{16,20},{18,... | collective-permute-start | bytes 393224 | tf_op jit(solution)/shard_map/ppermute | solution.py:621
  15.3 0.0 copy-done.18
  15.3 2.5 %collective-permute-start.2 = (bf16[128,4096]{1,0:T(8,128)(2,1)}, bf16[128,4096]{1,0:T(8,128)(2,1)S(1)}, u32[]{:S(2)}, u32[]{:S(2)}) collective-permute-start(bf16[128,4096]{1,0:T(8,128)(2,1)} %hold.1.tail_hbm), channel_id=1, source_target_pairs={{0,2},{2,4},{4,6},{6,8},{8,10},{10,12},{12,14},{14,16},{16,18},{18... | collective-permute-start | bytes 3145736 | tf_op jit(solution)/shard_map/ppermute | solution.py:683
  17.8 0.0 copy-start.3
  17.8 1.2 %copy-done.3 = bf16[128,4096]{1,0:T(8,128)(2,1)S(1)} copy-done((bf16[128,4096]{1,0:T(8,128)(2,1)S(1)}, bf16[128,4096]{1,0:T(8,128)(2,1)}, u32[]{:S(2)}) %copy-start.3) | copy-done | bytes 1048600
  19.1 0.7 %copy-done.15 = s32[256,9]{0,1:T(8,128)S(1)} copy-done((s32[256,9]{0,1:T(8,128)S(1)}, s32[256,9]{0,1:T(8,128)}, u32[]{:S(2)}) %copy-start.15) | copy-done | bytes 9240
  19.8 0.1 select_tails.1
  19.9 0.7 %collective-permute-start.7 = (bf16[4,2,160,256]{3,2,1,0:T(8,128)(2,1)S(1)}, bf16[4,2,160,256]{3,2,1,0:T(8,128)(2,1)S(1)}, u32[]{:S(2)}, u32[]{:S(2)}) collective-permute-start(bf16[4,2,160,256]{3,2,1,0:T(8,128)(2,1)S(1)} %get-tuple-element.48), channel_id=1, source_target_pairs={{30,26},{31,27}} | collective-permute-start | bytes 1966088 | tf_op jit(solution)/shard_map/ppermute | solution.py:595
  20.6 0.0 collective-permute-done.1
  20.6 1.2 %fusion.8.after = bf16[16,4096]{1,0:T(8,128)(2,1)S(1)} fusion(bf16[16,4096]{1,0:T(8,128)(2,1)} %collective-permute-done.1, f32[16,4096]{1,0:T(8,128)S(1)} %get-tuple-element.29.spread_ref, pred[]{:T(512)S(6)} %ne.22, f32[16,4096]{1,0:T(8,128)} %get-tuple-element.31, bf16[16,4096]{1,0:T(8,128)(2,1)} %copy-done.18, pred[]{:T(512)S(6)} %ne.23), kind=kLoop, calls=%fused_computation.24 | loop fusion | flops 1048576 | bytes 917506 | tf_op jit(solution)/shard_map/convert_element_type | solution.py:645
  21.8 2.1 %collective-permute-start.3 = (bf16[16,4096]{1,0:T(8,128)(2,1)S(1)}, bf16[16,4096]{1,0:T(8,128)(2,1)S(1)}, u32[]{:S(2)}, u32[]{:S(2)}) collective-permute-start(bf16[16,4096]{1,0:T(8,128)(2,1)S(1)} %fusion.8.after), channel_id=1, source_target_pairs={{0,8},{2,10},{4,12},{8,0},{10,2},{12,4},{14,6},{16,24},{18,26},{20... | collective-permute-start | bytes 393224 | tf_op jit(solution)/shard_map/ppermute | solution.py:625
  24.0 0.7 collective-permute-start.4
  24.7 0.0 copy-done
  24.7 0.0 copy-done.1
  24.7 0.0 copy-done.14
  24.7 0.0 copy-start.17
  24.7 0.0 copy-start.19
  24.7 9.9 %local_conv.1 = (bf16[384,4096]{1,0:T(8,128)(2,1)S(1)}, f32[8,128]{1,0:T(8,128)S(1)}) custom-call(bf16[384,4096]{1,0:T(8,128)(2,1)S(1)} %copy-done, bf16[384,4096]{1,0:T(8,128)(2,1)S(1)} %copy-done.1, f32[256,128]{1,0:T(8,128)S(1)} %get-tuple-element.27.taps_rev, f32[256,128]{1,0:T(8,128)S(1)} %copy-done.14, bf16[16,4096]{1,0:T(8,128)(2,1)S(1)} %fusion.8.after), custom_call_target="tpu_custom_call" | custom-call | flops 8589934592 | bytes 6291456 | tf_op jit(solution)/shard_map/local_conv/pallas_call | solution.py:228
  34.6 0.0 copy-start.2
  34.6 0.0 copy-start.4
  34.7 0.0 copy-start.5
  34.7 0.6 slice.26
  35.2 0.0 collective-permute-done.7
  35.3 1.0 %add_select_fusion = bf16[4,2,160,256]{3,2,1,0:T(8,128)(2,1)S(1)} fusion(bf16[4,2,160,256]{3,2,1,0:T(8,128)(2,1)S(1)} %get-tuple-element.47, bf16[4,2,160,256]{3,2,1,0:T(8,128)(2,1)S(1)} %collective-permute-done.7, pred[]{:T(512)S(6)} %ne.22, bf16[]{:T(256)} %bitcast.5), kind=kLoop, calls=%fused_computation | loop fusion | flops 655360 | bytes 1966083 | tf_op jit(solution)/shard_map/jit(_where)/select_n | solution.py:596
  36.3 0.7 collective-permute-start.10
  37.0 0.7 collective-permute-start.8
  37.7 0.0 collective-permute-done.3
  37.7 1.3 %collective-permute-start.9 = (bf16[2,160,256]{2,1,0:T(8,128)(2,1)S(1)}, bf16[2,160,256]{2,1,0:T(8,128)(2,1)S(1)}, u32[]{:S(2)}, u32[]{:S(2)}) collective-permute-start(bf16[2,160,256]{2,1,0:T(8,128)(2,1)S(1)} %get-tuple-element.57), channel_id=1, source_target_pairs={{26,10},{30,14},{27,11},{31,15}} | collective-permute-start | bytes 491528 | tf_op jit(solution)/shard_map/ppermute | solution.py:603
  39.0 0.0 collective-permute-done.4
  39.0 0.0 copy-done.17
  39.0 1.3 %fusion.10 = (bf16[16,4096]{1,0:T(8,128)(2,1)S(1)}, f32[16,4096]{1,0:T(8,128)S(1)}, f32[16,4096]{1,0:T(8,128)S(1)}) fusion(f32[16,4096]{1,0:T(8,128)S(1)} %copy-done.17, bf16[16,4096]{1,0:T(8,128)(2,1)S(1)} %copy-done.19, pred[]{:T(512)S(6)} %ne.23, bf16[16,4096]{1,0:T(8,128)(2,1)} %collective-permute-done.1, pred[]{:T(512)S(6)} %ne.22, ...), kind=kLoop, calls=%fused_computation.27 | loop fusion | flops 2359296 | bytes 1703947 | tf_op jit(solution)/shard_map/convert_element_type | solution.py:645
  40.4 9.1 %collective-permute-start.5 = (bf16[16,4096]{1,0:T(8,128)(2,1)S(1)}, bf16[16,4096]{1,0:T(8,128)(2,1)S(1)}, u32[]{:S(2)}, u32[]{:S(2)}) collective-permute-start(bf16[16,4096]{1,0:T(8,128)(2,1)S(1)} %get-tuple-element.52.after), channel_id=1, source_target_pairs={{0,16},{2,18},{4,20},{6,22},{8,24},{10,26},{12,28},{14,30},{16,0},... | collective-permute-start | bytes 393224 | tf_op jit(solution)/shard_map/ppermute | solution.py:621
  49.5 0.0 collective-permute-done.2.tail_ref
  49.5 4.0 %carry.1 = (bf16[128,4096]{1,0:T(8,128)(2,1)S(1)}, f32[8,128]{1,0:T(8,128)S(1)}, bf16[384,4096]{1,0:T(8,128)(2,1)S(1)}, f32[16,4096]{1,0:T(8,128)S(1)}, f32[16,4096]{1,0:T(8,128)S(1)}, /*index=5*/f32[32,128]{1,0:T(8,128)S(1)}) custom-call(bf16[384,4096]{1,0:T(8,128)(2,1)S(1)} %get-tuple-element.32.local_ref, ...), custom_call_target="tpu_custom_call" | custom-call | flops 536870912 | bytes 3145728 | tf_op jit(solution)/shard_map/carry/pallas_call | solution.py:283
  53.5 0.5 slice.28
  54.1 0.0 collective-permute-done.10
  54.1 0.0 collective-permute-done.8
  54.1 0.0 collective-permute-done.9
  54.1 0.7 fusion.7
  54.8 1.3 %collective-permute-start.11 = (bf16[1,160,256]{2,1,0:T(8,128)(2,1)S(1)}, bf16[1,160,256]{2,1,0:T(8,128)(2,1)S(1)}, u32[]{:S(2)}, u32[]{:S(2)}) collective-permute-start(bf16[1,160,256]{2,1,0:T(8,128)(2,1)S(1)} %get-tuple-element.58), channel_id=1, source_target_pairs={{2,0},{6,4},{10,8},{14,12},{18,16},{22,20},{26,24},{30,28},{3,1},{... | collective-permute-start | bytes 245768 | tf_op jit(solution)/shard_map/ppermute | solution.py:611
  56.1 0.5 collective-permute-done.5.other_ref
  56.6 3.9 %gate.1 = (bf16[384,4096]{1,0:T(8,128)(2,1)S(1)}, f32[8,384]{1,0:T(8,128)S(1)}) custom-call(s32[1]{0:T(128)} %bitcast.me_ref, bf16[128,4096]{1,0:T(8,128)(2,1)S(1)} %get-tuple-element.37.first_ref, bf16[384,4096]{1,0:T(8,128)(2,1)S(1)} %get-tuple-element.32.local_ref, bf16[384,4096]{1,0:T(8,128)(2,1)S(1)} %get-tuple-element.38.q_ref, ...), custom_call_target="tpu_custom_call" | custom-call | flops 1073741824 | bytes 9437184 | tf_op jit(solution)/shard_map/gate/pallas_call | solution.py:390
  60.4 4.1 %collective-permute-start.6 = (f32[8,384]{1,0:T(8,128)S(1)}, f32[8,384]{1,0:T(8,128)S(1)}, u32[]{:S(2)}, u32[]{:S(2)}) collective-permute-start(f32[8,384]{1,0:T(8,128)S(1)} %get-tuple-element.43.refs_0_), channel_id=1, source_target_pairs={{0,1},{1,0},{2,3},{3,2},{4,5},{5,4},{6,7},{7,6},{8,9},{9,8},{10,11... | collective-permute-start | bytes 36872 | tf_op jit(solution)/shard_map/ppermute | solution.py:651
  64.5 0.8 %collective-permute-done.6.refs_1_ = f32[8,384]{1,0:T(8,128)S(1)} collective-permute-done((f32[8,384]{1,0:T(8,128)S(1)}, f32[8,384]{1,0:T(8,128)S(1)}, u32[]{:S(2)}, u32[]{:S(2)}) %collective-permute-start.6) | collective-permute-done | bytes 12320 | tf_op jit(solution)/shard_map/ppermute | solution.py:651
  65.3 0.0 copy-done.8
  65.3 3.0 %norm.1 = (bf16[384,4096]{1,0:T(8,128)(2,1)}, f32[8,128]{1,0:T(8,128)S(1)}) custom-call(f32[8,384]{1,0:T(8,128)S(1)} %get-tuple-element.43.refs_0_, f32[8,384]{1,0:T(8,128)S(1)} %collective-permute-done.6.refs_1_, bf16[384,4096]{1,0:T(8,128)(2,1)S(1)} %get-tuple-element.44.refs_2_, f32[1,4096]{1,0:T(1,128)S(1)} %bitcast.28), custom_call_target="tpu_custom_call" | custom-call | flops 3145728 | bytes 6291456 | tf_op jit(solution)/shard_map/norm/pallas_call | solution.py:434
  68.3 0.0 collective-permute-done.11
  68.3 0.0 copy-done.12
  68.3 0.0 copy-done.16
  68.3 1.4 %handoff.1 = f32[16,16,145]{2,1,0:T(8,128)} custom-call(s32[1]{0:T(128)} %bitcast.me_ref, f32[16,4096]{1,0:T(8,128)S(1)} %get-tuple-element.53.total_ref, bf16[16,4096]{1,0:T(8,128)(2,1)S(1)} %collective-permute-done.5.other_ref, f32[16,4096]{1,0:T(8,128)S(1)} %get-tuple-element.29.spread_ref, f32[16,4096]{1,0:T(8,128)S(1)} %copy-done.12, ...), custom_call_target="tpu_custom_call" | custom-call | flops 1000000000 | bytes 1000000 | tf_op jit(solution)/shard_map/handoff/pallas_call | solution.py:565
  (21 shorter events, 0.1 us)
Async XLA Ops:
  0.6 7.4 %copy-start.6 = (f32[256,16]{0,1:T(8,128)S(1)}, f32[256,16]{0,1:T(8,128)}, u32[]{:S(2)}) copy-start(f32[256,16]{0,1:T(8,128)} %param.12) | copy-start | bytes 49156
  0.6 7.4 %copy-start.7 = (f32[256,128]{1,0:T(8,128)S(1)}, f32[256,128]{1,0:T(8,128)}, u32[]{:S(2)}) copy-start(f32[256,128]{1,0:T(8,128)} %taps_ref.1) | copy-start | bytes 393220
  0.7 7.4 %copy-start.10 = (f32[256,16]{0,1:T(8,128)S(1)}, f32[256,16]{0,1:T(8,128)}, u32[]{:S(2)}) copy-start(f32[256,16]{0,1:T(8,128)} %param.11) | copy-start | bytes 49156
  7.7 4.6 %collective-permute-start = (bf16[16,4096]{1,0:T(8,128)(2,1)}, bf16[16,4096]{1,0:T(8,128)(2,1)S(1)}, u32[]{:S(2)}, u32[]{:S(2)}) collective-permute-start(bf16[16,4096]{1,0:T(8,128)(2,1)} %get-tuple-element.30), channel_id=1, source_target_pairs={{0,2},{2,0},{4,6},{6,4},{8,10},{10,8},{12,14},{14,12},{16,18},{18,... | collective-permute-start | bytes 393224 | tf_op jit(solution)/shard_map/ppermute | solution.py:621
  9.7 0.7 copy-start.11
  10.4 0.7 copy-start.13
  12.3 3.0 %copy-start.18 = (bf16[16,4096]{1,0:T(8,128)(2,1)}, bf16[16,4096]{1,0:T(8,128)(2,1)S(1)}, u32[]{:S(2)}) copy-start(bf16[16,4096]{1,0:T(8,128)(2,1)S(1)} %collective-permute-done) | copy-start | bytes 393220
  14.1 6.5 %collective-permute-start.1 = (bf16[16,4096]{1,0:T(8,128)(2,1)}, bf16[16,4096]{1,0:T(8,128)(2,1)}, u32[]{:S(2)}, u32[]{:S(2)}) collective-permute-start(bf16[16,4096]{1,0:T(8,128)(2,1)} %fusion.9.refs_1_), channel_id=1, source_target_pairs={{0,4},{2,6},{4,0},{6,2},{8,12},{10,14},{12,8},{14,10},{16,20},{18,... | collective-permute-start | bytes 393224 | tf_op jit(solution)/shard_map/ppermute | solution.py:621
  15.3 9.3 %copy-start = (bf16[384,4096]{1,0:T(8,128)(2,1)S(1)}, bf16[384,4096]{1,0:T(8,128)(2,1)}, u32[]{:S(2)}) copy-start(bf16[384,4096]{1,0:T(8,128)(2,1)} %k_hbm.3) | copy-start | bytes 9437188
  15.3 9.4 %copy-start.1 = (bf16[384,4096]{1,0:T(8,128)(2,1)S(1)}, bf16[384,4096]{1,0:T(8,128)(2,1)}, u32[]{:S(2)}) copy-start(bf16[384,4096]{1,0:T(8,128)(2,1)} %v_hbm.3) | copy-start | bytes 9437188
  15.3 34.2 %collective-permute-start.2 = (bf16[128,4096]{1,0:T(8,128)(2,1)}, bf16[128,4096]{1,0:T(8,128)(2,1)S(1)}, u32[]{:S(2)}, u32[]{:S(2)}) collective-permute-start(bf16[128,4096]{1,0:T(8,128)(2,1)} %hold.1.tail_hbm), channel_id=1, source_target_pairs={{0,2},{2,4},{4,6},{6,8},{8,10},{10,12},{12,14},{14,16},{16,18},{18... | collective-permute-start | bytes 3145736 | tf_op jit(solution)/shard_map/ppermute | solution.py:683
  17.8 1.2 %copy-start.3 = (bf16[128,4096]{1,0:T(8,128)(2,1)S(1)}, bf16[128,4096]{1,0:T(8,128)(2,1)}, u32[]{:S(2)}) copy-start(bf16[128,4096]{1,0:T(8,128)(2,1)} %hold.1.tail_hbm) | copy-start | bytes 3145732
  19.1 0.7 %copy-start.15 = (s32[256,9]{0,1:T(8,128)S(1)}, s32[256,9]{0,1:T(8,128)}, u32[]{:S(2)}) copy-start(s32[256,9]{0,1:T(8,128)} %param.15) | copy-start | bytes 27652
  19.8 4.9 %copy-start.14 = (f32[256,128]{1,0:T(8,128)S(1)}, f32[256,128]{1,0:T(8,128)}, u32[]{:S(2)}) copy-start(f32[256,128]{1,0:T(8,128)} %copy-done.13) | copy-start | bytes 393220
  19.9 15.4 %collective-permute-start.7 = (bf16[4,2,160,256]{3,2,1,0:T(8,128)(2,1)S(1)}, bf16[4,2,160,256]{3,2,1,0:T(8,128)(2,1)S(1)}, u32[]{:S(2)}, u32[]{:S(2)}) collective-permute-start(bf16[4,2,160,256]{3,2,1,0:T(8,128)(2,1)S(1)} %get-tuple-element.48), channel_id=1, source_target_pairs={{30,26},{31,27}} | collective-permute-start | bytes 1966088 | tf_op jit(solution)/shard_map/ppermute | solution.py:595
  21.8 15.9 %collective-permute-start.3 = (bf16[16,4096]{1,0:T(8,128)(2,1)S(1)}, bf16[16,4096]{1,0:T(8,128)(2,1)S(1)}, u32[]{:S(2)}, u32[]{:S(2)}) collective-permute-start(bf16[16,4096]{1,0:T(8,128)(2,1)S(1)} %fusion.8.after), channel_id=1, source_target_pairs={{0,8},{2,10},{4,12},{8,0},{10,2},{12,4},{14,6},{16,24},{18,26},{20... | collective-permute-start | bytes 393224 | tf_op jit(solution)/shard_map/ppermute | solution.py:625
  24.0 15.0 %collective-permute-start.4 = (bf16[16,4096]{1,0:T(8,128)(2,1)S(1)}, bf16[16,4096]{1,0:T(8,128)(2,1)S(1)}, u32[]{:S(2)}, u32[]{:S(2)}) collective-permute-start(bf16[16,4096]{1,0:T(8,128)(2,1)S(1)} %fusion.8.after), channel_id=1, source_target_pairs={{2,14},{18,30},{3,15},{19,31}} | collective-permute-start | bytes 393224 | tf_op jit(solution)/shard_map/ppermute | solution.py:625
  24.7 14.3 %copy-start.17 = (f32[16,4096]{1,0:T(8,128)S(1)}, f32[16,4096]{1,0:T(8,128)}, u32[]{:S(2)}) copy-start(f32[16,4096]{1,0:T(8,128)} %get-tuple-element.31) | copy-start | bytes 786436
  24.7 14.3 %copy-start.19 = (bf16[16,4096]{1,0:T(8,128)(2,1)S(1)}, bf16[16,4096]{1,0:T(8,128)(2,1)}, u32[]{:S(2)}) copy-start(bf16[16,4096]{1,0:T(8,128)(2,1)} %copy-done.18) | copy-start | bytes 393220
  34.6 14.8 %copy-start.2 = (bf16[384,4096]{1,0:T(8,128)(2,1)S(1)}, bf16[384,4096]{1,0:T(8,128)(2,1)}, u32[]{:S(2)}) copy-start(bf16[384,4096]{1,0:T(8,128)(2,1)} %q_hbm.1) | copy-start | bytes 9437188
  34.6 14.8 %copy-start.4 = (f32[16,4096]{1,0:T(8,128)S(1)}, f32[16,4096]{1,0:T(8,128)}, u32[]{:S(2)}) copy-start(f32[16,4096]{1,0:T(8,128)} %get-tuple-element.34.p1_hbm) | copy-start | bytes 786436
  34.7 14.8 %copy-start.5 = (f32[16,4096]{1,0:T(8,128)S(1)}, f32[16,4096]{1,0:T(8,128)}, u32[]{:S(2)}) copy-start(f32[16,4096]{1,0:T(8,128)} %get-tuple-element.35.p2_hbm) | copy-start | bytes 786436
  36.3 17.7 %collective-permute-start.10 = (bf16[2,160,256]{2,1,0:T(8,128)(2,1)S(1)}, bf16[2,160,256]{2,1,0:T(8,128)(2,1)S(1)}, u32[]{:S(2)}, u32[]{:S(2)}) collective-permute-start(bf16[2,160,256]{2,1,0:T(8,128)(2,1)S(1)} %get-tuple-element.56), channel_id=1, source_target_pairs={{26,2},{30,6},{27,3},{31,7}} | collective-permute-start | bytes 491528 | tf_op jit(solution)/shard_map/ppermute | solution.py:603
  37.0 17.0 %collective-permute-start.8 = (bf16[2,160,256]{2,1,0:T(8,128)(2,1)S(1)}, bf16[2,160,256]{2,1,0:T(8,128)(2,1)S(1)}, u32[]{:S(2)}, u32[]{:S(2)}) collective-permute-start(bf16[2,160,256]{2,1,0:T(8,128)(2,1)S(1)} %get-tuple-element.55), channel_id=1, source_target_pairs={{26,18},{30,22},{27,19},{31,23}} | collective-permute-start | bytes 491528 | tf_op jit(solution)/shard_map/ppermute | solution.py:603
  37.7 16.3 %collective-permute-start.9 = (bf16[2,160,256]{2,1,0:T(8,128)(2,1)S(1)}, bf16[2,160,256]{2,1,0:T(8,128)(2,1)S(1)}, u32[]{:S(2)}, u32[]{:S(2)}) collective-permute-start(bf16[2,160,256]{2,1,0:T(8,128)(2,1)S(1)} %get-tuple-element.57), channel_id=1, source_target_pairs={{26,10},{30,14},{27,11},{31,15}} | collective-permute-start | bytes 491528 | tf_op jit(solution)/shard_map/ppermute | solution.py:603
  40.4 16.2 %collective-permute-start.5 = (bf16[16,4096]{1,0:T(8,128)(2,1)S(1)}, bf16[16,4096]{1,0:T(8,128)(2,1)S(1)}, u32[]{:S(2)}, u32[]{:S(2)}) collective-permute-start(bf16[16,4096]{1,0:T(8,128)(2,1)S(1)} %get-tuple-element.52.after), channel_id=1, source_target_pairs={{0,16},{2,18},{4,20},{6,22},{8,24},{10,26},{12,28},{14,30},{16,0},... | collective-permute-start | bytes 393224 | tf_op jit(solution)/shard_map/ppermute | solution.py:621
  49.5 7.1 %copy-start.9 = (f32[32,128]{1,0:T(8,128)S(1)}, f32[32,128]{1,0:T(8,128)}, u32[]{:S(2)}) copy-start(f32[32,128]{1,0:T(8,128)} %get-tuple-element.41.rates_ref) | copy-start | bytes 49156
  54.8 13.5 %collective-permute-start.11 = (bf16[1,160,256]{2,1,0:T(8,128)(2,1)S(1)}, bf16[1,160,256]{2,1,0:T(8,128)(2,1)S(1)}, u32[]{:S(2)}, u32[]{:S(2)}) collective-permute-start(bf16[1,160,256]{2,1,0:T(8,128)(2,1)S(1)} %get-tuple-element.58), channel_id=1, source_target_pairs={{2,0},{6,4},{10,8},{14,12},{18,16},{22,20},{26,24},{30,28},{3,1},{... | collective-permute-start | bytes 245768 | tf_op jit(solution)/shard_map/ppermute | solution.py:611
  56.5 8.8 %copy-start.8 = (f32[4096]{0:T(1024)S(1)}, f32[4096]{0:T(1024)}, u32[]{:S(2)}) copy-start(f32[4096]{0:T(1024)} %param.14) | copy-start | bytes 49156
  60.4 7.9 %copy-start.12 = (f32[16,4096]{1,0:T(8,128)S(1)}, f32[16,4096]{1,0:T(8,128)}, u32[]{:S(2)}) copy-start(f32[16,4096]{1,0:T(8,128)} %copy-done.11) | copy-start | bytes 786436
  60.4 7.9 %copy-start.16 = (s32[256,9]{0,1:T(8,128)S(1)}, s32[256,9]{0,1:T(8,128)}, u32[]{:S(2)}) copy-start(s32[256,9]{0,1:T(8,128)} %param.15) | copy-start | bytes 27652
  60.4 4.9 %collective-permute-start.6 = (f32[8,384]{1,0:T(8,128)S(1)}, f32[8,384]{1,0:T(8,128)S(1)}, u32[]{:S(2)}, u32[]{:S(2)}) collective-permute-start(f32[8,384]{1,0:T(8,128)S(1)} %get-tuple-element.43.refs_0_), channel_id=1, source_target_pairs={{0,1},{1,0},{2,3},{3,2},{4,5},{5,4},{6,7},{7,6},{8,9},{9,8},{10,11... | collective-permute-start | bytes 36872 | tf_op jit(solution)/shard_map/ppermute | solution.py:651

commit v4 on v3

--- a/solution.py
+++ b/solution.py
@@ -463,8 +463,8 @@
     return jnp.dot(present.astype(bf16), before, preferred_element_type=f32)
 
 
-def select_kernel(blocks, slots, inner, outer, me_ref, tail_hbm, plan_ref, *refs):
-    outs, (items_ref, picks_ref, tail_ref, sem) = refs[:2], refs[2:]
+def select_kernel(blocks, slots, inner, outer, me_ref, tail_ref, plan_ref, *refs):
+    outs, (items_ref, picks_ref) = refs[:2], refs[2:]
     groups = plan_ref.shape[1]
 
     @pl.when(me_ref[0] != inner * outer - 1)
@@ -474,9 +474,6 @@
 
     @pl.when(me_ref[0] == inner * outer - 1)
     def _():
-        copy = pltpu.make_async_copy(tail_hbm, tail_ref, sem)
-        copy.start()
-        copy.wait()
         for g in range(0, groups // PER_TILE, 2):
             halves = []
             for side in range(2):
@@ -517,12 +514,11 @@
     vmem = pl.BlockSpec(memory_space=pltpu.VMEM)
     return pl.pallas_call(
         functools.partial(select_kernel, blocks, slots, inner, outer),
-        in_specs=[SMEM, ANY, vmem],
+        in_specs=[SMEM, vmem, vmem],
         out_specs=[vmem, vmem],
         out_shape=[jax.ShapeDtypeStruct((outer, inner // 2, slots, MODES * GW), bf16)] * 2,
         scratch_shapes=[
             pltpu.VMEM((blocks * groups, MODES * GW), bf16), pltpu.VMEM((inner * slots, blocks * groups), bf16),
-            pltpu.VMEM(tail.shape, bf16), pltpu.SemaphoreType.DMA,
         ],
         compiler_params=params(20),
         cost_estimate=pl.CostEstimate(flops=10**9, bytes_accessed=2 * 10**6, transcendentals=0),

time: 70.2 us -> 70.1 us (level)
  no operation moved by 1% of the time
where the time goes in v4:
time: 70.1 us; the launch traced here: 69.7 us
  Pallas kernels  30.9 us (44%)
  starting transfers between devices  24.7 us (35%)
  other arithmetic  6.03 us (9%)
  local copies, waits for them, and re-layouts  4.49 us (6%)
  waiting for transfers between devices  2.51 us (4%)
  between operations  1.02 us (1%)
    ppermute x3, starting transfers between devices, exchange(): return [lax.ppermute(sent, 'seq', pairs)]  10.6 us
    pallas_call x1, Pallas kernels, local_part(): pl.pallas_call(functools.partial(local_kernel, chunks, tiles), in_specs=[...  9.92 us
    pallas_call x1, Pallas kernels, product_and_states(): pl.pallas_call(functools.partial(product_kernel, chunks, tiles), in_specs...  7.02 us
    convert_element_type x3, other arithmetic, scan_states(): sent = total.astype(bf16)  4.27 us
    ppermute x1, starting transfers between devices, sum_over_chan(): return [energy, lax.ppermute(energy, 'chan', [(0, 1), (1, 0)])]  4.15 us
    pallas_call x1, Pallas kernels, carry_part(): pl.pallas_call(functools.partial(carry_kernel, chunks, tiles), in_specs=[...  4.03 us
    pallas_call x1, Pallas kernels, gate_part(): pl.pallas_call(functools.partial(gate_kernel, chunks, tiles, step), in_sp...  3.86 us
    unnamed x40, local copies, waits for them, and re-layouts  3.35 us
  transfers between devices with their start and end apart: 12, of which 3 were waited for; matrix products, arithmetic and copies ran while one was open for 8% of the time, Pallas kernels for 32%

profile of v4, /device:TPU:11, one launch (start us, length us, event | category | flops | bytes accessed | tf_op | source)
XLA Modules:
  0.0 69.7 jit_solution(7103048842505043486)
XLA Ops:
  0.6 0.0 copy-start.6
  0.6 0.0 copy-start.7
  0.7 0.0 copy-start.10
  0.7 7.0 %product_states.1 = (bf16[128,4096]{1,0:T(8,128)(2,1)}, f32[16,4096]{1,0:T(8,128)}, f32[16,4096]{1,0:T(8,128)}, f32[16,4096]{1,0:T(8,128)}, bf16[16,4096]{1,0:T(8,128)(2,1)}, /*index=5*/f32[32,128]{1,0:T(8,128)}) custom-call(bf16[384,4096]{1,0:T(8,128)(2,1)} %k_hbm.3, bf16[384,4096]{1,0:T(8,128)(2,1)} %v_hbm.3, f32[16,256]{1,0:T(8,128)} %bitcast.26), custom_call_target="tpu_custom_call" | custom-call | flops 1207959552 | bytes 9437184 | tf_op jit(solution)/shard_map/product_states/pallas_call | solution.py:134
  7.7 0.3 collective-permute-start
  8.0 0.0 copy-done.6
  8.0 0.0 copy-done.7
  8.1 0.0 copy-done.10
  8.1 1.6 %prepare.1 = (f32[16,4096]{1,0:T(8,128)S(1)}, f32[16,4096]{1,0:T(8,128)S(1)}, f32[256,128]{1,0:T(8,128)S(1)}, f32[256,128]{1,0:T(8,128)S(1)}, f32[32,128]{1,0:T(8,128)S(1)}) custom-call(f32[16,256]{1,0:T(8,128)S(1)} %bitcast.27, f32[16,256]{1,0:T(8,128)S(1)} %negate_sqrt_fusion.factor_ref, f32[16,256]{1,0:T(8,128)S(1)} %bitcast.29, f32[256,128]{1,0:T(8,128)S(1)} %copy-done.7), custom_call_target="tpu_custom_call" | custom-call | tf_op jit(solution)/shard_map/prepare/pallas_call | solution.py:324
  9.7 0.0 copy-start.11
  9.7 0.7 copy-done.11
  10.4 0.7 copy-done.13
  11.1 1.3 %collective-permute-done = bf16[16,4096]{1,0:T(8,128)(2,1)S(1)} collective-permute-done((bf16[16,4096]{1,0:T(8,128)(2,1)}, bf16[16,4096]{1,0:T(8,128)(2,1)S(1)}, u32[]{:S(2)}, u32[]{:S(2)}) %collective-permute-start) | collective-permute-done | bytes 131104 | tf_op jit(solution)/shard_map/ppermute | solution.py:617
  12.3 1.7 %fusion.9.refs_1_ = bf16[16,4096]{1,0:T(8,128)(2,1)} fusion(f32[16,4096]{1,0:T(8,128)} %get-tuple-element.31, bf16[16,4096]{1,0:T(8,128)(2,1)S(1)} %collective-permute-done, f32[16,4096]{1,0:T(8,128)S(1)} %get-tuple-element.29.spread_ref, pred[]{:T(512)S(6)} %ne.23), kind=kLoop, calls=%fused_computation.26 | loop fusion | flops 589824 | bytes 786433 | tf_op jit(solution)/shard_map/convert_element_type | solution.py:641
  14.1 1.2 %collective-permute-start.1 = (bf16[16,4096]{1,0:T(8,128)(2,1)}, bf16[16,4096]{1,0:T(8,128)(2,1)}, u32[]{:S(2)}, u32[]{:S(2)}) collective-permute-start(bf16[16,4096]{1,0:T(8,128)(2,1)} %fusion.9.refs_1_), channel_id=1, source_target_pairs={{0,4},{2,6},{4,0},{6,2},{8,12},{10,14},{12,8},{14,10},{16,20},{18,... | collective-permute-start | bytes 393224 | tf_op jit(solution)/shard_map/ppermute | solution.py:617
  15.3 0.0 copy-done.18
  15.3 2.5 %collective-permute-start.2 = (bf16[128,4096]{1,0:T(8,128)(2,1)}, bf16[128,4096]{1,0:T(8,128)(2,1)S(1)}, u32[]{:S(2)}, u32[]{:S(2)}) collective-permute-start(bf16[128,4096]{1,0:T(8,128)(2,1)} %hold.1.tail_ref), channel_id=1, source_target_pairs={{0,2},{2,4},{4,6},{6,8},{8,10},{10,12},{12,14},{14,16},{16,18},{18... | collective-permute-start | bytes 3145736 | tf_op jit(solution)/shard_map/ppermute | solution.py:679
  17.8 0.0 copy-start.3
  17.8 1.2 %copy-done.3 = bf16[128,4096]{1,0:T(8,128)(2,1)S(1)} copy-done((bf16[128,4096]{1,0:T(8,128)(2,1)S(1)}, bf16[128,4096]{1,0:T(8,128)(2,1)}, u32[]{:S(2)}) %copy-start.3) | copy-done | bytes 1048600
  19.1 0.7 %copy-done.15 = s32[256,9]{0,1:T(8,128)S(1)} copy-done((s32[256,9]{0,1:T(8,128)S(1)}, s32[256,9]{0,1:T(8,128)}, u32[]{:S(2)}) %copy-start.15) | copy-done | bytes 9240
  19.8 0.1 select_tails.1
  19.9 0.7 %collective-permute-start.7 = (bf16[4,2,160,256]{3,2,1,0:T(8,128)(2,1)S(1)}, bf16[4,2,160,256]{3,2,1,0:T(8,128)(2,1)S(1)}, u32[]{:S(2)}, u32[]{:S(2)}) collective-permute-start(bf16[4,2,160,256]{3,2,1,0:T(8,128)(2,1)S(1)} %get-tuple-element.48), channel_id=1, source_target_pairs={{30,26},{31,27}} | collective-permute-start | bytes 1966088 | tf_op jit(solution)/shard_map/ppermute | solution.py:591
  20.6 0.0 collective-permute-done.1
  20.6 1.2 %fusion.8.after = bf16[16,4096]{1,0:T(8,128)(2,1)S(1)} fusion(bf16[16,4096]{1,0:T(8,128)(2,1)} %collective-permute-done.1, f32[16,4096]{1,0:T(8,128)S(1)} %get-tuple-element.29.spread_ref, pred[]{:T(512)S(6)} %ne.22, f32[16,4096]{1,0:T(8,128)} %get-tuple-element.31, bf16[16,4096]{1,0:T(8,128)(2,1)} %copy-done.18, pred[]{:T(512)S(6)} %ne.23), kind=kLoop, calls=%fused_computation.24 | loop fusion | flops 1048576 | bytes 917506 | tf_op jit(solution)/shard_map/convert_element_type | solution.py:641
  21.8 2.1 %collective-permute-start.3 = (bf16[16,4096]{1,0:T(8,128)(2,1)S(1)}, bf16[16,4096]{1,0:T(8,128)(2,1)S(1)}, u32[]{:S(2)}, u32[]{:S(2)}) collective-permute-start(bf16[16,4096]{1,0:T(8,128)(2,1)S(1)} %fusion.8.after), channel_id=1, source_target_pairs={{0,8},{2,10},{4,12},{8,0},{10,2},{12,4},{14,6},{16,24},{18,26},{20... | collective-permute-start | bytes 393224 | tf_op jit(solution)/shard_map/ppermute | solution.py:621
  24.0 0.7 collective-permute-start.4
  24.6 0.0 copy-done
  24.7 0.0 copy-done.1
  24.7 0.0 copy-done.14
  24.7 0.0 copy-start.17
  24.7 0.0 copy-start.19
  24.7 9.9 %local_conv.1 = (bf16[384,4096]{1,0:T(8,128)(2,1)S(1)}, f32[8,128]{1,0:T(8,128)S(1)}) custom-call(bf16[384,4096]{1,0:T(8,128)(2,1)S(1)} %copy-done, bf16[384,4096]{1,0:T(8,128)(2,1)S(1)} %copy-done.1, f32[256,128]{1,0:T(8,128)S(1)} %get-tuple-element.27.taps_rev, f32[256,128]{1,0:T(8,128)S(1)} %copy-done.14, bf16[16,4096]{1,0:T(8,128)(2,1)S(1)} %fusion.8.after), custom_call_target="tpu_custom_call" | custom-call | flops 8589934592 | bytes 6291456 | tf_op jit(solution)/shard_map/local_conv/pallas_call | solution.py:228
  34.6 0.0 copy-start.2
  34.6 0.0 copy-start.4
  34.6 0.0 copy-start.5
  34.7 0.6 slice.26
  35.2 0.0 collective-permute-done.7
  35.2 1.0 %add_select_fusion = bf16[4,2,160,256]{3,2,1,0:T(8,128)(2,1)S(1)} fusion(bf16[4,2,160,256]{3,2,1,0:T(8,128)(2,1)S(1)} %get-tuple-element.47, bf16[4,2,160,256]{3,2,1,0:T(8,128)(2,1)S(1)} %collective-permute-done.7, pred[]{:T(512)S(6)} %ne.22, bf16[]{:T(256)} %bitcast.5), kind=kLoop, calls=%fused_computation | loop fusion | flops 655360 | bytes 1966083 | tf_op jit(solution)/shard_map/jit(_where)/select_n | solution.py:592
  36.3 0.7 collective-permute-start.10
  37.0 0.7 collective-permute-start.8
  37.7 0.0 collective-permute-done.3
  37.7 1.3 %collective-permute-start.9 = (bf16[2,160,256]{2,1,0:T(8,128)(2,1)S(1)}, bf16[2,160,256]{2,1,0:T(8,128)(2,1)S(1)}, u32[]{:S(2)}, u32[]{:S(2)}) collective-permute-start(bf16[2,160,256]{2,1,0:T(8,128)(2,1)S(1)} %get-tuple-element.57), channel_id=1, source_target_pairs={{26,10},{30,14},{27,11},{31,15}} | collective-permute-start | bytes 491528 | tf_op jit(solution)/shard_map/ppermute | solution.py:599
  39.0 0.0 collective-permute-done.4
  39.0 0.0 copy-done.17
  39.0 0.0 copy-done.19
  39.0 1.3 %fusion.10 = (bf16[16,4096]{1,0:T(8,128)(2,1)S(1)}, f32[16,4096]{1,0:T(8,128)S(1)}, f32[16,4096]{1,0:T(8,128)S(1)}) fusion(f32[16,4096]{1,0:T(8,128)S(1)} %copy-done.17, bf16[16,4096]{1,0:T(8,128)(2,1)S(1)} %copy-done.19, pred[]{:T(512)S(6)} %ne.23, bf16[16,4096]{1,0:T(8,128)(2,1)} %collective-permute-done.1, pred[]{:T(512)S(6)} %ne.22, ...), kind=kLoop, calls=%fused_computation.27 | loop fusion | flops 2359296 | bytes 1703947 | tf_op jit(solution)/shard_map/convert_element_type | solution.py:641
  40.4 9.0 %collective-permute-start.5 = (bf16[16,4096]{1,0:T(8,128)(2,1)S(1)}, bf16[16,4096]{1,0:T(8,128)(2,1)S(1)}, u32[]{:S(2)}, u32[]{:S(2)}) collective-permute-start(bf16[16,4096]{1,0:T(8,128)(2,1)S(1)} %get-tuple-element.52.after), channel_id=1, source_target_pairs={{0,16},{2,18},{4,20},{6,22},{8,24},{10,26},{12,28},{14,30},{16,0},... | collective-permute-start | bytes 393224 | tf_op jit(solution)/shard_map/ppermute | solution.py:617
  49.4 0.0 collective-permute-done.2.tail_ref
  49.4 0.0 copy-done.2
  49.4 0.0 copy-done.4
  49.4 4.0 %carry.1 = (bf16[128,4096]{1,0:T(8,128)(2,1)S(1)}, f32[8,128]{1,0:T(8,128)S(1)}, bf16[384,4096]{1,0:T(8,128)(2,1)S(1)}, f32[16,4096]{1,0:T(8,128)S(1)}, f32[16,4096]{1,0:T(8,128)S(1)}, /*index=5*/f32[32,128]{1,0:T(8,128)S(1)}) custom-call(bf16[384,4096]{1,0:T(8,128)(2,1)S(1)} %get-tuple-element.32.local_ref, ...), custom_call_target="tpu_custom_call" | custom-call | flops 536870912 | bytes 3145728 | tf_op jit(solution)/shard_map/carry/pallas_call | solution.py:283
  53.5 0.5 slice.28
  54.0 0.0 collective-permute-done.10
  54.0 0.0 collective-permute-done.8
  54.0 0.0 collective-permute-done.9
  54.0 0.7 fusion.7
  54.7 1.3 %collective-permute-start.11 = (bf16[1,160,256]{2,1,0:T(8,128)(2,1)S(1)}, bf16[1,160,256]{2,1,0:T(8,128)(2,1)S(1)}, u32[]{:S(2)}, u32[]{:S(2)}) collective-permute-start(bf16[1,160,256]{2,1,0:T(8,128)(2,1)S(1)} %get-tuple-element.58), channel_id=1, source_target_pairs={{2,0},{6,4},{10,8},{14,12},{18,16},{22,20},{26,24},{30,28},{3,1},{... | collective-permute-start | bytes 245768 | tf_op jit(solution)/shard_map/ppermute | solution.py:607
  56.0 0.4 collective-permute-done.5.other_ref
  56.4 3.9 %gate.1 = (bf16[384,4096]{1,0:T(8,128)(2,1)S(1)}, f32[8,384]{1,0:T(8,128)S(1)}) custom-call(s32[1]{0:T(128)} %bitcast.me_ref, bf16[128,4096]{1,0:T(8,128)(2,1)S(1)} %get-tuple-element.37.first_ref, bf16[384,4096]{1,0:T(8,128)(2,1)S(1)} %get-tuple-element.32.local_ref, bf16[384,4096]{1,0:T(8,128)(2,1)S(1)} %get-tuple-element.38.q_ref, ...), custom_call_target="tpu_custom_call" | custom-call | flops 1073741824 | bytes 9437184 | tf_op jit(solution)/shard_map/gate/pallas_call | solution.py:390
  60.3 4.1 %collective-permute-start.6 = (f32[8,384]{1,0:T(8,128)S(1)}, f32[8,384]{1,0:T(8,128)S(1)}, u32[]{:S(2)}, u32[]{:S(2)}) collective-permute-start(f32[8,384]{1,0:T(8,128)S(1)} %get-tuple-element.43.refs_0_), channel_id=1, source_target_pairs={{0,1},{1,0},{2,3},{3,2},{4,5},{5,4},{6,7},{7,6},{8,9},{9,8},{10,11... | collective-permute-start | bytes 36872 | tf_op jit(solution)/shard_map/ppermute | solution.py:647
  64.4 0.8 %collective-permute-done.6.refs_1_ = f32[8,384]{1,0:T(8,128)S(1)} collective-permute-done((f32[8,384]{1,0:T(8,128)S(1)}, f32[8,384]{1,0:T(8,128)S(1)}, u32[]{:S(2)}, u32[]{:S(2)}) %collective-permute-start.6) | collective-permute-done | bytes 12320 | tf_op jit(solution)/shard_map/ppermute | solution.py:647
  65.3 3.0 %norm.1 = (bf16[384,4096]{1,0:T(8,128)(2,1)}, f32[8,128]{1,0:T(8,128)S(1)}) custom-call(f32[8,384]{1,0:T(8,128)S(1)} %get-tuple-element.43.refs_0_, f32[8,384]{1,0:T(8,128)S(1)} %collective-permute-done.6.refs_1_, bf16[384,4096]{1,0:T(8,128)(2,1)S(1)} %get-tuple-element.44.refs_2_, f32[1,4096]{1,0:T(1,128)S(1)} %bitcast.28), custom_call_target="tpu_custom_call" | custom-call | flops 3145728 | bytes 6291456 | tf_op jit(solution)/shard_map/norm/pallas_call | solution.py:434
  68.2 0.0 collective-permute-done.11
  68.3 1.4 %handoff.1 = f32[16,16,145]{2,1,0:T(8,128)} custom-call(s32[1]{0:T(128)} %bitcast.me_ref, f32[16,4096]{1,0:T(8,128)S(1)} %get-tuple-element.53.total_ref, bf16[16,4096]{1,0:T(8,128)(2,1)S(1)} %collective-permute-done.5.other_ref, f32[16,4096]{1,0:T(8,128)S(1)} %get-tuple-element.29.spread_ref, f32[16,4096]{1,0:T(8,128)S(1)} %copy-done.12, ...), custom_call_target="tpu_custom_call" | custom-call | flops 1000000000 | bytes 1000000 | tf_op jit(solution)/shard_map/handoff/pallas_call | solution.py:561
  (21 shorter events, 0.1 us)
Async XLA Ops:
  0.6 7.4 %copy-start.6 = (f32[256,16]{0,1:T(8,128)S(1)}, f32[256,16]{0,1:T(8,128)}, u32[]{:S(2)}) copy-start(f32[256,16]{0,1:T(8,128)} %param.12) | copy-start | bytes 49156
  0.6 7.4 %copy-start.7 = (f32[256,128]{1,0:T(8,128)S(1)}, f32[256,128]{1,0:T(8,128)}, u32[]{:S(2)}) copy-start(f32[256,128]{1,0:T(8,128)} %taps_ref.1) | copy-start | bytes 393220
  0.7 7.4 %copy-start.10 = (f32[256,16]{0,1:T(8,128)S(1)}, f32[256,16]{0,1:T(8,128)}, u32[]{:S(2)}) copy-start(f32[256,16]{0,1:T(8,128)} %param.11) | copy-start | bytes 49156
  7.7 4.6 %collective-permute-start = (bf16[16,4096]{1,0:T(8,128)(2,1)}, bf16[16,4096]{1,0:T(8,128)(2,1)S(1)}, u32[]{:S(2)}, u32[]{:S(2)}) collective-permute-start(bf16[16,4096]{1,0:T(8,128)(2,1)} %get-tuple-element.30), channel_id=1, source_target_pairs={{0,2},{2,0},{4,6},{6,4},{8,10},{10,8},{12,14},{14,12},{16,18},{18,... | collective-permute-start | bytes 393224 | tf_op jit(solution)/shard_map/ppermute | solution.py:617
  9.7 0.7 copy-start.11
  10.4 0.7 copy-start.13
  12.3 3.0 %copy-start.18 = (bf16[16,4096]{1,0:T(8,128)(2,1)}, bf16[16,4096]{1,0:T(8,128)(2,1)S(1)}, u32[]{:S(2)}) copy-start(bf16[16,4096]{1,0:T(8,128)(2,1)S(1)} %collective-permute-done) | copy-start | bytes 393220
  14.1 6.5 %collective-permute-start.1 = (bf16[16,4096]{1,0:T(8,128)(2,1)}, bf16[16,4096]{1,0:T(8,128)(2,1)}, u32[]{:S(2)}, u32[]{:S(2)}) collective-permute-start(bf16[16,4096]{1,0:T(8,128)(2,1)} %fusion.9.refs_1_), channel_id=1, source_target_pairs={{0,4},{2,6},{4,0},{6,2},{8,12},{10,14},{12,8},{14,10},{16,20},{18,... | collective-permute-start | bytes 393224 | tf_op jit(solution)/shard_map/ppermute | solution.py:617
  15.3 9.3 %copy-start = (bf16[384,4096]{1,0:T(8,128)(2,1)S(1)}, bf16[384,4096]{1,0:T(8,128)(2,1)}, u32[]{:S(2)}) copy-start(bf16[384,4096]{1,0:T(8,128)(2,1)} %k_hbm.3) | copy-start | bytes 9437188
  15.3 9.3 %copy-start.1 = (bf16[384,4096]{1,0:T(8,128)(2,1)S(1)}, bf16[384,4096]{1,0:T(8,128)(2,1)}, u32[]{:S(2)}) copy-start(bf16[384,4096]{1,0:T(8,128)(2,1)} %v_hbm.3) | copy-start | bytes 9437188
  15.3 34.1 %collective-permute-start.2 = (bf16[128,4096]{1,0:T(8,128)(2,1)}, bf16[128,4096]{1,0:T(8,128)(2,1)S(1)}, u32[]{:S(2)}, u32[]{:S(2)}) collective-permute-start(bf16[128,4096]{1,0:T(8,128)(2,1)} %hold.1.tail_ref), channel_id=1, source_target_pairs={{0,2},{2,4},{4,6},{6,8},{8,10},{10,12},{12,14},{14,16},{16,18},{18... | collective-permute-start | bytes 3145736 | tf_op jit(solution)/shard_map/ppermute | solution.py:679
  17.8 1.2 %copy-start.3 = (bf16[128,4096]{1,0:T(8,128)(2,1)S(1)}, bf16[128,4096]{1,0:T(8,128)(2,1)}, u32[]{:S(2)}) copy-start(bf16[128,4096]{1,0:T(8,128)(2,1)} %hold.1.tail_ref) | copy-start | bytes 3145732
  19.1 0.7 %copy-start.15 = (s32[256,9]{0,1:T(8,128)S(1)}, s32[256,9]{0,1:T(8,128)}, u32[]{:S(2)}) copy-start(s32[256,9]{0,1:T(8,128)} %param.15) | copy-start | bytes 27652
  19.8 4.9 %copy-start.14 = (f32[256,128]{1,0:T(8,128)S(1)}, f32[256,128]{1,0:T(8,128)}, u32[]{:S(2)}) copy-start(f32[256,128]{1,0:T(8,128)} %copy-done.13) | copy-start | bytes 393220
  19.9 15.4 %collective-permute-start.7 = (bf16[4,2,160,256]{3,2,1,0:T(8,128)(2,1)S(1)}, bf16[4,2,160,256]{3,2,1,0:T(8,128)(2,1)S(1)}, u32[]{:S(2)}, u32[]{:S(2)}) collective-permute-start(bf16[4,2,160,256]{3,2,1,0:T(8,128)(2,1)S(1)} %get-tuple-element.48), channel_id=1, source_target_pairs={{30,26},{31,27}} | collective-permute-start | bytes 1966088 | tf_op jit(solution)/shard_map/ppermute | solution.py:591
  21.8 15.9 %collective-permute-start.3 = (bf16[16,4096]{1,0:T(8,128)(2,1)S(1)}, bf16[16,4096]{1,0:T(8,128)(2,1)S(1)}, u32[]{:S(2)}, u32[]{:S(2)}) collective-permute-start(bf16[16,4096]{1,0:T(8,128)(2,1)S(1)} %fusion.8.after), channel_id=1, source_target_pairs={{0,8},{2,10},{4,12},{8,0},{10,2},{12,4},{14,6},{16,24},{18,26},{20... | collective-permute-start | bytes 393224 | tf_op jit(solution)/shard_map/ppermute | solution.py:621
  24.0 15.0 %collective-permute-start.4 = (bf16[16,4096]{1,0:T(8,128)(2,1)S(1)}, bf16[16,4096]{1,0:T(8,128)(2,1)S(1)}, u32[]{:S(2)}, u32[]{:S(2)}) collective-permute-start(bf16[16,4096]{1,0:T(8,128)(2,1)S(1)} %fusion.8.after), channel_id=1, source_target_pairs={{2,14},{18,30},{3,15},{19,31}} | collective-permute-start | bytes 393224 | tf_op jit(solution)/shard_map/ppermute | solution.py:621
  24.7 14.3 %copy-start.17 = (f32[16,4096]{1,0:T(8,128)S(1)}, f32[16,4096]{1,0:T(8,128)}, u32[]{:S(2)}) copy-start(f32[16,4096]{1,0:T(8,128)} %get-tuple-element.31) | copy-start | bytes 786436
  24.7 14.3 %copy-start.19 = (bf16[16,4096]{1,0:T(8,128)(2,1)S(1)}, bf16[16,4096]{1,0:T(8,128)(2,1)}, u32[]{:S(2)}) copy-start(bf16[16,4096]{1,0:T(8,128)(2,1)} %copy-done.18) | copy-start | bytes 393220
  34.6 14.8 %copy-start.2 = (bf16[384,4096]{1,0:T(8,128)(2,1)S(1)}, bf16[384,4096]{1,0:T(8,128)(2,1)}, u32[]{:S(2)}) copy-start(bf16[384,4096]{1,0:T(8,128)(2,1)} %q_hbm.1) | copy-start | bytes 9437188
  34.6 14.8 %copy-start.4 = (f32[16,4096]{1,0:T(8,128)S(1)}, f32[16,4096]{1,0:T(8,128)}, u32[]{:S(2)}) copy-start(f32[16,4096]{1,0:T(8,128)} %get-tuple-element.34.p1_hbm) | copy-start | bytes 786436
  34.6 14.8 %copy-start.5 = (f32[16,4096]{1,0:T(8,128)S(1)}, f32[16,4096]{1,0:T(8,128)}, u32[]{:S(2)}) copy-start(f32[16,4096]{1,0:T(8,128)} %get-tuple-element.35.p2_hbm) | copy-start | bytes 786436
  36.3 17.6 %collective-permute-start.10 = (bf16[2,160,256]{2,1,0:T(8,128)(2,1)S(1)}, bf16[2,160,256]{2,1,0:T(8,128)(2,1)S(1)}, u32[]{:S(2)}, u32[]{:S(2)}) collective-permute-start(bf16[2,160,256]{2,1,0:T(8,128)(2,1)S(1)} %get-tuple-element.56), channel_id=1, source_target_pairs={{26,2},{30,6},{27,3},{31,7}} | collective-permute-start | bytes 491528 | tf_op jit(solution)/shard_map/ppermute | solution.py:599
  37.0 17.0 %collective-permute-start.8 = (bf16[2,160,256]{2,1,0:T(8,128)(2,1)S(1)}, bf16[2,160,256]{2,1,0:T(8,128)(2,1)S(1)}, u32[]{:S(2)}, u32[]{:S(2)}) collective-permute-start(bf16[2,160,256]{2,1,0:T(8,128)(2,1)S(1)} %get-tuple-element.55), channel_id=1, source_target_pairs={{26,18},{30,22},{27,19},{31,23}} | collective-permute-start | bytes 491528 | tf_op jit(solution)/shard_map/ppermute | solution.py:599
  37.7 16.3 %collective-permute-start.9 = (bf16[2,160,256]{2,1,0:T(8,128)(2,1)S(1)}, bf16[2,160,256]{2,1,0:T(8,128)(2,1)S(1)}, u32[]{:S(2)}, u32[]{:S(2)}) collective-permute-start(bf16[2,160,256]{2,1,0:T(8,128)(2,1)S(1)} %get-tuple-element.57), channel_id=1, source_target_pairs={{26,10},{30,14},{27,11},{31,15}} | collective-permute-start | bytes 491528 | tf_op jit(solution)/shard_map/ppermute | solution.py:599
  40.4 16.0 %collective-permute-start.5 = (bf16[16,4096]{1,0:T(8,128)(2,1)S(1)}, bf16[16,4096]{1,0:T(8,128)(2,1)S(1)}, u32[]{:S(2)}, u32[]{:S(2)}) collective-permute-start(bf16[16,4096]{1,0:T(8,128)(2,1)S(1)} %get-tuple-element.52.after), channel_id=1, source_target_pairs={{0,16},{2,18},{4,20},{6,22},{8,24},{10,26},{12,28},{14,30},{16,0},... | collective-permute-start | bytes 393224 | tf_op jit(solution)/shard_map/ppermute | solution.py:617
  49.4 7.0 %copy-start.9 = (f32[32,128]{1,0:T(8,128)S(1)}, f32[32,128]{1,0:T(8,128)}, u32[]{:S(2)}) copy-start(f32[32,128]{1,0:T(8,128)} %get-tuple-element.41.rates_ref) | copy-start | bytes 49156
  54.7 13.5 %collective-permute-start.11 = (bf16[1,160,256]{2,1,0:T(8,128)(2,1)S(1)}, bf16[1,160,256]{2,1,0:T(8,128)(2,1)S(1)}, u32[]{:S(2)}, u32[]{:S(2)}) collective-permute-start(bf16[1,160,256]{2,1,0:T(8,128)(2,1)S(1)} %get-tuple-element.58), channel_id=1, source_target_pairs={{2,0},{6,4},{10,8},{14,12},{18,16},{22,20},{26,24},{30,28},{3,1},{... | collective-permute-start | bytes 245768 | tf_op jit(solution)/shard_map/ppermute | solution.py:607
  56.4 8.8 %copy-start.8 = (f32[4096]{0:T(1024)S(1)}, f32[4096]{0:T(1024)}, u32[]{:S(2)}) copy-start(f32[4096]{0:T(1024)} %param.14) | copy-start | bytes 49156
  60.3 8.0 %copy-start.12 = (f32[16,4096]{1,0:T(8,128)S(1)}, f32[16,4096]{1,0:T(8,128)}, u32[]{:S(2)}) copy-start(f32[16,4096]{1,0:T(8,128)} %copy-done.11) | copy-start | bytes 786436
  60.3 8.0 %copy-start.16 = (s32[256,9]{0,1:T(8,128)S(1)}, s32[256,9]{0,1:T(8,128)}, u32[]{:S(2)}) copy-start(s32[256,9]{0,1:T(8,128)} %param.15) | copy-start | bytes 27652
  60.3 5.0 %collective-permute-start.6 = (f32[8,384]{1,0:T(8,128)S(1)}, f32[8,384]{1,0:T(8,128)S(1)}, u32[]{:S(2)}, u32[]{:S(2)}) collective-permute-start(f32[8,384]{1,0:T(8,128)S(1)} %get-tuple-element.43.refs_0_), channel_id=1, source_target_pairs={{0,1},{1,0},{2,3},{3,2},{4,5},{5,4},{6,7},{7,6},{8,9},{9,8},{10,11... | collective-permute-start | bytes 36872 | tf_op jit(solution)/shard_map/ppermute | solution.py:647
